TPU v7x, 32 devices: a whole 2x2x4 slice. The times are simulated.
32 devices in a mesh: wide: 8 (over z, x), narrow: 4 (over y, core).
Axes of the slice: x: 2, y: 2, z: 4, core: 2. Of those that a mesh axis runs over, the one named last changes fastest.
Arguments:
- tokens: bfloat16 [32768, 512], P(('wide', 'narrow')), may hold values from -8 to 8
- image: bfloat16 [75264, 512], P(('wide', 'narrow')), may hold values from -6 to 6
- segments: int32 [32, 1024], P(('wide', 'narrow')), may hold values from 0 to 2, never falling along the last dimension, each value on 1 to 512 neighbouring positions
- valid_len: int32 [32], P(('wide', 'narrow')), may hold values from 768 to 1024
- cotangent: bfloat16 [32768, 512], P(('wide', 'narrow')), may hold values from -6 to 6
- w_attn: float32 [8, 512, 512], P(None, ('wide', 'narrow')), may hold values from -1.41421356 to 1.41421356
- w_ffn: float32 [2, 512, 1024], P(None, ('wide', 'narrow')), may hold values from -0.35355339 to 0.35355339
- norm_params: float32 [6, 512], P(None, ('wide', 'narrow')), may hold values from -1.2 to 2.8
- momentum_attn: float32 [8, 512, 512], P(None, ('wide', 'narrow')), may hold values from -162.9174 to 162.9174
- variance_attn: float32 [8, 512, 512], P(None, ('wide', 'narrow')), may hold values from 32.44032 to 134.3488
- momentum_ffn: float32 [2, 512, 1024], P(None, ('wide', 'narrow')), may hold values from -162.9174 to 162.9174
- variance_ffn: float32 [2, 512, 1024], P(None, ('wide', 'narrow')), may hold values from 32.44032 to 134.3488
- momentum_norm: float32 [6, 512], P(None, ('wide', 'narrow')), may hold values from -325.8348 to 325.8348
- variance_norm: float32 [6, 512], P(None, ('wide', 'narrow')), may hold values from 127.7952 to 527.5648
Outputs:
- result: bfloat16 [32768, 512], P(('wide', 'narrow'))
- token_grad: float32 [32768, 512], P(('wide', 'narrow'))
- image_grad: float32 [75264, 512], P(('wide', 'narrow'))
- grad_attn: float32 [8, 512, 512], P(None, ('wide', 'narrow'))
- grad_ffn: float32 [2, 512, 1024], P(None, ('wide', 'narrow'))
- grad_norm: float32 [6, 512], P(None, ('wide', 'narrow'))
- new_attn: float32 [8, 512, 512], P(None, ('wide', 'narrow'))
- new_ffn: float32 [2, 512, 1024], P(None, ('wide', 'narrow'))
- new_norm: float32 [6, 512], P(None, ('wide', 'narrow'))
- new_momentum_attn: float32 [8, 512, 512], P(None, ('wide', 'narrow'))
- new_variance_attn: float32 [8, 512, 512], P(None, ('wide', 'narrow'))
- new_momentum_ffn: float32 [2, 512, 1024], P(None, ('wide', 'narrow'))
- new_variance_ffn: float32 [2, 512, 1024], P(None, ('wide', 'narrow'))
- new_momentum_norm: float32 [6, 512], P(None, ('wide', 'narrow'))
- new_variance_norm: float32 [6, 512], P(None, ('wide', 'narrow'))
- weight_norms: float32 [16], replicated
- update_norms: float32 [16], replicated
Inputs may be any that keep to these rules, and one draw needn't show every extreme that they name: `segments`: each row holds its 3 tables in order, each 1 to 512 tags long.
All inputs are finite; a program needn't handle non-finite values.
Results may differ from a plain program's by a relative error of at most 0.04.
The roundings to bfloat16 on the way count: a program that leaves them out, or rounds other values in their place, can miss the bound.
Values may be sent and summed in bfloat16 or wider, within the bound.
No kernel may reach another device: no remote copies, remote signals or barrier semaphores. Data moves between devices by JAX's collectives and lax.ppermute only.
A program may use at most 256 MiB of HBM per device.

v0:
```python
import jax
import jax.numpy as jnp
from jax import lax
from jax.experimental import pallas as pl
from jax.experimental.pallas import tpu as pltpu
from jax.sharding import PartitionSpec as P

HD = 64
HEADS = 8
IMG = 784
TABLES = 3
STEP = 10
QB = 256

MASKED_SCORE = -1000000000.0
BETA_FIRST = 0.9
BETA_SECOND = 0.999
LEARN_RATE = 0.3
WEIGHT_DECAY = 0.01
ADAM_EPSILON = 1e-06
NORM_EPSILON = 1e-05

AXES = ("wide", "narrow")
F32 = jnp.float32
BF16 = jnp.bfloat16
VMEM = pl.BlockSpec(memory_space=pltpu.VMEM)
SMEM = pl.BlockSpec(memory_space=pltpu.SMEM)


def dot(left, right, left_dim, right_dim):
    return lax.dot_general(
        left, right, (((left_dim,), (right_dim,)), ((), ())), preferred_element_type=F32
    )


def normalise(hidden):
    centre = hidden - jnp.mean(hidden, axis=-1, keepdims=True)
    scale = lax.rsqrt(jnp.mean(centre * centre, axis=-1, keepdims=True) + NORM_EPSILON)
    return centre * scale, scale


def norm_back(grad, gain, normed, scale):
    inner = grad * gain
    return scale * (
        inner
        - jnp.mean(inner, axis=-1, keepdims=True)
        - normed * jnp.mean(inner * normed, axis=-1, keepdims=True)
    )


def column_sum(value):
    return jnp.sum(value, axis=0, keepdims=True)


def pipeline(chains):
    done = object()
    live = []
    waiting = list(chains)
    while live or waiting:
        if waiting:
            live.insert(0, waiting.pop(0))
        live = [chain for chain in live if next(chain, done) is not done]


def place_blocks(me, near_ref, far_ref, out_ref):
    if near_ref.shape == out_ref.shape:
        out_ref[...] = near_ref[...]
        return
    size = near_ref.shape[1]
    for k in range(2 * near_ref.shape[0]):
        ref = far_ref if k & 1 else near_ref
        row = pl.multiple_of((me ^ k) * size, size)
        out_ref[pl.ds(row, size), :] = ref[exchange_slot(k)]


def spread_blocks(me, source, near_ref, far_ref, col):
    cols = slice(col, col + source.shape[1])
    if near_ref.shape[0] == source.shape[0]:
        near_ref[:, cols] = source[...].astype(BF16)
        far_ref[...] = jnp.zeros(far_ref.shape, BF16)
        return
    size = near_ref.shape[1]
    for k in range(2 * near_ref.shape[0]):
        ref = far_ref if k & 1 else near_ref
        row = pl.multiple_of((me ^ k) * size, size)
        ref[exchange_slot(k), :, cols] = source[pl.ds(row, size), :].astype(BF16)


def project_kernel(info_ref, x_ref, near_ref, far_ref, w_ref, norm_ref, q_ref, k_ref, v_ref):
    place_blocks(info_ref[3], near_ref, far_ref, w_ref)
    width = x_ref.shape[1]
    norm_ref[...] = jnp.transpose(w_ref[:, 3 * width :].astype(F32))[0:8, :]
    for block in range(x_ref.shape[0] // QB):
        cols = slice(block * QB, (block + 1) * QB)
        x = x_ref[cols, :]
        q_ref[:, cols] = (dot(w_ref[:, 0:width], x, 0, 1).astype(BF16) * 0.125).astype(BF16)
        k_ref[:, cols] = dot(w_ref[:, width : 2 * width], x, 0, 1).astype(BF16)
        v_ref[:, cols] = dot(w_ref[:, 2 * width : 3 * width], x, 0, 1).astype(BF16)


def head_rows(index):
    return slice(index * HD, (index + 1) * HD)


def forward_heads(query, key, value, finish, heads, count, bias, score_ref, prob_ref):
    def chain(index):
        slot = index % 2
        scores = dot(key(index), query(index), 0, 0)
        score_ref[slot, 0:count] = scores if bias is None else scores + bias[0:count]
        yield
        scores = score_ref[slot, 0:count]
        highest = jnp.max(scores, axis=0, keepdims=True)
        prob_ref[slot, 0:count] = jnp.exp(scores - highest).astype(BF16)
        yield
        ones = jnp.ones((16, count), BF16)
        mixed = dot(jnp.concatenate([value(index), ones], axis=0), prob_ref[slot, 0:count], 1, 0)
        total = mixed[HD : HD + 1]
        finish(index, (mixed[0:HD] / total).astype(BF16), highest + jnp.log(total))

    pipeline([chain(index) for index in range(heads)])


def backward_heads(
    query, key, value, grad, mixed, logs, finish, heads, count, bias,
    score_ref, level_ref, prob_ref, delta_ref,
):
    def chain(index):
        slot = index % 2
        scores = dot(key(index), query(index), 0, 0)
        score_ref[slot, 0:count] = scores if bias is None else scores + bias[0:count]
        level_ref[slot, 0:count] = dot(value(index), grad(index), 0, 0)
        yield
        level = column_sum(grad(index).astype(F32) * mixed(index).astype(F32))
        probs = jnp.exp(score_ref[slot, 0:count] - logs(index))
        prob_ref[slot, 0:count] = probs.astype(BF16)
        delta_ref[slot, 0:count] = (probs * (level_ref[slot, 0:count] - level)).astype(BF16)
        yield
        delta = delta_ref[slot, 0:count]
        finish(
            index,
            (dot(key(index), delta, 1, 0) * 0.125).astype(BF16),
            dot(query(index), delta, 1, 1),
            dot(grad(index), prob_ref[slot, 0:count], 1, 1),
        )

    pipeline([chain(index) for index in range(heads)])


def self_blocks(info_ref, rows, bias, run):
    second, third, valid = info_ref[0], info_ref[1], info_ref[2]

    def step(block, carry):
        start = block * QB
        first = jnp.where(start < second, 0, jnp.where(start < third, second, third))
        back = block - first // QB
        for extent in range(3):

            @pl.when(back == extent)
            def _():
                begin = (block - extent) * QB
                count = (extent + 1) * QB
                place = start + lax.broadcasted_iota(jnp.int32, (1, QB), 1)
                low = jnp.where(place < second, 0, jnp.where(place < third, second, third))
                high = jnp.minimum(place, valid - 1)
                key = begin + lax.broadcasted_iota(jnp.int32, (count, QB), 0)
                allowed = (key >= low) & ((key <= high) | (key == place))
                bias[0:count] = jnp.where(allowed, 0.0, MASKED_SCORE)
                run(
                    pl.ds(pl.multiple_of(start, QB), QB),
                    pl.ds(pl.multiple_of(begin, QB), count),
                    count,
                )

        return carry

    lax.fori_loop(0, rows // QB, step, 0)


def self_forward_kernel(
    info_ref, q_ref, k_ref, v_ref, o_ref, log_ref, bias_ref, score_ref, prob_ref
):
    def run(cols, keys, count):
        def finish(index, mixed, logs):
            o_ref[head_rows(index), cols] = mixed
            log_ref[index, :, cols] = logs

        forward_heads(
            lambda index: q_ref[head_rows(index), cols],
            lambda index: k_ref[head_rows(index), keys],
            lambda index: v_ref[head_rows(index), keys],
            finish, q_ref.shape[0] // HD, count, bias_ref, score_ref, prob_ref,
        )

    self_blocks(info_ref, q_ref.shape[1], bias_ref, run)


def self_backward_kernel(
    info_ref, q_ref, k_ref, v_ref, o_ref, log_ref, do_ref, dq_ref, dk_ref, dv_ref,
    sum_k, sum_v, bias_ref, score_ref, level_ref, prob_ref, delta_ref,
):
    sum_k[...] = jnp.zeros(sum_k.shape, F32)
    sum_v[...] = jnp.zeros(sum_v.shape, F32)

    def run(cols, keys, count):
        def finish(index, grad_query, grad_key, grad_value):
            dq_ref[head_rows(index), cols] = grad_query
            sum_k[head_rows(index), keys] += grad_key
            sum_v[head_rows(index), keys] += grad_value

        backward_heads(
            lambda index: q_ref[head_rows(index), cols],
            lambda index: k_ref[head_rows(index), keys],
            lambda index: v_ref[head_rows(index), keys],
            lambda index: do_ref[head_rows(index), cols],
            lambda index: o_ref[head_rows(index), cols],
            lambda index: log_ref[index, :, cols],
            finish, q_ref.shape[0] // HD, count, bias_ref,
            score_ref, level_ref, prob_ref, delta_ref,
        )

    self_blocks(info_ref, q_ref.shape[1], bias_ref, run)
    dk_ref[...] = sum_k[...].astype(BF16)
    dv_ref[...] = sum_v[...].astype(BF16)


def mid_kernel(x_ref, o_ref, w_ref, norm_ref, n_ref, r_ref, q_ref):
    gain, shift = norm_ref[0:1, :], norm_ref[3:4, :]
    width = x_ref.shape[1]

    def chain(block):
        rows = slice(block * QB, (block + 1) * QB)
        branch = dot(o_ref[:, rows], w_ref[:, 0:width], 0, 0)
        yield
        normed, scale = normalise(x_ref[rows, :].astype(F32) + branch)
        n_ref[rows, :] = normed
        r_ref[rows, :] = scale
        low = (normed * gain + shift).astype(BF16)
        yield
        query = dot(w_ref[:, width : 2 * width], low, 0, 1).astype(BF16)
        q_ref[:, rows] = (query * 0.125).astype(BF16)

    pipeline([chain(block) for block in range(x_ref.shape[0] // QB)])


def image_kernel(info_ref, image_ref, near_ref, far_ref, w_ref, k_ref, v_ref):
    place_blocks(info_ref[3], near_ref, far_ref, w_ref)
    width = image_ref.shape[1]
    for table in range(TABLES):
        image = image_ref[table * IMG : (table + 1) * IMG, :]
        k_ref[table] = dot(w_ref[:, 2 * width : 3 * width], image, 0, 1).astype(BF16)
        v_ref[table] = dot(w_ref[:, 3 * width : 4 * width], image, 0, 1).astype(BF16)


def cross_blocks(info_ref, rows, run):
    def pair(index, carry):
        block = index // TABLES
        table = index % TABLES
        second, third = info_ref[0], info_ref[1]
        begin = jnp.where(table == 0, 0, jnp.where(table == 1, second, third))
        end = jnp.where(table == 0, second, jnp.where(table == 1, third, rows))
        start = block * QB

        @pl.when(jnp.logical_and(begin < start + QB, end > start))
        def _():
            place = start + lax.broadcasted_iota(jnp.int32, (1, QB), 1)
            run(pl.ds(pl.multiple_of(start, QB), QB), table, (place >= begin) & (place < end))

        return carry

    lax.fori_loop(0, rows // QB * TABLES, pair, 0)


def cross_forward_kernel(info_ref, q_ref, k_ref, v_ref, o_ref, log_ref, score_ref, prob_ref):
    def run(cols, table, here):
        def finish(index, mixed, logs):
            rows = head_rows(index)
            o_ref[rows, cols] = jnp.where(here, mixed, o_ref[rows, cols])
            log_ref[index, :, cols] = jnp.where(here, logs, log_ref[index, :, cols])

        forward_heads(
            lambda index: q_ref[head_rows(index), cols],
            lambda index: k_ref[table, head_rows(index), :],
            lambda index: v_ref[table, head_rows(index), :],
            finish, q_ref.shape[0] // HD, IMG, None, score_ref, prob_ref,
        )

    cross_blocks(info_ref, q_ref.shape[1], run)


def cross_backward_kernel(
    info_ref, q_ref, k_ref, v_ref, o_ref, log_ref, do_ref, dq_ref, dk_ref, dv_ref,
    sum_k, sum_v, score_ref, level_ref, prob_ref, delta_ref,
):
    sum_k[...] = jnp.zeros(sum_k.shape, F32)
    sum_v[...] = jnp.zeros(sum_v.shape, F32)

    def run(cols, table, here):
        def finish(index, grad_query, grad_key, grad_value):
            rows = head_rows(index)
            dq_ref[rows, cols] = jnp.where(here, grad_query, dq_ref[rows, cols])
            sum_k[table, rows, :] += grad_key
            sum_v[table, rows, :] += grad_value

        zero = jnp.zeros((), BF16)
        backward_heads(
            lambda index: q_ref[head_rows(index), cols],
            lambda index: k_ref[table, head_rows(index), :],
            lambda index: v_ref[table, head_rows(index), :],
            lambda index: jnp.where(here, do_ref[head_rows(index), cols], zero),
            lambda index: o_ref[head_rows(index), cols],
            lambda index: jnp.where(here, log_ref[index, :, cols], -MASKED_SCORE),
            finish, q_ref.shape[0] // HD, IMG, None,
            score_ref, level_ref, prob_ref, delta_ref,
        )

    cross_blocks(info_ref, q_ref.shape[1], run)
    dk_ref[...] = sum_k[...].astype(BF16)
    dv_ref[...] = sum_v[...].astype(BF16)


def feed_kernel(
    info_ref, o_ref, n1_ref, cot_ref, co_ref, up_ref, down_ref, norm_ref,
    result_ref, dh_ref, do_ref, near_ref, far_ref, dnorm_ref,
    sum_up, sum_out, sum_norm, all_x2, all_active, all_du, all_dz, all_dac,
):
    valid = info_ref[2]
    hidden_width = up_ref.shape[1]
    sum_norm[...] = jnp.zeros(sum_norm.shape, F32)
    root = 0.7978845608028654

    def chain(block):
        rows = slice(block * QB, (block + 1) * QB)
        branch = dot(o_ref[:, rows], co_ref[...], 0, 0)
        yield
        first = n1_ref[rows, :] * norm_ref[0:1, :] + norm_ref[3:4, :]
        n2, r2 = normalise(first + branch)
        x2 = n2 * norm_ref[1:2, :] + norm_ref[4:5, :]
        x2_low = x2.astype(BF16)
        all_x2[rows, :] = x2_low
        yield
        u = dot(x2_low, up_ref[...], 1, 0)
        yield
        square = u * u
        curve = jnp.tanh(root * u * (1.0 + 0.044715 * square))
        half = 0.5 * (1.0 + curve)
        active = (u * half).astype(BF16)
        slope = half + 0.5 * u * (1.0 - curve * curve) * (root * (1.0 + 3 * 0.044715 * square))
        all_active[rows, :] = active
        yield
        down = dot(active, down_ref[...], 1, 1)
        yield
        n3, r3 = normalise(x2 + down)
        result_ref[rows, :] = (n3 * norm_ref[2:3, :] + norm_ref[5:6, :]).astype(BF16)
        place = block * QB + lax.broadcasted_iota(jnp.int32, (QB, 1), 0)
        dy = jnp.where(place < valid, cot_ref[rows, :].astype(F32), 0.0)
        sum_norm[2:3, :] += column_sum(dy * n3)
        sum_norm[5:6, :] += column_sum(dy)
        dh3 = norm_back(dy, norm_ref[2:3, :], n3, r3)
        dz = dh3.astype(BF16)
        all_dz[rows, :] = dz
        yield
        df = dot(dz, down_ref[...], 1, 0)
        yield
        du = (df * slope).astype(BF16)
        all_du[rows, :] = du
        yield
        back = dot(du, up_ref[...], 1, 1)
        yield
        dx2 = dh3 + back
        sum_norm[1:2, :] += column_sum(dx2 * n2)
        sum_norm[4:5, :] += column_sum(dx2)
        dh2 = norm_back(dx2, norm_ref[1:2, :], n2, r2)
        dh_ref[rows, :] = dh2
        dac = dh2.astype(BF16)
        all_dac[rows, :] = dac
        yield
        do_ref[:, rows] = dot(co_ref[...], dac, 1, 1).astype(BF16)

    pipeline([chain(block) for block in range(cot_ref.shape[0] // QB)])
    me = info_ref[3]
    sum_up[...] = dot(all_x2[...], all_du[...], 0, 0)
    spread_blocks(me, sum_up, near_ref, far_ref, 0)
    sum_up[...] = dot(all_dz[...], all_active[...], 0, 0)
    spread_blocks(me, sum_up, near_ref, far_ref, hidden_width)
    sum_out[...] = dot(o_ref[...], all_dac[...], 1, 0)
    spread_blocks(me, sum_out, near_ref, far_ref, 2 * hidden_width)
    dnorm_ref[...] = sum_norm[...]


def inner_kernel(
    info_ref, dq0_ref, dq1_ref, dh2_ref, n1_ref, r1_ref, o_ref, w_ref, norm_ref,
    image_ref, dk0_ref, dk1_ref, dv0_ref, dv1_ref,
    dh_ref, do_ref, near_ref, far_ref, dnorm_ref, sum_image, sum_inner, sum_norm, all_low, all_da,
):
    sum_norm[...] = jnp.zeros(sum_norm.shape, F32)
    width = dh_ref.shape[1]
    gain, shift = norm_ref[0:1, :], norm_ref[3:4, :]

    def chain(block):
        rows = slice(block * QB, (block + 1) * QB)
        dq = jnp.concatenate([dq0_ref[:, rows], dq1_ref[:, rows]], axis=0)
        back = dot(dq, w_ref[:, width : 2 * width], 0, 1)
        yield
        normed = n1_ref[rows, :]
        all_low[rows, :] = (normed * gain + shift).astype(BF16)
        dx1 = dh2_ref[rows, :] + back
        sum_norm[0:1, :] += column_sum(dx1 * normed)
        sum_norm[1:2, :] += column_sum(dx1)
        dh1 = norm_back(dx1, gain, normed, r1_ref[rows, :])
        dh_ref[rows, :] = dh1
        da = dh1.astype(BF16)
        all_da[rows, :] = da
        yield
        do_ref[:, rows] = dot(w_ref[:, 0:width], da, 1, 1).astype(BF16)

    pipeline([chain(block) for block in range(dh2_ref.shape[0] // QB)])
    me = info_ref[3]
    total = None
    for table in range(TABLES):
        image = image_ref[table * IMG : (table + 1) * IMG, :]
        grads = jnp.concatenate(
            [dk0_ref[table], dk1_ref[table], dv0_ref[table], dv1_ref[table]], axis=0
        )
        part = dot(image, grads, 0, 1)
        total = part if total is None else total + part
    sum_image[...] = total
    spread_blocks(me, sum_image, near_ref, far_ref, 2 * width)
    sum_inner[...] = dot(o_ref[...], all_da[...], 1, 0)
    spread_blocks(me, sum_inner, near_ref, far_ref, 0)
    dq = jnp.concatenate([dq0_ref[...], dq1_ref[...]], axis=0)
    sum_inner[...] = dot(all_low[...], dq, 0, 1)
    spread_blocks(me, sum_inner, near_ref, far_ref, width)
    dnorm_ref[...] = sum_norm[...]


def image_grad_kernel(info_ref, dk0_ref, dk1_ref, dv0_ref, dv1_ref, w_ref, out_ref):
    width = out_ref.shape[1]
    for table in range(TABLES):
        rows = slice(table * IMG, (table + 1) * IMG)
        grads = jnp.concatenate(
            [dk0_ref[table], dk1_ref[table], dv0_ref[table], dv1_ref[table]], axis=0
        )
        out_ref[rows, :] = dot(grads, w_ref[:, 2 * width : 4 * width], 0, 1)


def project_weight_kernel(
    info_ref, x_ref, dq0_ref, dq1_ref, dk0_ref, dk1_ref, dv0_ref, dv1_ref, inner_ref, feed_ref,
    near_ref, far_ref, total,
):
    width = x_ref.shape[1]
    refs = (dq0_ref, dq1_ref, dk0_ref, dk1_ref, dv0_ref, dv1_ref)
    grads = jnp.concatenate([ref[...] for ref in refs], axis=0)
    total[:, 0 : 3 * width] = dot(x_ref[...], grads, 0, 1)
    order = [inner_ref[0:1], feed_ref[1:2], feed_ref[2:3]]
    order += [inner_ref[1:2], feed_ref[4:5], feed_ref[5:6], jnp.zeros((122, width), F32)]
    total[:, 3 * width :] = jnp.transpose(jnp.concatenate(order, axis=0))
    spread_blocks(info_ref[3], total, near_ref, far_ref, 0)


def token_grad_kernel(
    info_ref, dq0_ref, dq1_ref, dk0_ref, dk1_ref, dv0_ref, dv1_ref, w_ref, dh_ref, out_ref
):
    width = dh_ref.shape[1]
    refs = (dq0_ref, dq1_ref, dk0_ref, dk1_ref, dv0_ref, dv1_ref)
    for block in range(dh_ref.shape[0] // QB):
        rows = slice(block * QB, (block + 1) * QB)
        grads = jnp.concatenate([ref[:, rows] for ref in refs], axis=0)
        out_ref[rows, :] = dh_ref[rows, :] + dot(grads, w_ref[:, 0 : 3 * width], 0, 1)


def lamb_moments(weight, grad, first, second, decay):
    first_new = BETA_FIRST * first + (1.0 - BETA_FIRST) * grad
    second_new = BETA_SECOND * second + (1.0 - BETA_SECOND) * grad * grad
    first_hat = first_new / (1.0 - BETA_FIRST**STEP)
    second_hat = second_new / (1.0 - BETA_SECOND**STEP)
    update = first_hat / (jnp.sqrt(second_hat) + ADAM_EPSILON) + decay * weight
    return (first_new, second_new, update)


def total_of(value):
    return jnp.sum(jnp.sum(value * value, axis=0, keepdims=True), axis=1, keepdims=True)


def moments_kernel(per, *refs):
    feed, inner, last = refs[0:per], refs[per : 2 * per], refs[2 * per : 3 * per]
    wa, wf, wn, ma, va, mf, vf, mn, vn = refs[3 * per : 3 * per + 9]
    ga, gf, gn, oma, ova, omf, ovf, omn, ovn, ua, uf, un, sums = refs[3 * per + 9 :]
    width, hidden = wa.shape[2], wf.shape[2]
    lane = lax.broadcasted_iota(jnp.int32, (1, 128), 1)
    weights = jnp.zeros((1, 128), F32)
    updates = jnp.zeros((1, 128), F32)

    def grad(pieces, col, size):
        cols = slice(col, col + size)
        near = [ref[:, cols].astype(F32) for ref in pieces]
        total = near[0]
        for part in near[1:]:
            total += part
        return total

    def tensor(slot, value, index, weight, first, second, outs, decay):
        nonlocal weights, updates
        first_new, second_new, update = lamb_moments(
            weight[index], value, first[index], second[index], decay
        )
        for ref, part in zip(outs, (value, first_new, second_new, update)):
            ref[index] = part
        weights = jnp.where(lane == slot, total_of(weight[index]), weights)
        updates = jnp.where(lane == slot, total_of(update), updates)

    for slot in range(8):
        pieces, col = (last, slot) if slot < 3 else (inner, slot - 3)
        if slot == 7:
            pieces, col = feed, 2 * hidden // width
        value = grad(pieces, col * width, width)
        tensor(slot, value, slot, wa, ma, va, (ga, oma, ova, ua), WEIGHT_DECAY)
    for slot in range(2):
        value = grad(feed, slot * hidden, hidden)
        tensor(8 + slot, value, slot, wf, mf, vf, (gf, omf, ovf, uf), WEIGHT_DECAY)
    norms = jnp.transpose(grad(last, 3 * width, 128))
    for slot in range(6):
        row = slice(slot, slot + 1)
        tensor(10 + slot, norms[row, :], row, wn, mn, vn, (gn, omn, ovn, un), 0.0)
    sums[...] = jnp.concatenate([weights, updates, jnp.zeros((6, 128), F32)], axis=0)


def apply_kernel(*refs):
    wa, wf, wn, ua, uf, un, na, nf, nn = refs[-10:-1]
    pieces, norms = refs[0:-10], refs[-1]
    total = pair_sum([ref[...] for ref in pieces])
    root = jnp.sqrt(total)
    norms[...] = root
    ratio = LEARN_RATE * (root[0:1, :] / root[1:2, :])
    for slot in range(8):
        na[slot] = wa[slot] - ratio[:, slot : slot + 1] * ua[slot]
    for slot in range(2):
        nf[slot] = wf[slot] - ratio[:, slot + 8 : slot + 9] * uf[slot]
    for slot in range(6):
        row = slice(slot, slot + 1)
        nn[row] = wn[row] - ratio[:, slot + 10 : slot + 11] * un[row]


def pair_sum(parts):
    while len(parts) > 1:
        parts = [parts[i] + parts[i + 1] for i in range(0, len(parts), 2)]
    return parts[0]


def shaped(*dims, kind=BF16):
    return jax.ShapeDtypeStruct(dims, kind)


def call(kernel, out_shape, operands, name, micros, info=True, scratch=(), mib=32):
    specs = []
    operands = list(operands)
    for position, operand in enumerate(operands):
        if info and position == 0:
            specs.append(SMEM)
        elif isinstance(operand, tuple):
            array, dims, index = operand
            operands[position] = array
            specs.append(
                pl.BlockSpec(
                    dims, lambda _, index=index: index, pipeline_mode=pl.Buffered(buffer_count=1)
                )
            )
        else:
            specs.append(VMEM)
    split = any(spec.block_shape is not None for spec in specs)
    return pl.pallas_call(
        kernel,
        grid=(1,) if split else (),
        out_shape=out_shape,
        in_specs=specs,
        out_specs=jax.tree.map(lambda _: VMEM, out_shape),
        scratch_shapes=[
            pltpu.VMEM(dims[:-1], BF16) if dims[-1] is BF16 else pltpu.VMEM(dims, F32)
            for dims in scratch
        ],
        compiler_params=pltpu.CompilerParams(vmem_limit_bytes=mib * 2**20),
        cost_estimate=pl.CostEstimate(
            flops=int(micros * 1.1e9), bytes_accessed=int(micros * 3.0e6), transcendentals=0
        ),
        name=name,
    )(*operands)


def device_index():
    return lax.axis_index("wide") * lax.axis_size("narrow") + lax.axis_index("narrow")


def device_count():
    return lax.axis_size("wide") * lax.axis_size("narrow")


def exchange_slot(k):
    return (k >> 3) * 4 + ((k >> 1) & 3)


def swap(value, mask):
    count = device_count()
    return lax.ppermute(value, AXES, [(i, i ^ mask) for i in range(count)])


def before(value, *others):
    return lax.optimization_barrier((value, others))[0]


def far_masks():
    return [k << 3 for k in range(1, device_count() >> 3)]


PLANE_MASKS = [2, 4, 6]


def gather_far(part):
    return jnp.stack([part] + [swap(part, mask) for mask in far_masks()])


def gather_plane(part):
    value = jnp.stack([part] + [swap(part, mask) for mask in PLANE_MASKS], axis=1)
    return value.reshape((-1,) + part.shape[1:])


def scatter_core(near, far):
    total = near.astype(F32) + swap(far, 1).astype(F32)
    total = total.reshape((-1, 4) + near.shape[1:])
    return [total[:, k] for k in range(4)]


def scatter_plane(parts):
    sends = [part.astype(BF16) for part in parts[1:]]
    return parts[0], sends


def scatter_plane_end(own, sends):
    total = own
    for mask, send in zip(PLANE_MASKS, sends):
        total = total + swap(send, mask).astype(F32)
    return total[0], [total[k].astype(BF16) for k in range(1, total.shape[0])]


def scatter_far_end(own, sends):
    return [own] + [swap(send, mask) for mask, send in zip(far_masks(), sends)]


def block_order():
    order = [0] * device_count()
    for k in range(device_count()):
        order[exchange_slot(k) + (k & 1) * (device_count() // 2)] = k
    return jnp.array(order, jnp.int32) ^ device_index()


def whole_blocks(near, far):
    if near.shape[1] % 16 == 0:
        return near, far
    blocks = jnp.concatenate([near, far])
    full = jnp.zeros_like(blocks).at[block_order()].set(blocks)
    return full.reshape(-1, near.shape[2]), jnp.zeros((16, 128), BF16)


def spread_shapes(shard, cols):
    if shard % 16 == 0:
        return [shaped(device_count() // 2, shard, cols)] * 2
    return [shaped(device_count() * shard, cols), shaped(16, 128)]


def split_blocks(near, far):
    if near.ndim == 3:
        return near, far
    blocks = near.reshape(device_count(), -1, near.shape[1])[block_order()]
    return blocks[: device_count() // 2], blocks[device_count() // 2 :]


def pack(stack):
    return jnp.swapaxes(stack, 0, 1).reshape(stack.shape[1], -1)


def local(
    tokens,
    image,
    segments,
    valid_len,
    cotangent,
    w_attn,
    w_ffn,
    norm_params,
    momentum_attn,
    variance_attn,
    momentum_ffn,
    variance_ffn,
    momentum_norm,
    variance_norm,
):
    tags, width = tokens.shape
    hidden_width = w_ffn.shape[2]
    shard = w_attn.shape[1]
    segment = segments[0]
    info = jnp.stack(
        [jnp.sum(segment < 1), jnp.sum(segment < 2), valid_len[0], device_index()]
    ).astype(jnp.int32)

    attn_low = w_attn.astype(BF16)
    norm_low = jnp.pad(norm_params.astype(BF16).T, ((0, 0), (0, 122)))
    first_part = jnp.concatenate([pack(attn_low[0:3]), norm_low], axis=1)
    first_far = gather_far(first_part)
    second_part = before(pack(attn_low[3:7]), first_far)
    first_plane = gather_plane(first_far)
    second_far = gather_far(second_part)
    first_core = swap(first_plane, 1)
    rest_part = before(
        jnp.concatenate([pack(attn_low[7:8]), pack(w_ffn.astype(BF16))], axis=1), first_plane
    )
    rest_full = lax.all_gather(rest_part, AXES, axis=0, tiled=True)
    second_plane = gather_plane(second_far)

    wide_shape = shaped(width, tags)
    half_shape = shaped(width // 2, tags)
    log_shape = shaped(HEADS, 1, tags, kind=F32)
    f32_rows = shaped(tags, width, kind=F32)
    w_first, norms, q, k, v = call(
        project_kernel,
        [shaped(width, 3 * width + 128), shaped(8, width, kind=F32)] + [wide_shape] * 3,
        (info, tokens, *whole_blocks(first_plane, first_core)),
        "project",
        3,
    )
    o, log_self = call(
        self_forward_kernel,
        [wide_shape, log_shape],
        (before(info, second_far), q, k, v),
        "self_forward",
        10,
        True,
        [(3 * QB, QB), (2, 3 * QB, QB), (2, 3 * QB, QB, BF16)],
        24,
    )
    second_core = swap(second_plane, 1)
    image_shape = shaped(TABLES, width, IMG)
    image_half = shaped(TABLES, width // 2, IMG)
    w_second, kc, vc = call(
        image_kernel,
        [shaped(width, 4 * width)] + [image_shape] * 2,
        (info, image, *whole_blocks(second_plane, second_core)),
        "image_project",
        6,
    )
    n1, r1, qc = call(
        mid_kernel,
        [f32_rows, shaped(tags, 1, kind=F32), wide_shape],
        (tokens, o, w_second, norms),
        "mid",
        5,
        False,
    )
    oc, log_cross = call(
        cross_forward_kernel,
        [wide_shape, log_shape],
        (info, qc, kc, vc),
        "cross_forward",
        18,
        True,
        [(2, IMG, QB), (2, IMG, QB, BF16)],
        24,
    )
    co = rest_full[:, 0:width]
    up = rest_full[:, width : width + hidden_width]
    down = rest_full[:, width + hidden_width :]
    feed_cols = 2 * hidden_width + width
    result, dh2, doc, feed_near, feed_far, norm_feed = call(
        feed_kernel,
        [
            shaped(tags, width),
            f32_rows,
            wide_shape,
            *spread_shapes(shard, feed_cols),
            shaped(8, width, kind=F32),
        ],
        (info, oc, n1, cotangent, co, up, down, norms),
        "feed",
        15,
        True,
        [(width, hidden_width), (width, width), (8, width), (tags, width, BF16)]
        + [(tags, hidden_width, BF16)] * 2
        + [(tags, width, BF16)] * 2,
        40,
    )

    def half(array, index):
        axis = 1 if array.shape[0] == TABLES else 0
        dims = tuple(size // 2 if i == axis else size for i, size in enumerate(array.shape))
        return array, dims, tuple(index if i == axis else 0 for i in range(len(dims)))

    def cross_backward(index, *deps):
        parts = [half(array, index) for array in (qc, kc, vc, oc, log_cross, doc)]
        return call(
            cross_backward_kernel,
            [half_shape, image_half, image_half],
            [before(info, *deps)] + parts,
            "cross_backward",
            16,
            True,
            [(TABLES, width // 2, IMG)] * 2 + [(2, IMG, QB)] * 2 + [(2, IMG, QB, BF16)] * 2,
        )

    def self_backward(index, *deps):
        parts = [half(array, index) for array in (q, k, v, o, log_self, do)]
        return call(
            self_backward_kernel,
            [half_shape] * 3,
            [before(info, *deps)] + parts,
            "self_backward",
            8,
            True,
            [(width // 2, tags)] * 2
            + [(3 * QB, QB)]
            + [(2, 3 * QB, QB)] * 2
            + [(2, 3 * QB, QB, BF16)] * 2,
            24,
        )

    feed_near, feed_far = split_blocks(feed_near, feed_far)
    dqc0, dkc0, dvc0 = cross_backward(0)
    feed_near = before(feed_near, dqc0)
    own_feed, send_feed = scatter_plane(scatter_core(feed_near, feed_far))
    dqc1, dkc1, dvc1 = cross_backward(1, send_feed)
    own_feed = before(own_feed, dqc1)
    own_feed, send_feed = scatter_plane_end(own_feed, send_feed)
    dh1, do, inner_near, inner_far, norm_inner = call(
        inner_kernel,
        [
            f32_rows,
            wide_shape,
            *spread_shapes(shard, 4 * width),
            shaped(8, width, kind=F32),
        ],
        (before(info, send_feed), dqc0, dqc1, dh2, n1, r1, o, w_second, norms)
        + (image, dkc0, dkc1, dvc0, dvc1),
        "inner",
        10,
        True,
        [(width, 2 * width), (width, width), (8, width)] + [(tags, width, BF16)] * 2,
        36,
    )
    inner_near, inner_far = split_blocks(inner_near, inner_far)
    pieces_feed = scatter_far_end(own_feed, send_feed)
    dq0, dk0, dv0 = self_backward(0)
    inner_near = before(inner_near, dq0)
    own_inner, send_inner = scatter_plane(scatter_core(inner_near, inner_far))
    dq1, dk1, dv1 = self_backward(1, send_inner)
    grads = (dq0, dq1, dk0, dk1, dv0, dv1)
    last_cols = 3 * width + 128
    last_near, last_far = call(
        project_weight_kernel,
        spread_shapes(shard, last_cols),
        (info, tokens) + grads + (norm_inner, norm_feed),
        "project_weight",
        3,
        True,
        [(width, last_cols)],
    )
    last_near, last_far = split_blocks(last_near, last_far)
    own_inner, send_inner = scatter_plane_end(before(own_inner, dq1), send_inner)
    image_grad = call(
        image_grad_kernel,
        shaped(image.shape[0], width, kind=F32),
        (before(info, last_far, send_inner), dkc0, dkc1, dvc0, dvc1, w_second),
        "image_grad",
        7,
    )
    own_last, send_last = scatter_plane(scatter_core(before(last_near, image_grad), last_far))
    token_grad = call(
        token_grad_kernel,
        f32_rows,
        (before(info, send_last),) + grads + (w_first, dh1),
        "token_grad",
        5,
    )
    pieces_inner = scatter_far_end(own_inner, send_inner)
    own_last, send_last = scatter_plane_end(before(own_last, token_grad), send_last)
    pieces_last = scatter_far_end(own_last, send_last)

    weights = (w_attn, w_ffn, norm_params)
    moments = (momentum_attn, variance_attn, momentum_ffn, variance_ffn)
    moments = moments + (momentum_norm, variance_norm)
    like = [shaped(*array.shape, kind=F32) for array in weights + moments + weights]
    pieces = [*pieces_feed, *pieces_inner, *pieces_last]
    per_chunk = len(pieces) // 3
    outs = call(
        lambda *refs: moments_kernel(per_chunk, *refs),
        like + [shaped(8, 128, kind=F32)],
        (*pieces, *weights, *moments),
        "moments",
        3,
        False,
    )
    grad_attn, grad_ffn, grad_norm = outs[0:3]
    first_attn, second_attn, first_ffn, second_ffn, first_norm, second_norm = outs[3:9]
    sums = outs[12]
    sums = sums + swap(sums, 1)
    sums = pair_sum([sums] + [swap(sums, mask) for mask in PLANE_MASKS])
    pieces = [sums] + [swap(sums, mask) for mask in far_masks()]
    new_attn, new_ffn, new_norm, norms_both = call(
        apply_kernel,
        like[0:3] + [shaped(8, 128, kind=F32)],
        (*pieces, *weights, *outs[9:12]),
        "apply",
        2,
        False,
    )
    weight_norms = norms_both[0, 0:16]
    update_norms = norms_both[1, 0:16]
    return (
        result,
        token_grad,
        image_grad,
        grad_attn,
        grad_ffn,
        grad_norm,
        new_attn,
        new_ffn,
        new_norm,
        first_attn,
        second_attn,
        first_ffn,
        second_ffn,
        first_norm,
        second_norm,
        weight_norms,
        update_norms,
    )


def solution(mesh):
    rows = P(AXES, None)
    stack = P(None, AXES, None)
    flat = P(None, AXES)
    in_specs = (rows, rows, rows, P(AXES), rows) + (stack, stack, flat)
    in_specs = in_specs + (stack, stack, stack, stack, flat, flat)
    out_specs = (rows, rows, rows, stack, stack, flat, stack, stack, flat)
    out_specs = out_specs + (stack, stack, stack, stack, flat, flat, P(), P())
    return jax.shard_map(local, mesh=mesh, in_specs=in_specs, out_specs=out_specs, check_vma=False)
```

profile of v0, /device:TPU:0, one launch (start us, length us, event | category | flops | bytes accessed | tf_op | source)
XLA Modules:
  0.0 233.0 jit_solution(11302243267119004364)
XLA Ops:
  9.0 4.1 %collective-permute-start.1 = (bf16[16,1664]{1,0:T(8,128)(2,1)S(1)}, bf16[16,1664]{1,0:T(8,128)(2,1)S(1)}, u32[]{:S(2)}, u32[]{:S(2)}) collective-permute-start(bf16[16,1664]{1,0:T(8,128)(2,1)S(1)} %get-tuple-element.192), channel_id=1, source_target_pairs={{0,16},{1,17},{2,18},{3,19},{4,20},{5,21},{6,22},{7,23},{8,24},{9,... | collective-permute-start | bytes 159752 | tf_op jit(solution)/shard_map/ppermute | solution.py:602
  17.3 3.4 %collective-permute-done.2 = bf16[16,1664]{1,0:T(8,128)(2,1)S(1)} collective-permute-done((bf16[16,1664]{1,0:T(8,128)(2,1)S(1)}, bf16[16,1664]{1,0:T(8,128)(2,1)S(1)}, u32[]{:S(2)}, u32[]{:S(2)}) %collective-permute-start.2) | collective-permute-done | bytes 53280 | tf_op jit(solution)/shard_map/ppermute | solution.py:602
  25.1 3.5 %collective-permute-done.7 = bf16[4,16,1664]{2,1,0:T(8,128)(2,1)S(1)} collective-permute-done((bf16[4,16,1664]{2,1,0:T(8,128)(2,1)S(1)}, bf16[4,16,1664]{2,1,0:T(8,128)(2,1)S(1)}, u32[]{:S(2)}, u32[]{:S(2)}) %collective-permute-start.7) | collective-permute-done | bytes 213024 | tf_op jit(solution)/shard_map/ppermute | solution.py:602
  28.6 3.4 %collective-permute-done.6 = bf16[4,16,1664]{2,1,0:T(8,128)(2,1)S(1)} collective-permute-done((bf16[4,16,1664]{2,1,0:T(8,128)(2,1)S(1)}, bf16[4,16,1664]{2,1,0:T(8,128)(2,1)S(1)}, u32[]{:S(2)}, u32[]{:S(2)}) %collective-permute-start.6) | collective-permute-done | bytes 213024 | tf_op jit(solution)/shard_map/ppermute | solution.py:602
  39.3 2.9 %collective-permute-done.11 = bf16[4,16,2048]{2,1,0:T(8,128)(2,1)S(1)} collective-permute-done((bf16[4,16,2048]{2,1,0:T(8,128)(2,1)S(1)}, bf16[4,16,2048]{2,1,0:T(8,128)(2,1)S(1)}, u32[]{:S(2)}, u32[]{:S(2)}) %collective-permute-start.11) | collective-permute-done | bytes 262176 | tf_op jit(solution)/shard_map/ppermute | solution.py:602
  42.3 2.1 collective-permute-done.10
  44.4 4.5 %collective-permute-done.12 = bf16[4,16,2048]{2,1,0:T(8,128)(2,1)S(1)} collective-permute-done((bf16[4,16,2048]{2,1,0:T(8,128)(2,1)S(1)}, bf16[4,16,2048]{2,1,0:T(8,128)(2,1)S(1)}, u32[]{:S(2)}, u32[]{:S(2)}) %collective-permute-start.12) | collective-permute-done | bytes 262176 | tf_op jit(solution)/shard_map/ppermute | solution.py:602
  50.1 2.5 %project.1 = (bf16[512,1664]{1,0:T(8,128)(2,1)S(1)}, f32[8,512]{1,0:T(8,128)S(1)}, bf16[512,1024]{1,0:T(8,128)(2,1)S(1)}, bf16[512,1024]{1,0:T(8,128)(2,1)S(1)}, bf16[512,1024]{1,0:T(8,128)(2,1)S(1)}) custom-call(s32[4]{0:T(128)S(1)} %pad_add_fusion.info_ref, bf16[1024,512]{1,0:T(8,128)(2,1)S(1)} %copy-done.5, bf16[16,16,1664]{2,1,0:T(8,128)(2,1)S(1)} %bitcast.98, ...), custom_call_target="tpu_custom_call" | custom-call | flops 3300000000 | bytes 9000000 | tf_op jit(solution)/shard_map/project/pallas_call | solution.py:570
  52.7 6.8 %self_forward.1 = (bf16[512,1024]{1,0:T(8,128)(2,1)S(1)}, f32[8,1,1024]{2,1,0:T(1,128)S(1)}) custom-call(s32[4]{0:T(128)S(1)} %pad_add_fusion.info_ref, bf16[512,1024]{1,0:T(8,128)(2,1)S(1)} %get-tuple-element.90.q_ref, bf16[512,1024]{1,0:T(8,128)(2,1)S(1)} %get-tuple-element.91.k_ref, bf16[512,1024]{1,0:T(8,128)(2,1)S(1)} %get-tuple-element.92.v_ref), custom_call_target="tpu_custom_call" | custom-call | flops 11000000512 | bytes 30000000 | tf_op jit(solution)/shard_map/self_forward/pallas_call | solution.py:570
  59.6 4.1 %image_project.1 = (bf16[512,2048]{1,0:T(8,128)(2,1)S(1)}, bf16[3,512,784]{2,1,0:T(8,128)(2,1)S(1)}, bf16[3,512,784]{2,1,0:T(8,128)(2,1)S(1)}) custom-call(s32[4]{0:T(128)S(1)} %pad_add_fusion.info_ref, bf16[2352,512]{1,0:T(8,128)(2,1)S(1)} %copy-done.3, bf16[16,16,2048]{2,1,0:T(8,128)(2,1)S(1)} %bitcast.96, ...), custom_call_target="tpu_custom_call" | custom-call | flops 6600000000 | bytes 18000000 | tf_op jit(solution)/shard_map/image_project/pallas_call | solution.py:570
  66.9 13.4 %cross_forward.1 = (bf16[512,1024]{1,0:T(8,128)(2,1)S(1)}, f32[8,1,1024]{2,1,0:T(1,128)S(1)}) custom-call(s32[4]{0:T(128)S(1)} %pad_add_fusion.info_ref, bf16[512,1024]{1,0:T(8,128)(2,1)S(1)} %get-tuple-element.96.q_ref, bf16[3,512,784]{2,1,0:T(8,128)(2,1)S(1)} %get-tuple-element.97.k_ref, bf16[3,512,784]{2,1,0:T(8,128)(2,1)S(1)} %get-tuple-element.98.v_ref), custom_call_target="tpu_custom_call" | custom-call | flops 19800000512 | bytes 54000000 | tf_op jit(solution)/shard_map/cross_forward/pallas_call | solution.py:570
  82.3 10.2 %all-gather.2.cloned.1.call-done = bf16[512,2560]{1,0:T(8,128)(2,1)} async-done(((bf16[16,2560]{1,0:T(8,128)(2,1)}), bf16[512,2560]{1,0:T(8,128)(2,1)}) %all-gather.2.cloned.1.call-update) | async-done | bytes 2621456 | tf_op jit(solution)/shard_map/all_gather | solution.py:714
  95.8 13.3 %feed.1 = (bf16[1024,512]{1,0:T(8,128)(2,1)}, f32[1024,512]{1,0:T(8,128)S(1)}, bf16[512,1024]{1,0:T(8,128)(2,1)S(1)}, bf16[16,16,2560]{2,1,0:T(8,128)(2,1)S(1)},...) custom-call(s32[4]{0:T(128)S(1)} %pad_add_fusion.info_ref, bf16[512,1024]{1,0:T(8,128)(2,1)S(1)} %copy-done.34, ...), custom_call_target="tpu_custom_call" | custom-call | flops 16499999744 | bytes 45000000 | tf_op jit(solution)/shard_map/feed/pallas_call | solution.py:570
  109.4 12.4 %cross_backward.2 = (bf16[256,1024]{1,0:T(8,128)(2,1)S(1)}, bf16[3,256,784]{2,1,0:T(8,128)(2,1)S(1)}, bf16[3,256,784]{2,1,0:T(8,128)(2,1)S(1)}) custom-call(s32[4]{0:T(128)S(1)} %pad_add_fusion.info_ref, bf16[512,1024]{1,0:T(8,128)(2,1)S(1)} %copy-done.30, bf16[3,512,784]{2,1,0:T(8,128)(2,1)S(1)} %copy-done.24, bf16[3,512,784]{2,1,0:T(8,128)(2,1)S(1)} %copy-done.26, ...), custom_call_target="tpu_custom_call" | custom-call | flops 17600000000 | bytes 48000000 | tf_op jit(solution)/shard_map/cross_backward/pallas_call | solution.py:570
  122.4 3.7 %collective-permute-start.15 = (bf16[4,16,2560]{2,1,0:T(8,128)(2,1)S(1)}, bf16[4,16,2560]{2,1,0:T(8,128)(2,1)S(1)}, u32[]{:S(2)}, u32[]{:S(2)}) collective-permute-start(bf16[4,16,2560]{2,1,0:T(8,128)(2,1)S(1)} %get-tuple-element.169), channel_id=1, source_target_pairs={{0,2},{1,3},{2,0},{3,1},{4,6},{5,7},{6,4},{7,5},{8,10},{9,11},{10,... | collective-permute-start | bytes 983048 | tf_op jit(solution)/shard_map/ppermute | solution.py:602
  127.6 12.4 %cross_backward.3 = (bf16[256,1024]{1,0:T(8,128)(2,1)S(1)}, bf16[3,256,784]{2,1,0:T(8,128)(2,1)S(1)}, bf16[3,256,784]{2,1,0:T(8,128)(2,1)S(1)}) custom-call(s32[4]{0:T(128)S(1)} %pad_add_fusion.info_ref, bf16[512,1024]{1,0:T(8,128)(2,1)S(1)} %copy-done.30, bf16[3,512,784]{2,1,0:T(8,128)(2,1)S(1)} %copy-done.24, bf16[3,512,784]{2,1,0:T(8,128)(2,1)S(1)} %copy-done.26, ...), custom_call_target="tpu_custom_call" | custom-call | flops 17600000000 | bytes 48000000 | tf_op jit(solution)/shard_map/cross_backward/pallas_call | solution.py:570
  140.7 4.6 %collective-permute-start.25 = (bf16[16,2560]{1,0:T(8,128)(2,1)S(1)}, bf16[16,2560]{1,0:T(8,128)(2,1)S(1)}, u32[]{:S(2)}, u32[]{:S(2)}) collective-permute-start(bf16[16,2560]{1,0:T(8,128)(2,1)S(1)} %get-tuple-element.178), channel_id=1, source_target_pairs={{0,24},{1,25},{2,26},{3,27},{4,28},{5,29},{6,30},{7,31},{8,16},{9,... | collective-permute-start | bytes 245768 | tf_op jit(solution)/shard_map/ppermute | solution.py:602
  145.3 9.5 %inner.1 = (f32[1024,512]{1,0:T(8,128)S(1)}, bf16[512,1024]{1,0:T(8,128)(2,1)S(1)}, bf16[16,16,2048]{2,1,0:T(8,128)(2,1)S(1)}, bf16[16,16,2048]{2,1,0:T(8,128)(2,1)S(1)}, f32[8,512]{1,0:T(8,128)S(1)}) custom-call(s32[4]{0:T(128)S(1)} %pad_add_fusion.info_ref, bf16[256,1024]{1,0:T(8,128)(2,1)S(1)} %get-tuple-element.107.dq0_ref, ...), custom_call_target="tpu_custom_call" | custom-call | flops 11000000512 | bytes 30000000 | tf_op jit(solution)/shard_map/inner/pallas_call | solution.py:570
  154.9 5.7 %self_backward.2 = (bf16[256,1024]{1,0:T(8,128)(2,1)S(1)}, bf16[256,1024]{1,0:T(8,128)(2,1)S(1)}, bf16[256,1024]{1,0:T(8,128)(2,1)S(1)}) custom-call(s32[4]{0:T(128)S(1)} %pad_add_fusion.info_ref, bf16[512,1024]{1,0:T(8,128)(2,1)S(1)} %copy-done.16, bf16[512,1024]{1,0:T(8,128)(2,1)S(1)} %copy-done.18, bf16[512,1024]{1,0:T(8,128)(2,1)S(1)} %copy-done.20, ...), custom_call_target="tpu_custom_call" | custom-call | flops 8800000000 | bytes 24000000 | tf_op jit(solution)/shard_map/self_backward/pallas_call | solution.py:570
  161.2 3.0 %collective-permute-start.21 = (bf16[4,16,2048]{2,1,0:T(8,128)(2,1)S(1)}, bf16[4,16,2048]{2,1,0:T(8,128)(2,1)S(1)}, u32[]{:S(2)}, u32[]{:S(2)}) collective-permute-start(bf16[4,16,2048]{2,1,0:T(8,128)(2,1)S(1)} %get-tuple-element.172), channel_id=1, source_target_pairs={{0,6},{1,7},{2,4},{3,5},{4,2},{5,3},{6,0},{7,1},{8,14},{9,15},{10,... | collective-permute-start | bytes 786440 | tf_op jit(solution)/shard_map/ppermute | solution.py:602
  165.3 6.0 %self_backward.3 = (bf16[256,1024]{1,0:T(8,128)(2,1)S(1)}, bf16[256,1024]{1,0:T(8,128)(2,1)S(1)}, bf16[256,1024]{1,0:T(8,128)(2,1)S(1)}) custom-call(s32[4]{0:T(128)S(1)} %pad_add_fusion.info_ref, bf16[512,1024]{1,0:T(8,128)(2,1)S(1)} %copy-done.16, bf16[512,1024]{1,0:T(8,128)(2,1)S(1)} %copy-done.18, bf16[512,1024]{1,0:T(8,128)(2,1)S(1)} %copy-done.20, ...), custom_call_target="tpu_custom_call" | custom-call | flops 8800000000 | bytes 24000000 | tf_op jit(solution)/shard_map/self_backward/pallas_call | solution.py:570
  171.2 2.5 %project_weight.1 = (bf16[16,16,1664]{2,1,0:T(8,128)(2,1)S(1)}, bf16[16,16,1664]{2,1,0:T(8,128)(2,1)S(1)}) custom-call(s32[4]{0:T(128)S(1)} %pad_add_fusion.info_ref, bf16[1024,512]{1,0:T(8,128)(2,1)S(1)} %copy-done.6, bf16[256,1024]{1,0:T(8,128)(2,1)S(1)} %get-tuple-element.121.dq0_ref, bf16[256,1024]{1,0:T(8,128)(2,1)S(1)} %get-tuple-element.126.dq1_ref, ...), custom_call_target="tpu_custom_call" | custom-call | flops 3300000000 | bytes 9000000 | tf_op jit(solution)/shard_map/project_weight/pallas_call | solution.py:570
  173.9 2.2 collective-permute-done.20
  176.6 5.4 %image_grad.1 = f32[2352,512]{1,0:T(8,128)} custom-call(s32[4]{0:T(128)S(1)} %pad_add_fusion.info_ref, bf16[3,256,784]{2,1,0:T(8,128)(2,1)S(1)} %get-tuple-element.116.dk0_ref, bf16[3,256,784]{2,1,0:T(8,128)(2,1)S(1)} %get-tuple-element.117.dk1_ref, bf16[3,256,784]{2,1,0:T(8,128)(2,1)S(1)} %get-tuple-element.118.dv0_ref, ...), custom_call_target="tpu_custom_call" | custom-call | flops 7699999744 | bytes 21000000 | tf_op jit(solution)/shard_map/image_grad/pallas_call | solution.py:570
  182.3 2.7 %collective-permute-start.31 = (bf16[4,16,1664]{2,1,0:T(8,128)(2,1)S(1)}, bf16[4,16,1664]{2,1,0:T(8,128)(2,1)S(1)}, u32[]{:S(2)}, u32[]{:S(2)}) collective-permute-start(bf16[4,16,1664]{2,1,0:T(8,128)(2,1)S(1)} %get-tuple-element.175), channel_id=1, source_target_pairs={{0,6},{1,7},{2,4},{3,5},{4,2},{5,3},{6,0},{7,1},{8,14},{9,15},{10,... | collective-permute-start | bytes 638984 | tf_op jit(solution)/shard_map/ppermute | solution.py:602
  186.2 3.7 %token_grad.1 = f32[1024,512]{1,0:T(8,128)} custom-call(s32[4]{0:T(128)S(1)} %pad_add_fusion.info_ref, bf16[256,1024]{1,0:T(8,128)(2,1)S(1)} %get-tuple-element.121.dq0_ref, bf16[256,1024]{1,0:T(8,128)(2,1)S(1)} %get-tuple-element.126.dq1_ref, bf16[256,1024]{1,0:T(8,128)(2,1)S(1)} %get-tuple-element.127.dk0_ref, ...), custom_call_target="tpu_custom_call" | custom-call | flops 5500000256 | bytes 15000000 | tf_op jit(solution)/shard_map/token_grad/pallas_call | solution.py:570
  191.4 2.5 %collective-permute-start.23 = (bf16[16,2560]{1,0:T(8,128)(2,1)S(1)}, bf16[16,2560]{1,0:T(8,128)(2,1)S(1)}, u32[]{:S(2)}, u32[]{:S(2)}) collective-permute-start(bf16[16,2560]{1,0:T(8,128)(2,1)S(1)} %get-tuple-element.180), channel_id=1, source_target_pairs={{0,8},{1,9},{2,10},{3,11},{4,12},{5,13},{6,14},{7,15},{8,0},{9,1},... | collective-permute-start | bytes 245768 | tf_op jit(solution)/shard_map/ppermute | solution.py:602
  195.1 2.4 %collective-permute-start.28 = (bf16[16,2048]{1,0:T(8,128)(2,1)S(1)}, bf16[16,2048]{1,0:T(8,128)(2,1)S(1)}, u32[]{:S(2)}, u32[]{:S(2)}) collective-permute-start(bf16[16,2048]{1,0:T(8,128)(2,1)S(1)} %get-tuple-element.181), channel_id=1, source_target_pairs={{0,24},{1,25},{2,26},{3,27},{4,28},{5,29},{6,30},{7,31},{8,16},{9,... | collective-permute-start | bytes 196616 | tf_op jit(solution)/shard_map/ppermute | solution.py:602
  199.7 2.4 %collective-permute-start.34 = (bf16[16,1664]{1,0:T(8,128)(2,1)S(1)}, bf16[16,1664]{1,0:T(8,128)(2,1)S(1)}, u32[]{:S(2)}, u32[]{:S(2)}) collective-permute-start(bf16[16,1664]{1,0:T(8,128)(2,1)S(1)} %get-tuple-element.186), channel_id=1, source_target_pairs={{0,24},{1,25},{2,26},{3,27},{4,28},{5,29},{6,30},{7,31},{8,16},{9,... | collective-permute-start | bytes 159752 | tf_op jit(solution)/shard_map/ppermute | solution.py:602
  202.8 2.6 %collective-permute-start.32 = (bf16[16,1664]{1,0:T(8,128)(2,1)S(1)}, bf16[16,1664]{1,0:T(8,128)(2,1)S(1)}, u32[]{:S(2)}, u32[]{:S(2)}) collective-permute-start(bf16[16,1664]{1,0:T(8,128)(2,1)S(1)} %get-tuple-element.188), channel_id=1, source_target_pairs={{0,8},{1,9},{2,10},{3,11},{4,12},{5,13},{6,14},{7,15},{8,0},{9,1},... | collective-permute-start | bytes 159752 | tf_op jit(solution)/shard_map/ppermute | solution.py:602
  205.5 2.2 collective-permute-done.27.refs_6_
  217.7 2.3 collective-permute-start.41
  (186 shorter events, 54.6 us)
Async XLA Ops:
  7.2 85.3 %all-gather.2.cloned.1.call-start = ((), (), s32[]{:S(2)}) async-start(), calls=%async_computation | async-start | bytes 2703360 | tf_op jit(solution)/shard_map/all_gather | solution.py:714
  9.0 6.9 %collective-permute-start.1 = (bf16[16,1664]{1,0:T(8,128)(2,1)S(1)}, bf16[16,1664]{1,0:T(8,128)(2,1)S(1)}, u32[]{:S(2)}, u32[]{:S(2)}) collective-permute-start(bf16[16,1664]{1,0:T(8,128)(2,1)S(1)} %get-tuple-element.192), channel_id=1, source_target_pairs={{0,16},{1,17},{2,18},{3,19},{4,20},{5,21},{6,22},{7,23},{8,24},{9,... | collective-permute-start | bytes 159752 | tf_op jit(solution)/shard_map/ppermute | solution.py:602
  20.7 7.8 %collective-permute-start.7 = (bf16[4,16,1664]{2,1,0:T(8,128)(2,1)S(1)}, bf16[4,16,1664]{2,1,0:T(8,128)(2,1)S(1)}, u32[]{:S(2)}, u32[]{:S(2)}) collective-permute-start(bf16[4,16,1664]{2,1,0:T(8,128)(2,1)S(1)} %get-tuple-element.190), channel_id=1, source_target_pairs={{0,4},{1,5},{2,6},{3,7},{4,0},{5,1},{6,2},{7,3},{8,12},{9,13},{10,... | collective-permute-start | bytes 638984 | tf_op jit(solution)/shard_map/ppermute | solution.py:602
  22.3 9.8 %collective-permute-start.6 = (bf16[4,16,1664]{2,1,0:T(8,128)(2,1)S(1)}, bf16[4,16,1664]{2,1,0:T(8,128)(2,1)S(1)}, u32[]{:S(2)}, u32[]{:S(2)}) collective-permute-start(bf16[4,16,1664]{2,1,0:T(8,128)(2,1)S(1)} %get-tuple-element.190), channel_id=1, source_target_pairs={{0,2},{1,3},{2,0},{3,1},{4,6},{5,7},{6,4},{7,5},{8,10},{9,11},{10,... | collective-permute-start | bytes 638984 | tf_op jit(solution)/shard_map/ppermute | solution.py:602
  23.8 8.3 %collective-permute-start.8 = (bf16[4,16,1664]{2,1,0:T(8,128)(2,1)S(1)}, bf16[4,16,1664]{2,1,0:T(8,128)(2,1)S(1)}, u32[]{:S(2)}, u32[]{:S(2)}) collective-permute-start(bf16[4,16,1664]{2,1,0:T(8,128)(2,1)S(1)} %get-tuple-element.190), channel_id=1, source_target_pairs={{0,6},{1,7},{2,4},{3,5},{4,2},{5,3},{6,0},{7,1},{8,14},{9,15},{10,... | collective-permute-start | bytes 638984 | tf_op jit(solution)/shard_map/ppermute | solution.py:602
  24.3 8.8 %collective-permute-start.5 = (bf16[16,2048]{1,0:T(8,128)(2,1)S(1)}, bf16[16,2048]{1,0:T(8,128)(2,1)S(1)}, u32[]{:S(2)}, u32[]{:S(2)}) collective-permute-start(bf16[16,2048]{1,0:T(8,128)(2,1)S(1)} %bitcast.105), channel_id=1, source_target_pairs={{0,24},{1,25},{2,26},{3,27},{4,28},{5,29},{6,30},{7,31},{8,16},{9,... | collective-permute-start | bytes 196616 | tf_op jit(solution)/shard_map/ppermute | solution.py:602
  25.1 8.0 %collective-permute-start.4 = (bf16[16,2048]{1,0:T(8,128)(2,1)S(1)}, bf16[16,2048]{1,0:T(8,128)(2,1)S(1)}, u32[]{:S(2)}, u32[]{:S(2)}) collective-permute-start(bf16[16,2048]{1,0:T(8,128)(2,1)S(1)} %bitcast.106), channel_id=1, source_target_pairs={{0,16},{1,17},{2,18},{3,19},{4,20},{5,21},{6,22},{7,23},{8,24},{9,... | collective-permute-start | bytes 196616 | tf_op jit(solution)/shard_map/ppermute | solution.py:602
  32.3 16.9 %collective-permute-start.9 = (bf16[16,16,1664]{2,1,0:T(8,128)(2,1)S(1)}, bf16[16,16,1664]{2,1,0:T(8,128)(2,1)S(1)}, u32[]{:S(2)}, u32[]{:S(2)}) collective-permute-start(bf16[16,16,1664]{2,1,0:T(8,128)(2,1)S(1)} %bitcast.97), channel_id=1, source_target_pairs={{0,1},{1,0},{2,3},{3,2},{4,5},{5,4},{6,7},{7,6},{8,9},{9,8},{10,11... | collective-permute-start | bytes 2555912 | tf_op jit(solution)/shard_map/ppermute | solution.py:602
  33.1 9.2 %collective-permute-start.11 = (bf16[4,16,2048]{2,1,0:T(8,128)(2,1)S(1)}, bf16[4,16,2048]{2,1,0:T(8,128)(2,1)S(1)}, u32[]{:S(2)}, u32[]{:S(2)}) collective-permute-start(bf16[4,16,2048]{2,1,0:T(8,128)(2,1)S(1)} %get-tuple-element.185), channel_id=1, source_target_pairs={{0,4},{1,5},{2,6},{3,7},{4,0},{5,1},{6,2},{7,3},{8,12},{9,13},{10,... | collective-permute-start | bytes 786440 | tf_op jit(solution)/shard_map/ppermute | solution.py:602
  34.3 10.1 %collective-permute-start.10 = (bf16[4,16,2048]{2,1,0:T(8,128)(2,1)S(1)}, bf16[4,16,2048]{2,1,0:T(8,128)(2,1)S(1)}, u32[]{:S(2)}, u32[]{:S(2)}) collective-permute-start(bf16[4,16,2048]{2,1,0:T(8,128)(2,1)S(1)} %get-tuple-element.185), channel_id=1, source_target_pairs={{0,2},{1,3},{2,0},{3,1},{4,6},{5,7},{6,4},{7,5},{8,10},{9,11},{10,... | collective-permute-start | bytes 786440 | tf_op jit(solution)/shard_map/ppermute | solution.py:602
  35.8 13.1 %collective-permute-start.12 = (bf16[4,16,2048]{2,1,0:T(8,128)(2,1)S(1)}, bf16[4,16,2048]{2,1,0:T(8,128)(2,1)S(1)}, u32[]{:S(2)}, u32[]{:S(2)}) collective-permute-start(bf16[4,16,2048]{2,1,0:T(8,128)(2,1)S(1)} %get-tuple-element.185), channel_id=1, source_target_pairs={{0,6},{1,7},{2,4},{3,5},{4,2},{5,3},{6,0},{7,1},{8,14},{9,15},{10,... | collective-permute-start | bytes 786440 | tf_op jit(solution)/shard_map/ppermute | solution.py:602
  49.1 10.5 %collective-permute-start.13 = (bf16[16,16,2048]{2,1,0:T(8,128)(2,1)S(1)}, bf16[16,16,2048]{2,1,0:T(8,128)(2,1)S(1)}, u32[]{:S(2)}, u32[]{:S(2)}) collective-permute-start(bf16[16,16,2048]{2,1,0:T(8,128)(2,1)S(1)} %bitcast.95), channel_id=1, source_target_pairs={{0,1},{1,0},{2,3},{3,2},{4,5},{5,4},{6,7},{7,6},{8,9},{9,8},{10,11... | collective-permute-start | bytes 3145736 | tf_op jit(solution)/shard_map/ppermute | solution.py:602
  109.1 12.7 %collective-permute-start.14 = (bf16[16,16,2560]{2,1,0:T(8,128)(2,1)S(1)}, bf16[16,16,2560]{2,1,0:T(8,128)(2,1)S(1)}, u32[]{:S(2)}, u32[]{:S(2)}) collective-permute-start(bf16[16,16,2560]{2,1,0:T(8,128)(2,1)S(1)} %get-tuple-element.109), channel_id=1, source_target_pairs={{0,1},{1,0},{2,3},{3,2},{4,5},{5,4},{6,7},{7,6},{8,9},{9,8},{10,11... | collective-permute-start | bytes 3932168 | tf_op jit(solution)/shard_map/ppermute | solution.py:602
  122.4 17.8 %collective-permute-start.15 = (bf16[4,16,2560]{2,1,0:T(8,128)(2,1)S(1)}, bf16[4,16,2560]{2,1,0:T(8,128)(2,1)S(1)}, u32[]{:S(2)}, u32[]{:S(2)}) collective-permute-start(bf16[4,16,2560]{2,1,0:T(8,128)(2,1)S(1)} %get-tuple-element.169), channel_id=1, source_target_pairs={{0,2},{1,3},{2,0},{3,1},{4,6},{5,7},{6,4},{7,5},{8,10},{9,11},{10,... | collective-permute-start | bytes 983048 | tf_op jit(solution)/shard_map/ppermute | solution.py:602
  126.1 14.1 %collective-permute-start.17 = (bf16[4,16,2560]{2,1,0:T(8,128)(2,1)S(1)}, bf16[4,16,2560]{2,1,0:T(8,128)(2,1)S(1)}, u32[]{:S(2)}, u32[]{:S(2)}) collective-permute-start(bf16[4,16,2560]{2,1,0:T(8,128)(2,1)S(1)} %get-tuple-element.170), channel_id=1, source_target_pairs={{0,6},{1,7},{2,4},{3,5},{4,2},{5,3},{6,0},{7,1},{8,14},{9,15},{10,... | collective-permute-start | bytes 983048 | tf_op jit(solution)/shard_map/ppermute | solution.py:602
  127.3 13.2 %collective-permute-start.16 = (bf16[4,16,2560]{2,1,0:T(8,128)(2,1)S(1)}, bf16[4,16,2560]{2,1,0:T(8,128)(2,1)S(1)}, u32[]{:S(2)}, u32[]{:S(2)}) collective-permute-start(bf16[4,16,2560]{2,1,0:T(8,128)(2,1)S(1)} %get-tuple-element.171), channel_id=1, source_target_pairs={{0,4},{1,5},{2,6},{3,7},{4,0},{5,1},{6,2},{7,3},{8,12},{9,13},{10,... | collective-permute-start | bytes 983048 | tf_op jit(solution)/shard_map/ppermute | solution.py:602
  140.7 58.6 %collective-permute-start.25 = (bf16[16,2560]{1,0:T(8,128)(2,1)S(1)}, bf16[16,2560]{1,0:T(8,128)(2,1)S(1)}, u32[]{:S(2)}, u32[]{:S(2)}) collective-permute-start(bf16[16,2560]{1,0:T(8,128)(2,1)S(1)} %get-tuple-element.178), channel_id=1, source_target_pairs={{0,24},{1,25},{2,26},{3,27},{4,28},{5,29},{6,30},{7,31},{8,16},{9,... | collective-permute-start | bytes 245768 | tf_op jit(solution)/shard_map/ppermute | solution.py:602
  145.3 54.4 %collective-permute-start.24 = (bf16[16,2560]{1,0:T(8,128)(2,1)S(1)}, bf16[16,2560]{1,0:T(8,128)(2,1)S(1)}, u32[]{:S(2)}, u32[]{:S(2)}) collective-permute-start(bf16[16,2560]{1,0:T(8,128)(2,1)S(1)} %get-tuple-element.179), channel_id=1, source_target_pairs={{0,16},{1,17},{2,18},{3,19},{4,20},{5,21},{6,22},{7,23},{8,24},{9,... | collective-permute-start | bytes 245768 | tf_op jit(solution)/shard_map/ppermute | solution.py:602
  161.2 12.6 %collective-permute-start.21 = (bf16[4,16,2048]{2,1,0:T(8,128)(2,1)S(1)}, bf16[4,16,2048]{2,1,0:T(8,128)(2,1)S(1)}, u32[]{:S(2)}, u32[]{:S(2)}) collective-permute-start(bf16[4,16,2048]{2,1,0:T(8,128)(2,1)S(1)} %get-tuple-element.172), channel_id=1, source_target_pairs={{0,6},{1,7},{2,4},{3,5},{4,2},{5,3},{6,0},{7,1},{8,14},{9,15},{10,... | collective-permute-start | bytes 786440 | tf_op jit(solution)/shard_map/ppermute | solution.py:602
  164.2 11.9 %collective-permute-start.20 = (bf16[4,16,2048]{2,1,0:T(8,128)(2,1)S(1)}, bf16[4,16,2048]{2,1,0:T(8,128)(2,1)S(1)}, u32[]{:S(2)}, u32[]{:S(2)}) collective-permute-start(bf16[4,16,2048]{2,1,0:T(8,128)(2,1)S(1)} %get-tuple-element.173), channel_id=1, source_target_pairs={{0,4},{1,5},{2,6},{3,7},{4,0},{5,1},{6,2},{7,3},{8,12},{9,13},{10,... | collective-permute-start | bytes 786440 | tf_op jit(solution)/shard_map/ppermute | solution.py:602
  165.3 11.2 %collective-permute-start.19 = (bf16[4,16,2048]{2,1,0:T(8,128)(2,1)S(1)}, bf16[4,16,2048]{2,1,0:T(8,128)(2,1)S(1)}, u32[]{:S(2)}, u32[]{:S(2)}) collective-permute-start(bf16[4,16,2048]{2,1,0:T(8,128)(2,1)S(1)} %get-tuple-element.174), channel_id=1, source_target_pairs={{0,2},{1,3},{2,0},{3,1},{4,6},{5,7},{6,4},{7,5},{8,10},{9,11},{10,... | collective-permute-start | bytes 786440 | tf_op jit(solution)/shard_map/ppermute | solution.py:602
  173.8 8.2 %collective-permute-start.22 = (bf16[16,16,1664]{2,1,0:T(8,128)(2,1)S(1)}, bf16[16,16,1664]{2,1,0:T(8,128)(2,1)S(1)}, u32[]{:S(2)}, u32[]{:S(2)}) collective-permute-start(bf16[16,16,1664]{2,1,0:T(8,128)(2,1)S(1)} %get-tuple-element.134), channel_id=1, source_target_pairs={{0,1},{1,0},{2,3},{3,2},{4,5},{5,4},{6,7},{7,6},{8,9},{9,8},{10,11... | collective-permute-start | bytes 2555912 | tf_op jit(solution)/shard_map/ppermute | solution.py:602
  182.3 9.1 %collective-permute-start.31 = (bf16[4,16,1664]{2,1,0:T(8,128)(2,1)S(1)}, bf16[4,16,1664]{2,1,0:T(8,128)(2,1)S(1)}, u32[]{:S(2)}, u32[]{:S(2)}) collective-permute-start(bf16[4,16,1664]{2,1,0:T(8,128)(2,1)S(1)} %get-tuple-element.175), channel_id=1, source_target_pairs={{0,6},{1,7},{2,4},{3,5},{4,2},{5,3},{6,0},{7,1},{8,14},{9,15},{10,... | collective-permute-start | bytes 638984 | tf_op jit(solution)/shard_map/ppermute | solution.py:602
  185.0 10.1 %collective-permute-start.30 = (bf16[4,16,1664]{2,1,0:T(8,128)(2,1)S(1)}, bf16[4,16,1664]{2,1,0:T(8,128)(2,1)S(1)}, u32[]{:S(2)}, u32[]{:S(2)}) collective-permute-start(bf16[4,16,1664]{2,1,0:T(8,128)(2,1)S(1)} %get-tuple-element.176), channel_id=1, source_target_pairs={{0,4},{1,5},{2,6},{3,7},{4,0},{5,1},{6,2},{7,3},{8,12},{9,13},{10,... | collective-permute-start | bytes 638984 | tf_op jit(solution)/shard_map/ppermute | solution.py:602
  186.2 11.3 %collective-permute-start.29 = (bf16[4,16,1664]{2,1,0:T(8,128)(2,1)S(1)}, bf16[4,16,1664]{2,1,0:T(8,128)(2,1)S(1)}, u32[]{:S(2)}, u32[]{:S(2)}) collective-permute-start(bf16[4,16,1664]{2,1,0:T(8,128)(2,1)S(1)} %get-tuple-element.177), channel_id=1, source_target_pairs={{0,2},{1,3},{2,0},{3,1},{4,6},{5,7},{6,4},{7,5},{8,10},{9,11},{10,... | collective-permute-start | bytes 638984 | tf_op jit(solution)/shard_map/ppermute | solution.py:602
  191.4 10.6 %collective-permute-start.23 = (bf16[16,2560]{1,0:T(8,128)(2,1)S(1)}, bf16[16,2560]{1,0:T(8,128)(2,1)S(1)}, u32[]{:S(2)}, u32[]{:S(2)}) collective-permute-start(bf16[16,2560]{1,0:T(8,128)(2,1)S(1)} %get-tuple-element.180), channel_id=1, source_target_pairs={{0,8},{1,9},{2,10},{3,11},{4,12},{5,13},{6,14},{7,15},{8,0},{9,1},... | collective-permute-start | bytes 245768 | tf_op jit(solution)/shard_map/ppermute | solution.py:602
  195.1 7.7 %collective-permute-start.28 = (bf16[16,2048]{1,0:T(8,128)(2,1)S(1)}, bf16[16,2048]{1,0:T(8,128)(2,1)S(1)}, u32[]{:S(2)}, u32[]{:S(2)}) collective-permute-start(bf16[16,2048]{1,0:T(8,128)(2,1)S(1)} %get-tuple-element.181), channel_id=1, source_target_pairs={{0,24},{1,25},{2,26},{3,27},{4,28},{5,29},{6,30},{7,31},{8,16},{9,... | collective-permute-start | bytes 196616 | tf_op jit(solution)/shard_map/ppermute | solution.py:602
  197.5 10.2 %collective-permute-start.27 = (bf16[16,2048]{1,0:T(8,128)(2,1)S(1)}, bf16[16,2048]{1,0:T(8,128)(2,1)S(1)}, u32[]{:S(2)}, u32[]{:S(2)}) collective-permute-start(bf16[16,2048]{1,0:T(8,128)(2,1)S(1)} %get-tuple-element.182), channel_id=1, source_target_pairs={{0,16},{1,17},{2,18},{3,19},{4,20},{5,21},{6,22},{7,23},{8,24},{9,... | collective-permute-start | bytes 196616 | tf_op jit(solution)/shard_map/ppermute | solution.py:602
  199.3 8.4 %collective-permute-start.26 = (bf16[16,2048]{1,0:T(8,128)(2,1)S(1)}, bf16[16,2048]{1,0:T(8,128)(2,1)S(1)}, u32[]{:S(2)}, u32[]{:S(2)}) collective-permute-start(bf16[16,2048]{1,0:T(8,128)(2,1)S(1)} %get-tuple-element.183), channel_id=1, source_target_pairs={{0,8},{1,9},{2,10},{3,11},{4,12},{5,13},{6,14},{7,15},{8,0},{9,1},... | collective-permute-start | bytes 196616 | tf_op jit(solution)/shard_map/ppermute | solution.py:602
  199.7 8.0 %collective-permute-start.34 = (bf16[16,1664]{1,0:T(8,128)(2,1)S(1)}, bf16[16,1664]{1,0:T(8,128)(2,1)S(1)}, u32[]{:S(2)}, u32[]{:S(2)}) collective-permute-start(bf16[16,1664]{1,0:T(8,128)(2,1)S(1)} %get-tuple-element.186), channel_id=1, source_target_pairs={{0,24},{1,25},{2,26},{3,27},{4,28},{5,29},{6,30},{7,31},{8,16},{9,... | collective-permute-start | bytes 159752 | tf_op jit(solution)/shard_map/ppermute | solution.py:602
  202.1 6.8 %collective-permute-start.33 = (bf16[16,1664]{1,0:T(8,128)(2,1)S(1)}, bf16[16,1664]{1,0:T(8,128)(2,1)S(1)}, u32[]{:S(2)}, u32[]{:S(2)}) collective-permute-start(bf16[16,1664]{1,0:T(8,128)(2,1)S(1)} %get-tuple-element.187), channel_id=1, source_target_pairs={{0,16},{1,17},{2,18},{3,19},{4,20},{5,21},{6,22},{7,23},{8,24},{9,... | collective-permute-start | bytes 159752 | tf_op jit(solution)/shard_map/ppermute | solution.py:602
  202.8 6.1 %collective-permute-start.32 = (bf16[16,1664]{1,0:T(8,128)(2,1)S(1)}, bf16[16,1664]{1,0:T(8,128)(2,1)S(1)}, u32[]{:S(2)}, u32[]{:S(2)}) collective-permute-start(bf16[16,1664]{1,0:T(8,128)(2,1)S(1)} %get-tuple-element.188), channel_id=1, source_target_pairs={{0,8},{1,9},{2,10},{3,11},{4,12},{5,13},{6,14},{7,15},{8,0},{9,1},... | collective-permute-start | bytes 159752 | tf_op jit(solution)/shard_map/ppermute | solution.py:602
  (47 other events, 383.5 us)
Sparse Core Ops, SparseCore 0:
  33.1 59.3 all-gather.1
where the time goes:
time: 237 us; the launch traced here: 233 us
  Pallas kernels  102 us (43%)
  starting transfers between devices  52.7 us (22%)
  waiting for transfers between devices  46.9 us (20%)
  between operations  15.8 us (7%)
  local copies, waits for them, and re-layouts  8.61 us (4%)
  other arithmetic  6.85 us (3%)
    pallas_call x16, Pallas kernels, call(): pl.pallas_call(kernel, grid=(1,) if split else (), out_shape=out_shape, i...  102 us
    ppermute x42, starting transfers between devices, swap(): return lax.ppermute(value, AXES, [(i, i ^ mask) for i in range(count)])  52.6 us
    ppermute x42, waiting for transfers between devices, swap(): return lax.ppermute(value, AXES, [(i, i ^ mask) for i in range(count)])  36.6 us
    all_gather x1, waiting for transfers between devices, local(): rest_full = lax.all_gather(rest_part, AXES, axis=0, tiled=True)  10.2 us
  transfers between devices with their start and end apart: 43, of which 22 were waited for; matrix products, arithmetic and copies ran while one was open for 2% of the time, Pallas kernels for 37%

commit v1 on v0

--- a/solution.py
+++ b/solution.py
@@ -1,3 +1,5 @@
+import functools
+
 import jax
 import jax.numpy as jnp
 from jax import lax
@@ -19,6 +21,8 @@
 WEIGHT_DECAY = 0.01
 ADAM_EPSILON = 1e-06
 NORM_EPSILON = 1e-05
+
+VMEM_GRANT = 28 * 2**20
 
 AXES = ("wide", "narrow")
 F32 = jnp.float32
@@ -86,7 +90,21 @@
         ref[exchange_slot(k), :, cols] = source[pl.ds(row, size), :].astype(BF16)
 
 
-def project_kernel(info_ref, x_ref, near_ref, far_ref, w_ref, norm_ref, q_ref, k_ref, v_ref):
+def pack_kernel(wa_ref, wf_ref, wn_ref, first_ref, second_ref, rest_ref):
+    width, hidden = wa_ref.shape[2], wf_ref.shape[2]
+    for slot in range(3):
+        first_ref[:, slot * width : (slot + 1) * width] = wa_ref[slot].astype(BF16)
+    rows = [wn_ref[...], jnp.zeros((128 - wn_ref.shape[0], wn_ref.shape[1]), F32)]
+    first_ref[:, 3 * width :] = jnp.transpose(jnp.concatenate(rows, axis=0)).astype(BF16)
+    for slot in range(4):
+        second_ref[:, slot * width : (slot + 1) * width] = wa_ref[slot + 3].astype(BF16)
+    rest_ref[:, 0:width] = wa_ref[7].astype(BF16)
+    for slot in range(2):
+        begin = width + slot * hidden
+        rest_ref[:, begin : begin + hidden] = wf_ref[slot].astype(BF16)
+
+
+def project_kernel(info_ref, x_ref, near_ref, far_ref, norm_ref, q_ref, k_ref, v_ref, w_ref):
     place_blocks(info_ref[3], near_ref, far_ref, w_ref)
     width = x_ref.shape[1]
     norm_ref[...] = jnp.transpose(w_ref[:, 3 * width :].astype(F32))[0:8, :]
@@ -177,7 +195,7 @@
 
 
 def self_forward_kernel(
-    info_ref, q_ref, k_ref, v_ref, o_ref, log_ref, bias_ref, score_ref, prob_ref
+    base, info_ref, q_ref, k_ref, v_ref, o_ref, log_ref, bias_ref, score_ref, prob_ref
 ):
     def run(cols, keys, count):
         def finish(index, mixed, logs):
@@ -185,17 +203,17 @@
             log_ref[index, :, cols] = logs
 
         forward_heads(
-            lambda index: q_ref[head_rows(index), cols],
-            lambda index: k_ref[head_rows(index), keys],
-            lambda index: v_ref[head_rows(index), keys],
-            finish, q_ref.shape[0] // HD, count, bias_ref, score_ref, prob_ref,
+            lambda index: q_ref[head_rows(base + index), cols],
+            lambda index: k_ref[head_rows(base + index), keys],
+            lambda index: v_ref[head_rows(base + index), keys],
+            finish, o_ref.shape[0] // HD, count, bias_ref, score_ref, prob_ref,
         )
 
     self_blocks(info_ref, q_ref.shape[1], bias_ref, run)
 
 
 def self_backward_kernel(
-    info_ref, q_ref, k_ref, v_ref, o_ref, log_ref, do_ref, dq_ref, dk_ref, dv_ref,
+    base, info_ref, q_ref, k_ref, v_ref, o_ref, log_ref, do_ref, dq_ref, dk_ref, dv_ref,
     sum_k, sum_v, bias_ref, score_ref, level_ref, prob_ref, delta_ref,
 ):
     sum_k[...] = jnp.zeros(sum_k.shape, F32)
@@ -208,13 +226,13 @@
             sum_v[head_rows(index), keys] += grad_value
 
         backward_heads(
-            lambda index: q_ref[head_rows(index), cols],
-            lambda index: k_ref[head_rows(index), keys],
-            lambda index: v_ref[head_rows(index), keys],
-            lambda index: do_ref[head_rows(index), cols],
-            lambda index: o_ref[head_rows(index), cols],
-            lambda index: log_ref[index, :, cols],
-            finish, q_ref.shape[0] // HD, count, bias_ref,
+            lambda index: q_ref[head_rows(base + index), cols],
+            lambda index: k_ref[head_rows(base + index), keys],
+            lambda index: v_ref[head_rows(base + index), keys],
+            lambda index: do_ref[head_rows(base + index), cols],
+            lambda index: o_ref[head_rows(base + index), cols],
+            lambda index: log_ref[base + index, :, cols],
+            finish, dq_ref.shape[0] // HD, count, bias_ref,
             score_ref, level_ref, prob_ref, delta_ref,
         )
 
@@ -233,7 +251,7 @@
         yield
         normed, scale = normalise(x_ref[rows, :].astype(F32) + branch)
         n_ref[rows, :] = normed
-        r_ref[rows, :] = scale
+        r_ref[:, rows] = jnp.transpose(jnp.broadcast_to(scale, (QB, 128)))[0:8]
         low = (normed * gain + shift).astype(BF16)
         yield
         query = dot(w_ref[:, width : 2 * width], low, 0, 1).astype(BF16)
@@ -288,7 +306,7 @@
 
 
 def cross_backward_kernel(
-    info_ref, q_ref, k_ref, v_ref, o_ref, log_ref, do_ref, dq_ref, dk_ref, dv_ref,
+    base, info_ref, q_ref, k_ref, v_ref, o_ref, log_ref, do_ref, dq_ref, dk_ref, dv_ref,
     sum_k, sum_v, score_ref, level_ref, prob_ref, delta_ref,
 ):
     sum_k[...] = jnp.zeros(sum_k.shape, F32)
@@ -303,13 +321,13 @@
 
         zero = jnp.zeros((), BF16)
         backward_heads(
-            lambda index: q_ref[head_rows(index), cols],
-            lambda index: k_ref[table, head_rows(index), :],
-            lambda index: v_ref[table, head_rows(index), :],
-            lambda index: jnp.where(here, do_ref[head_rows(index), cols], zero),
-            lambda index: o_ref[head_rows(index), cols],
-            lambda index: jnp.where(here, log_ref[index, :, cols], -MASKED_SCORE),
-            finish, q_ref.shape[0] // HD, IMG, None,
+            lambda index: q_ref[head_rows(base + index), cols],
+            lambda index: k_ref[table, head_rows(base + index), :],
+            lambda index: v_ref[table, head_rows(base + index), :],
+            lambda index: jnp.where(here, do_ref[head_rows(base + index), cols], zero),
+            lambda index: o_ref[head_rows(base + index), cols],
+            lambda index: jnp.where(here, log_ref[base + index, :, cols], -MASKED_SCORE),
+            finish, dq_ref.shape[0] // HD, IMG, None,
             score_ref, level_ref, prob_ref, delta_ref,
         )
 
@@ -319,12 +337,16 @@
 
 
 def feed_kernel(
-    info_ref, o_ref, n1_ref, cot_ref, co_ref, up_ref, down_ref, norm_ref,
+    info_ref, o_ref, n1_ref, cot_ref, w_ref, norm_ref,
     result_ref, dh_ref, do_ref, near_ref, far_ref, dnorm_ref,
     sum_up, sum_out, sum_norm, all_x2, all_active, all_du, all_dz, all_dac,
 ):
     valid = info_ref[2]
-    hidden_width = up_ref.shape[1]
+    width = cot_ref.shape[1]
+    hidden_width = (w_ref.shape[1] - width) // 2
+    co_ref = w_ref.at[:, 0:width]
+    up_ref = w_ref.at[:, width : width + hidden_width]
+    down_ref = w_ref.at[:, width + hidden_width :]
     sum_norm[...] = jnp.zeros(sum_norm.shape, F32)
     root = 0.7978845608028654
 
@@ -388,10 +410,12 @@
 
 
 def inner_kernel(
-    info_ref, dq0_ref, dq1_ref, dh2_ref, n1_ref, r1_ref, o_ref, w_ref, norm_ref,
-    image_ref, dk0_ref, dk1_ref, dv0_ref, dv1_ref,
-    dh_ref, do_ref, near_ref, far_ref, dnorm_ref, sum_image, sum_inner, sum_norm, all_low, all_da,
+    info_ref, dq0_ref, dq1_ref, dh2_ref, n1_ref, r1_ref, o_ref, wnear_ref, wfar_ref,
+    norm_ref, image_ref, dk0_ref, dk1_ref, dv0_ref, dv1_ref,
+    dh_ref, do_ref, near_ref, far_ref, dnorm_ref,
+    sum_image, sum_inner, sum_norm, all_low, all_da, w_ref,
 ):
+    place_blocks(info_ref[3], wnear_ref, wfar_ref, w_ref)
     sum_norm[...] = jnp.zeros(sum_norm.shape, F32)
     width = dh_ref.shape[1]
     gain, shift = norm_ref[0:1, :], norm_ref[3:4, :]
@@ -406,7 +430,7 @@
         dx1 = dh2_ref[rows, :] + back
         sum_norm[0:1, :] += column_sum(dx1 * normed)
         sum_norm[1:2, :] += column_sum(dx1)
-        dh1 = norm_back(dx1, gain, normed, r1_ref[rows, :])
+        dh1 = norm_back(dx1, gain, normed, jnp.transpose(jnp.broadcast_to(r1_ref[0:1, rows], (128, QB)))[:, 0:1])
         dh_ref[rows, :] = dh1
         da = dh1.astype(BF16)
         all_da[rows, :] = da
@@ -433,7 +457,10 @@
     dnorm_ref[...] = sum_norm[...]
 
 
-def image_grad_kernel(info_ref, dk0_ref, dk1_ref, dv0_ref, dv1_ref, w_ref, out_ref):
+def image_grad_kernel(
+    info_ref, dk0_ref, dk1_ref, dv0_ref, dv1_ref, near_ref, far_ref, out_ref, w_ref
+):
+    place_blocks(info_ref[3], near_ref, far_ref, w_ref)
     width = out_ref.shape[1]
     for table in range(TABLES):
         rows = slice(table * IMG, (table + 1) * IMG)
@@ -458,8 +485,10 @@
 
 
 def token_grad_kernel(
-    info_ref, dq0_ref, dq1_ref, dk0_ref, dk1_ref, dv0_ref, dv1_ref, w_ref, dh_ref, out_ref
+    info_ref, dq0_ref, dq1_ref, dk0_ref, dk1_ref, dv0_ref, dv1_ref, near_ref, far_ref, dh_ref,
+    out_ref, w_ref,
 ):
+    place_blocks(info_ref[3], near_ref, far_ref, w_ref)
     width = dh_ref.shape[1]
     refs = (dq0_ref, dq1_ref, dk0_ref, dk1_ref, dv0_ref, dv1_ref)
     for block in range(dh_ref.shape[0] // QB):
@@ -482,9 +511,9 @@
 
 
 def moments_kernel(per, *refs):
-    feed, inner, last = refs[0:per], refs[per : 2 * per], refs[2 * per : 3 * per]
-    wa, wf, wn, ma, va, mf, vf, mn, vn = refs[3 * per : 3 * per + 9]
-    ga, gf, gn, oma, ova, omf, ovf, omn, ovn, ua, uf, un, sums = refs[3 * per + 9 :]
+    both, last = refs[0:per], refs[per : 2 * per]
+    wa, wf, wn, ma, va, mf, vf, mn, vn = refs[2 * per : 2 * per + 9]
+    ga, gf, gn, oma, ova, omf, ovf, omn, ovn, ua, uf, un, sums = refs[2 * per + 9 :]
     width, hidden = wa.shape[2], wf.shape[2]
     lane = lax.broadcasted_iota(jnp.int32, (1, 128), 1)
     weights = jnp.zeros((1, 128), F32)
@@ -509,13 +538,13 @@
         updates = jnp.where(lane == slot, total_of(update), updates)
 
     for slot in range(8):
-        pieces, col = (last, slot) if slot < 3 else (inner, slot - 3)
+        pieces, col = (last, slot) if slot < 3 else (both, 2 * hidden // width + slot - 2)
         if slot == 7:
-            pieces, col = feed, 2 * hidden // width
+            pieces, col = both, 2 * hidden // width
         value = grad(pieces, col * width, width)
         tensor(slot, value, slot, wa, ma, va, (ga, oma, ova, ua), WEIGHT_DECAY)
     for slot in range(2):
-        value = grad(feed, slot * hidden, hidden)
+        value = grad(both, slot * hidden, hidden)
         tensor(8 + slot, value, slot, wf, mf, vf, (gf, omf, ovf, uf), WEIGHT_DECAY)
     norms = jnp.transpose(grad(last, 3 * width, 128))
     for slot in range(6):
@@ -550,26 +579,12 @@
     return jax.ShapeDtypeStruct(dims, kind)
 
 
-def call(kernel, out_shape, operands, name, micros, info=True, scratch=(), mib=32):
-    specs = []
-    operands = list(operands)
-    for position, operand in enumerate(operands):
-        if info and position == 0:
-            specs.append(SMEM)
-        elif isinstance(operand, tuple):
-            array, dims, index = operand
-            operands[position] = array
-            specs.append(
-                pl.BlockSpec(
-                    dims, lambda _, index=index: index, pipeline_mode=pl.Buffered(buffer_count=1)
-                )
-            )
-        else:
-            specs.append(VMEM)
-    split = any(spec.block_shape is not None for spec in specs)
+def call(kernel, out_shape, operands, name, micros, info=True, scratch=(), grant=VMEM_GRANT):
+    specs = [VMEM] * len(operands)
+    if info:
+        specs[0] = SMEM
     return pl.pallas_call(
         kernel,
-        grid=(1,) if split else (),
         out_shape=out_shape,
         in_specs=specs,
         out_specs=jax.tree.map(lambda _: VMEM, out_shape),
@@ -577,9 +592,9 @@
             pltpu.VMEM(dims[:-1], BF16) if dims[-1] is BF16 else pltpu.VMEM(dims, F32)
             for dims in scratch
         ],
-        compiler_params=pltpu.CompilerParams(vmem_limit_bytes=mib * 2**20),
+        compiler_params=pltpu.CompilerParams(vmem_limit_bytes=grant),
         cost_estimate=pl.CostEstimate(
-            flops=int(micros * 1.1e9), bytes_accessed=int(micros * 3.0e6), transcendentals=0
+            flops=int(micros * 0.02e9), bytes_accessed=0, transcendentals=0
         ),
         name=name,
     )(*operands)
@@ -617,9 +632,8 @@
     return jnp.stack([part] + [swap(part, mask) for mask in far_masks()])
 
 
-def gather_plane(part):
-    value = jnp.stack([part] + [swap(part, mask) for mask in PLANE_MASKS], axis=1)
-    return value.reshape((-1,) + part.shape[1:])
+def join_plane(parts):
+    return jnp.stack(parts, axis=1).reshape((-1,) + parts[0].shape[1:])
 
 
 def scatter_core(near, far):
@@ -670,10 +684,6 @@
         return near, far
     blocks = near.reshape(device_count(), -1, near.shape[1])[block_order()]
     return blocks[: device_count() // 2], blocks[device_count() // 2 :]
-
-
-def pack(stack):
-    return jnp.swapaxes(stack, 0, 1).reshape(stack.shape[1], -1)
 
 
 def local(
@@ -700,72 +710,84 @@
         [jnp.sum(segment < 1), jnp.sum(segment < 2), valid_len[0], device_index()]
     ).astype(jnp.int32)
 
-    attn_low = w_attn.astype(BF16)
-    norm_low = jnp.pad(norm_params.astype(BF16).T, ((0, 0), (0, 122)))
-    first_part = jnp.concatenate([pack(attn_low[0:3]), norm_low], axis=1)
+    first_part, second_part, rest_part = call(
+        pack_kernel,
+        [shaped(shard, 3 * width + 128), shaped(shard, 4 * width)]
+        + [shaped(shard, width + 2 * hidden_width)],
+        (w_attn, w_ffn, norm_params),
+        "pack",
+        1,
+        False,
+        (),
+        60 * 2**20,
+    )
+    rest_full = lax.all_gather(rest_part, AXES, axis=0, tiled=True)
     first_far = gather_far(first_part)
-    second_part = before(pack(attn_low[3:7]), first_far)
-    first_plane = gather_plane(first_far)
-    second_far = gather_far(second_part)
+    second_part = before(second_part, first_far)
+    first_sent = [swap(first_far, mask) for mask in PLANE_MASKS]
+    second_sent = [swap(second_part, mask) for mask in far_masks()]
+    first_sent, second_sent, info = lax.optimization_barrier((first_sent, second_sent, info))
+    second_far = jnp.stack([second_part] + second_sent)
+    first_plane = join_plane([first_far] + before(first_sent, second_far))
     first_core = swap(first_plane, 1)
-    rest_part = before(
-        jnp.concatenate([pack(attn_low[7:8]), pack(w_ffn.astype(BF16))], axis=1), first_plane
-    )
-    rest_full = lax.all_gather(rest_part, AXES, axis=0, tiled=True)
-    second_plane = gather_plane(second_far)
+    second_sent = [swap(second_far, mask) for mask in PLANE_MASKS]
 
     wide_shape = shaped(width, tags)
     half_shape = shaped(width // 2, tags)
     log_shape = shaped(HEADS, 1, tags, kind=F32)
     f32_rows = shaped(tags, width, kind=F32)
-    w_first, norms, q, k, v = call(
+    first_blocks = whole_blocks(first_plane, first_core)
+    norms, q, k, v = call(
         project_kernel,
-        [shaped(width, 3 * width + 128), shaped(8, width, kind=F32)] + [wide_shape] * 3,
-        (info, tokens, *whole_blocks(first_plane, first_core)),
+        [shaped(8, width, kind=F32)] + [wide_shape] * 3,
+        (info, tokens, *first_blocks),
         "project",
         3,
-    )
+        True,
+        [(width, 3 * width + 128, BF16)],
+    )
+
     o, log_self = call(
-        self_forward_kernel,
+        functools.partial(self_forward_kernel, 0),
         [wide_shape, log_shape],
         (before(info, second_far), q, k, v),
         "self_forward",
-        10,
+        8,
         True,
         [(3 * QB, QB), (2, 3 * QB, QB), (2, 3 * QB, QB, BF16)],
-        24,
-    )
+    )
+    second_plane = join_plane([second_far] + before(second_sent, o))
     second_core = swap(second_plane, 1)
     image_shape = shaped(TABLES, width, IMG)
     image_half = shaped(TABLES, width // 2, IMG)
+    second_blocks = whole_blocks(second_plane, second_core)
     w_second, kc, vc = call(
         image_kernel,
         [shaped(width, 4 * width)] + [image_shape] * 2,
-        (info, image, *whole_blocks(second_plane, second_core)),
+        (info, image, *second_blocks),
         "image_project",
         6,
+        True,
+        (),
     )
     n1, r1, qc = call(
         mid_kernel,
-        [f32_rows, shaped(tags, 1, kind=F32), wide_shape],
+        [f32_rows, shaped(8, tags, kind=F32), wide_shape],
         (tokens, o, w_second, norms),
         "mid",
-        5,
+        3,
         False,
+        (),
     )
     oc, log_cross = call(
         cross_forward_kernel,
         [wide_shape, log_shape],
         (info, qc, kc, vc),
         "cross_forward",
-        18,
+        16,
         True,
         [(2, IMG, QB), (2, IMG, QB, BF16)],
-        24,
-    )
-    co = rest_full[:, 0:width]
-    up = rest_full[:, width : width + hidden_width]
-    down = rest_full[:, width + hidden_width :]
+    )
     feed_cols = 2 * hidden_width + width
     result, dh2, doc, feed_near, feed_far, norm_feed = call(
         feed_kernel,
@@ -776,47 +798,38 @@
             *spread_shapes(shard, feed_cols),
             shaped(8, width, kind=F32),
         ],
-        (info, oc, n1, cotangent, co, up, down, norms),
+        (info, oc, n1, cotangent, rest_full, norms),
         "feed",
         15,
         True,
         [(width, hidden_width), (width, width), (8, width), (tags, width, BF16)]
         + [(tags, hidden_width, BF16)] * 2
         + [(tags, width, BF16)] * 2,
-        40,
-    )
-
-    def half(array, index):
-        axis = 1 if array.shape[0] == TABLES else 0
-        dims = tuple(size // 2 if i == axis else size for i, size in enumerate(array.shape))
-        return array, dims, tuple(index if i == axis else 0 for i in range(len(dims)))
+    )
 
     def cross_backward(index, *deps):
-        parts = [half(array, index) for array in (qc, kc, vc, oc, log_cross, doc)]
         return call(
-            cross_backward_kernel,
+            functools.partial(cross_backward_kernel, index * HEADS // 2),
             [half_shape, image_half, image_half],
-            [before(info, *deps)] + parts,
+            [before(info, *deps), qc, kc, vc, oc, log_cross, doc],
             "cross_backward",
-            16,
+            14,
             True,
             [(TABLES, width // 2, IMG)] * 2 + [(2, IMG, QB)] * 2 + [(2, IMG, QB, BF16)] * 2,
         )
 
     def self_backward(index, *deps):
-        parts = [half(array, index) for array in (q, k, v, o, log_self, do)]
         return call(
-            self_backward_kernel,
+            functools.partial(self_backward_kernel, index * HEADS // 2),
             [half_shape] * 3,
-            [before(info, *deps)] + parts,
+            [before(info, *deps), q, k, v, o, log_self, do],
             "self_backward",
-            8,
+            7,
             True,
             [(width // 2, tags)] * 2
             + [(3 * QB, QB)]
             + [(2, 3 * QB, QB)] * 2
             + [(2, 3 * QB, QB, BF16)] * 2,
-            24,
         )
 
     feed_near, feed_far = split_blocks(feed_near, feed_far)
@@ -834,16 +847,16 @@
             *spread_shapes(shard, 4 * width),
             shaped(8, width, kind=F32),
         ],
-        (before(info, send_feed), dqc0, dqc1, dh2, n1, r1, o, w_second, norms)
+        (before(info, send_feed), dqc0, dqc1, dh2, n1, r1, o, *second_blocks, norms)
         + (image, dkc0, dkc1, dvc0, dvc1),
         "inner",
         10,
         True,
-        [(width, 2 * width), (width, width), (8, width)] + [(tags, width, BF16)] * 2,
-        36,
+        [(width, 2 * width), (width, width), (8, width)]
+        + [(tags, width, BF16)] * 2
+        + [(width, 4 * width, BF16)],
     )
     inner_near, inner_far = split_blocks(inner_near, inner_far)
-    pieces_feed = scatter_far_end(own_feed, send_feed)
     dq0, dk0, dv0 = self_backward(0)
     inner_near = before(inner_near, dq0)
     own_inner, send_inner = scatter_plane(scatter_core(inner_near, inner_far))
@@ -861,31 +874,36 @@
     )
     last_near, last_far = split_blocks(last_near, last_far)
     own_inner, send_inner = scatter_plane_end(before(own_inner, dq1), send_inner)
+    send_both = [jnp.concatenate(pair, axis=1) for pair in zip(send_feed, send_inner)]
+    pieces_both = scatter_far_end(jnp.concatenate([own_feed, own_inner], axis=1), send_both)
+    own_last, send_last = scatter_plane(scatter_core(before(last_near, send_both), last_far))
     image_grad = call(
         image_grad_kernel,
         shaped(image.shape[0], width, kind=F32),
-        (before(info, last_far, send_inner), dkc0, dkc1, dvc0, dvc1, w_second),
+        (before(info, send_last), dkc0, dkc1, dvc0, dvc1, *second_blocks),
         "image_grad",
-        7,
-    )
-    own_last, send_last = scatter_plane(scatter_core(before(last_near, image_grad), last_far))
+        6,
+        True,
+        [(width, 4 * width, BF16)],
+    )
     token_grad = call(
         token_grad_kernel,
         f32_rows,
-        (before(info, send_last),) + grads + (w_first, dh1),
+        (before(info, image_grad),) + grads + (*first_blocks, dh1),
         "token_grad",
-        5,
-    )
-    pieces_inner = scatter_far_end(own_inner, send_inner)
-    own_last, send_last = scatter_plane_end(before(own_last, token_grad), send_last)
+        4,
+        True,
+        [(width, 3 * width + 128, BF16)],
+    )
+    own_last, send_last = scatter_plane_end(before(own_last, token_grad, pieces_both), send_last)
     pieces_last = scatter_far_end(own_last, send_last)
 
     weights = (w_attn, w_ffn, norm_params)
     moments = (momentum_attn, variance_attn, momentum_ffn, variance_ffn)
     moments = moments + (momentum_norm, variance_norm)
     like = [shaped(*array.shape, kind=F32) for array in weights + moments + weights]
-    pieces = [*pieces_feed, *pieces_inner, *pieces_last]
-    per_chunk = len(pieces) // 3
+    pieces = [*pieces_both, *pieces_last]
+    per_chunk = len(pieces) // 2
     outs = call(
         lambda *refs: moments_kernel(per_chunk, *refs),
         like + [shaped(8, 128, kind=F32)],

time: 237 us -> 222 us (0.937)
  waiting for transfers between devices: 46.9 us -> 28.9 us
    all_gather x1, waiting for transfers between devices: 10.2 us -> 0.01 us  [local(): rest_full = lax.all_gather(rest_part, AXES, axis=0, tiled=True)]
    ppermute x42 -> x39, waiting for transfers between devices: 36.6 us -> 28.9 us  [swap(): return lax.ppermute(value, AXES, [(i, i ^ mask) for i in range(count)])]
    unnamed x75 -> x82, local copies, waits for them, and re-layouts: 4.53 us -> 9.22 us
    slice x2 -> x0, local copies, waits for them, and re-layouts: 2.94 us -> none  [the longest x1 1.86 us: local(): down = rest_full[:, width + hidden_width:]]
    pallas_call x16 -> x17, Pallas kernels: 102 us -> 104 us  [call(): pl.pallas_call(kernel, out_shape=out_shape, in_specs=specs, out_specs=jax...]
    ppermute x42 -> x39, starting transfers between devices: 52.6 us -> 52.4 us  [swap(): return lax.ppermute(value, AXES, [(i, i ^ mask) for i in range(count)])]
  transfers between devices with their start and end apart: 43 -> 40, of which waited for: 22 -> 19; matrix products, arithmetic and copies ran while one was open for 2% -> 3% of each run, Pallas kernels for 37% -> 36%
where the time goes in v1:
time: 222 us; the launch traced here: 218 us
  Pallas kernels  104 us (47%)
  starting transfers between devices  52.4 us (24%)
  waiting for transfers between devices  28.9 us (13%)
  between operations  15.7 us (7%)
  local copies, waits for them, and re-layouts  10.4 us (5%)
  other arithmetic  6.13 us (3%)
    pallas_call x17, Pallas kernels, call(): pl.pallas_call(kernel, out_shape=out_shape, in_specs=specs, out_specs=jax...  104 us
    ppermute x39, starting transfers between devices, swap(): return lax.ppermute(value, AXES, [(i, i ^ mask) for i in range(count)])  52.4 us
    ppermute x39, waiting for transfers between devices, swap(): return lax.ppermute(value, AXES, [(i, i ^ mask) for i in range(count)])  28.9 us
    unnamed x82, local copies, waits for them, and re-layouts  9.22 us
  transfers between devices with their start and end apart: 40, of which 19 were waited for; matrix products, arithmetic and copies ran while one was open for 3% of the time, Pallas kernels for 36%

profile of v1, /device:TPU:0, one launch (start us, length us, event | category | flops | bytes accessed | tf_op | source)
XLA Modules:
  0.0 217.9 jit_solution(14944324058751705048)
XLA Ops:
  9.0 5.1 %collective-permute-start.2 = (bf16[16,1664]{1,0:T(8,128)(2,1)}, bf16[16,1664]{1,0:T(8,128)(2,1)S(1)}, u32[]{:S(2)}, u32[]{:S(2)}) collective-permute-start(bf16[16,1664]{1,0:T(8,128)(2,1)} %get-tuple-element.102), channel_id=1, source_target_pairs={{0,24},{1,25},{2,26},{3,27},{4,28},{5,29},{6,30},{7,31},{8,16},{9,... | collective-permute-start | bytes 159752 | tf_op jit(solution)/shard_map/ppermute | solution.py:617
  16.6 2.7 %collective-permute-done.1 = bf16[16,1664]{1,0:T(8,128)(2,1)S(1)} collective-permute-done((bf16[16,1664]{1,0:T(8,128)(2,1)}, bf16[16,1664]{1,0:T(8,128)(2,1)S(1)}, u32[]{:S(2)}, u32[]{:S(2)}) %collective-permute-start.1) | collective-permute-done | bytes 53280 | tf_op jit(solution)/shard_map/ppermute | solution.py:617
  20.2 2.5 %collective-permute-start.5 = (bf16[4,16,1664]{2,1,0:T(8,128)(2,1)S(1)}, bf16[4,16,1664]{2,1,0:T(8,128)(2,1)S(1)}, u32[]{:S(2)}, u32[]{:S(2)}) collective-permute-start(bf16[4,16,1664]{2,1,0:T(8,128)(2,1)S(1)} %get-tuple-element.216), channel_id=1, source_target_pairs={{0,6},{1,7},{2,4},{3,5},{4,2},{5,3},{6,0},{7,1},{8,14},{9,15},{10,... | collective-permute-start | bytes 638984 | tf_op jit(solution)/shard_map/ppermute | solution.py:617
  23.8 2.4 %collective-permute-start.8 = (bf16[16,2048]{1,0:T(8,128)(2,1)}, bf16[16,2048]{1,0:T(8,128)(2,1)S(1)}, u32[]{:S(2)}, u32[]{:S(2)}) collective-permute-start(bf16[16,2048]{1,0:T(8,128)(2,1)} %get-tuple-element.104), channel_id=1, source_target_pairs={{0,24},{1,25},{2,26},{3,27},{4,28},{5,29},{6,30},{7,31},{8,16},{9,... | collective-permute-start | bytes 196616 | tf_op jit(solution)/shard_map/ppermute | solution.py:617
  27.5 2.6 %collective-permute-done.8 = bf16[16,2048]{1,0:T(8,128)(2,1)S(1)} collective-permute-done((bf16[16,2048]{1,0:T(8,128)(2,1)}, bf16[16,2048]{1,0:T(8,128)(2,1)S(1)}, u32[]{:S(2)}, u32[]{:S(2)}) %collective-permute-start.8) | collective-permute-done | bytes 65568 | tf_op jit(solution)/shard_map/ppermute | solution.py:617
  39.6 2.6 %project.1 = (f32[8,512]{1,0:T(8,128)S(1)}, bf16[512,1024]{1,0:T(8,128)(2,1)S(1)}, bf16[512,1024]{1,0:T(8,128)(2,1)S(1)}, bf16[512,1024]{1,0:T(8,128)(2,1)S(1)}) custom-call(s32[4]{0:T(128)S(1)} %pad_add_fusion.info_ref, bf16[1024,512]{1,0:T(8,128)(2,1)S(1)} %copy-done.15, bf16[16,16,1664]{2,1,0:T(8,128)(2,1)S(1)} %bitcast.83, ...), custom_call_target="tpu_custom_call" | custom-call | flops 60000000 | tf_op jit(solution)/shard_map/project/pallas_call | solution.py:586
  42.2 7.2 %self_forward.1 = (bf16[512,1024]{1,0:T(8,128)(2,1)S(1)}, f32[8,1,1024]{2,1,0:T(1,128)S(1)}) custom-call(s32[4]{0:T(128)S(1)} %pad_add_fusion.info_ref, bf16[512,1024]{1,0:T(8,128)(2,1)S(1)} %get-tuple-element.116.q_ref, bf16[512,1024]{1,0:T(8,128)(2,1)S(1)} %get-tuple-element.117.k_ref, bf16[512,1024]{1,0:T(8,128)(2,1)S(1)} %get-tuple-element.118.v_ref), custom_call_target="tpu_custom_call" | custom-call | flops 160000000 | tf_op jit(solution)/shard_map/self_forward/pallas_call | solution.py:586
  49.4 4.3 %collective-permute-done.12 = bf16[4,16,2048]{2,1,0:T(8,128)(2,1)S(1)} collective-permute-done((bf16[4,16,2048]{2,1,0:T(8,128)(2,1)S(1)}, bf16[4,16,2048]{2,1,0:T(8,128)(2,1)S(1)}, u32[]{:S(2)}, u32[]{:S(2)}) %collective-permute-start.12) | collective-permute-done | bytes 262176 | tf_op jit(solution)/shard_map/ppermute | solution.py:617
  54.1 2.6 %collective-permute-done.13.far_ref.wfar_ref = bf16[16,16,2048]{2,1,0:T(8,128)(2,1)S(1)} collective-permute-done((bf16[16,16,2048]{2,1,0:T(8,128)(2,1)S(1)}, bf16[16,16,2048]{2,1,0:T(8,128)(2,1)S(1)}, u32[]{:S(2)}, u32[]{:S(2)}) %collective-permute-start.13) | collective-permute-done | bytes 1048608 | tf_op jit(solution)/shard_map/ppermute | solution.py:617
  56.7 4.2 %image_project.1 = (bf16[512,2048]{1,0:T(8,128)(2,1)S(1)}, bf16[3,512,784]{2,1,0:T(8,128)(2,1)S(1)}, bf16[3,512,784]{2,1,0:T(8,128)(2,1)S(1)}) custom-call(s32[4]{0:T(128)S(1)} %pad_add_fusion.info_ref, bf16[2352,512]{1,0:T(8,128)(2,1)S(1)} %copy-done.6, bf16[16,16,2048]{2,1,0:T(8,128)(2,1)S(1)} %bitcast.79, ...), custom_call_target="tpu_custom_call" | custom-call | flops 120000000 | tf_op jit(solution)/shard_map/image_project/pallas_call | solution.py:586
  60.9 2.0 mid.1
  64.3 13.3 %cross_forward.1 = (bf16[512,1024]{1,0:T(8,128)(2,1)S(1)}, f32[8,1,1024]{2,1,0:T(1,128)S(1)}) custom-call(s32[4]{0:T(128)S(1)} %pad_add_fusion.info_ref, bf16[512,1024]{1,0:T(8,128)(2,1)S(1)} %get-tuple-element.125.q_ref, bf16[3,512,784]{2,1,0:T(8,128)(2,1)S(1)} %get-tuple-element.126.k_ref, bf16[3,512,784]{2,1,0:T(8,128)(2,1)S(1)} %get-tuple-element.127.v_ref), custom_call_target="tpu_custom_call" | custom-call | flops 320000000 | tf_op jit(solution)/shard_map/cross_forward/pallas_call | solution.py:586
  85.4 14.0 %feed.1 = (bf16[1024,512]{1,0:T(8,128)(2,1)}, f32[1024,512]{1,0:T(8,128)S(1)}, bf16[512,1024]{1,0:T(8,128)(2,1)S(1)}, bf16[16,16,2560]{2,1,0:T(8,128)(2,1)S(1)},...) custom-call(s32[4]{0:T(128)S(1)} %pad_add_fusion.info_ref, bf16[512,1024]{1,0:T(8,128)(2,1)S(1)} %copy-done.13, ...), custom_call_target="tpu_custom_call" | custom-call | flops 300000000 | tf_op jit(solution)/shard_map/feed/pallas_call | solution.py:586
  99.4 2.6 %collective-permute-start.14 = (bf16[16,16,2560]{2,1,0:T(8,128)(2,1)S(1)}, bf16[16,16,2560]{2,1,0:T(8,128)(2,1)S(1)}, u32[]{:S(2)}, u32[]{:S(2)}) collective-permute-start(bf16[16,16,2560]{2,1,0:T(8,128)(2,1)S(1)} %get-tuple-element.138), channel_id=1, source_target_pairs={{0,1},{1,0},{2,3},{3,2},{4,5},{5,4},{6,7},{7,6},{8,9},{9,8},{10,11... | collective-permute-start | bytes 3932168 | tf_op jit(solution)/shard_map/ppermute | solution.py:617
  102.0 12.6 %cross_backward.2 = (bf16[256,1024]{1,0:T(8,128)(2,1)S(1)}, bf16[3,256,784]{2,1,0:T(8,128)(2,1)S(1)}, bf16[3,256,784]{2,1,0:T(8,128)(2,1)S(1)}) custom-call(s32[4]{0:T(128)S(1)} %pad_add_fusion.info_ref, bf16[512,1024]{1,0:T(8,128)(2,1)S(1)} %copy-done.11, bf16[3,512,784]{2,1,0:T(8,128)(2,1)S(1)} %get-tuple-element.126.k_ref, ...), custom_call_target="tpu_custom_call" | custom-call | flops 280000000 | tf_op jit(solution)/shard_map/cross_backward/pallas_call | solution.py:586
  116.7 2.0 collective-permute-start.16
  118.8 12.4 %cross_backward.3 = (bf16[256,1024]{1,0:T(8,128)(2,1)S(1)}, bf16[3,256,784]{2,1,0:T(8,128)(2,1)S(1)}, bf16[3,256,784]{2,1,0:T(8,128)(2,1)S(1)}) custom-call(s32[4]{0:T(128)S(1)} %pad_add_fusion.info_ref, bf16[512,1024]{1,0:T(8,128)(2,1)S(1)} %copy-done.11, bf16[3,512,784]{2,1,0:T(8,128)(2,1)S(1)} %get-tuple-element.126.k_ref, ...), custom_call_target="tpu_custom_call" | custom-call | flops 280000000 | tf_op jit(solution)/shard_map/cross_backward/pallas_call | solution.py:586
  133.6 7.8 %inner.1 = (f32[1024,512]{1,0:T(8,128)S(1)}, bf16[512,1024]{1,0:T(8,128)(2,1)S(1)}, bf16[16,16,2048]{2,1,0:T(8,128)(2,1)S(1)}, bf16[16,16,2048]{2,1,0:T(8,128)(2,1)S(1)}, f32[8,512]{1,0:T(8,128)S(1)}) custom-call(s32[4]{0:T(128)S(1)} %pad_add_fusion.info_ref, bf16[256,1024]{1,0:T(8,128)(2,1)S(1)} %get-tuple-element.136.dq0_ref, ...), custom_call_target="tpu_custom_call" | custom-call | flops 200000000 | tf_op jit(solution)/shard_map/inner/pallas_call | solution.py:586
  141.4 2.8 %collective-permute-start.18 = (bf16[16,16,2048]{2,1,0:T(8,128)(2,1)S(1)}, bf16[16,16,2048]{2,1,0:T(8,128)(2,1)S(1)}, u32[]{:S(2)}, u32[]{:S(2)}) collective-permute-start(bf16[16,16,2048]{2,1,0:T(8,128)(2,1)S(1)} %get-tuple-element.153), channel_id=1, source_target_pairs={{0,1},{1,0},{2,3},{3,2},{4,5},{5,4},{6,7},{7,6},{8,9},{9,8},{10,11... | collective-permute-start | bytes 3145736 | tf_op jit(solution)/shard_map/ppermute | solution.py:617
  144.2 6.1 %self_backward.2 = (bf16[256,1024]{1,0:T(8,128)(2,1)S(1)}, bf16[256,1024]{1,0:T(8,128)(2,1)S(1)}, bf16[256,1024]{1,0:T(8,128)(2,1)S(1)}) custom-call(s32[4]{0:T(128)S(1)} %pad_add_fusion.info_ref, bf16[512,1024]{1,0:T(8,128)(2,1)S(1)} %copy-done.18, bf16[512,1024]{1,0:T(8,128)(2,1)S(1)} %copy-done.20, bf16[512,1024]{1,0:T(8,128)(2,1)S(1)} %copy-done.22, ...), custom_call_target="tpu_custom_call" | custom-call | flops 140000000 | tf_op jit(solution)/shard_map/self_backward/pallas_call | solution.py:586
  152.3 2.1 collective-permute-start.19
  154.4 5.9 %self_backward.3 = (bf16[256,1024]{1,0:T(8,128)(2,1)S(1)}, bf16[256,1024]{1,0:T(8,128)(2,1)S(1)}, bf16[256,1024]{1,0:T(8,128)(2,1)S(1)}) custom-call(s32[4]{0:T(128)S(1)} %pad_add_fusion.info_ref, bf16[512,1024]{1,0:T(8,128)(2,1)S(1)} %copy-done.18, bf16[512,1024]{1,0:T(8,128)(2,1)S(1)} %copy-done.20, bf16[512,1024]{1,0:T(8,128)(2,1)S(1)} %copy-done.22, ...), custom_call_target="tpu_custom_call" | custom-call | flops 140000000 | tf_op jit(solution)/shard_map/self_backward/pallas_call | solution.py:586
  160.4 2.5 %project_weight.1 = (bf16[16,16,1664]{2,1,0:T(8,128)(2,1)S(1)}, bf16[16,16,1664]{2,1,0:T(8,128)(2,1)S(1)}) custom-call(s32[4]{0:T(128)S(1)} %pad_add_fusion.info_ref, bf16[1024,512]{1,0:T(8,128)(2,1)S(1)} %copy-done.16, bf16[256,1024]{1,0:T(8,128)(2,1)S(1)} %get-tuple-element.150.dq0_ref, bf16[256,1024]{1,0:T(8,128)(2,1)S(1)} %get-tuple-element.155.dq1_ref, ...), custom_call_target="tpu_custom_call" | custom-call | flops 60000000 | tf_op jit(solution)/shard_map/project_weight/pallas_call | solution.py:586
  162.9 2.3 %collective-permute-start.22 = (bf16[16,16,1664]{2,1,0:T(8,128)(2,1)S(1)}, bf16[16,16,1664]{2,1,0:T(8,128)(2,1)S(1)}, u32[]{:S(2)}, u32[]{:S(2)}) collective-permute-start(bf16[16,16,1664]{2,1,0:T(8,128)(2,1)S(1)} %get-tuple-element.165), channel_id=1, source_target_pairs={{0,1},{1,0},{2,3},{3,2},{4,5},{5,4},{6,7},{7,6},{8,9},{9,8},{10,11... | collective-permute-start | bytes 2555912 | tf_op jit(solution)/shard_map/ppermute | solution.py:617
  166.8 2.2 %collective-permute-start.23 = (bf16[16,4608]{1,0:T(8,128)(2,1)S(1)}, bf16[16,4608]{1,0:T(8,128)(2,1)S(1)}, u32[]{:S(2)}, u32[]{:S(2)}) collective-permute-start(bf16[16,4608]{1,0:T(8,128)(2,1)S(1)} %pad_maximum_fusion.5), channel_id=1, source_target_pairs={{0,8},{1,9},{2,10},{3,11},{4,12},{5,13},{6,14},{7,15},{8,0},{9,1},... | collective-permute-start | bytes 442376 | tf_op jit(solution)/shard_map/ppermute | solution.py:617
  171.8 2.7 %collective-permute-start.28 = (bf16[4,16,1664]{2,1,0:T(8,128)(2,1)S(1)}, bf16[4,16,1664]{2,1,0:T(8,128)(2,1)S(1)}, u32[]{:S(2)}, u32[]{:S(2)}) collective-permute-start(bf16[4,16,1664]{2,1,0:T(8,128)(2,1)S(1)} %get-tuple-element.201), channel_id=1, source_target_pairs={{0,6},{1,7},{2,4},{3,5},{4,2},{5,3},{6,0},{7,1},{8,14},{9,15},{10,... | collective-permute-start | bytes 638984 | tf_op jit(solution)/shard_map/ppermute | solution.py:617
  176.0 5.6 %image_grad.1 = f32[2352,512]{1,0:T(8,128)} custom-call(s32[4]{0:T(128)S(1)} %pad_add_fusion.info_ref, bf16[3,256,784]{2,1,0:T(8,128)(2,1)S(1)} %get-tuple-element.145.dk0_ref, bf16[3,256,784]{2,1,0:T(8,128)(2,1)S(1)} %get-tuple-element.146.dk1_ref, bf16[3,256,784]{2,1,0:T(8,128)(2,1)S(1)} %get-tuple-element.147.dv0_ref, ...), custom_call_target="tpu_custom_call" | custom-call | flops 120000000 | tf_op jit(solution)/shard_map/image_grad/pallas_call | solution.py:586
  181.6 3.9 %token_grad.1 = f32[1024,512]{1,0:T(8,128)} custom-call(s32[4]{0:T(128)S(1)} %pad_add_fusion.info_ref, bf16[256,1024]{1,0:T(8,128)(2,1)S(1)} %get-tuple-element.150.dq0_ref, bf16[256,1024]{1,0:T(8,128)(2,1)S(1)} %get-tuple-element.155.dq1_ref, bf16[256,1024]{1,0:T(8,128)(2,1)S(1)} %get-tuple-element.156.dk0_ref, ...), custom_call_target="tpu_custom_call" | custom-call | flops 80000000 | tf_op jit(solution)/shard_map/token_grad/pallas_call | solution.py:586
  185.8 3.5 %collective-permute-start.31 = (bf16[16,1664]{1,0:T(8,128)(2,1)S(1)}, bf16[16,1664]{1,0:T(8,128)(2,1)S(1)}, u32[]{:S(2)}, u32[]{:S(2)}) collective-permute-start(bf16[16,1664]{1,0:T(8,128)(2,1)S(1)} %get-tuple-element.212), channel_id=1, source_target_pairs={{0,24},{1,25},{2,26},{3,27},{4,28},{5,29},{6,30},{7,31},{8,16},{9,... | collective-permute-start | bytes 159752 | tf_op jit(solution)/shard_map/ppermute | solution.py:617
  191.8 2.5 %collective-permute-done.30.refs_6_ = bf16[16,1664]{1,0:T(8,128)(2,1)S(1)} collective-permute-done((bf16[16,1664]{1,0:T(8,128)(2,1)S(1)}, bf16[16,1664]{1,0:T(8,128)(2,1)S(1)}, u32[]{:S(2)}, u32[]{:S(2)}) %collective-permute-start.30) | collective-permute-done | bytes 53280 | tf_op jit(solution)/shard_map/ppermute | solution.py:617
  197.1 2.6 %collective-permute-start.35 = (f32[8,128]{1,0:T(8,128)S(1)}, f32[8,128]{1,0:T(8,128)S(1)}, u32[]{:S(2)}, u32[]{:S(2)}) collective-permute-start(f32[8,128]{1,0:T(8,128)S(1)} %add.64), channel_id=1, source_target_pairs={{0,6},{1,7},{2,4},{3,5},{4,2},{5,3},{6,0},{7,1},{8,14},{9,15},{10,... | collective-permute-start | bytes 12296 | tf_op jit(solution)/shard_map/ppermute | solution.py:617
  205.5 2.3 %collective-permute-start.36 = (f32[8,128]{1,0:T(8,128)S(1)}, f32[8,128]{1,0:T(8,128)S(1)}, u32[]{:S(2)}, u32[]{:S(2)}) collective-permute-start(f32[8,128]{1,0:T(8,128)S(1)} %add_add_fusion.refs_0_), channel_id=1, source_target_pairs={{0,8},{1,9},{2,10},{3,11},{4,12},{5,13},{6,14},{7,15},{8,0},{9,1},... | collective-permute-start | bytes 12296 | tf_op jit(solution)/shard_map/ppermute | solution.py:617
  (181 shorter events, 52.2 us)
Async XLA Ops:
  7.2 72.4 %all-gather.2.cloned.1.call-start = ((), (), s32[]{:S(2)}) async-start(), calls=%async_computation | async-start | bytes 2703360 | tf_op jit(solution)/shard_map/all_gather | solution.py:724
  9.0 7.7 %collective-permute-start.2 = (bf16[16,1664]{1,0:T(8,128)(2,1)}, bf16[16,1664]{1,0:T(8,128)(2,1)S(1)}, u32[]{:S(2)}, u32[]{:S(2)}) collective-permute-start(bf16[16,1664]{1,0:T(8,128)(2,1)} %get-tuple-element.102), channel_id=1, source_target_pairs={{0,24},{1,25},{2,26},{3,27},{4,28},{5,29},{6,30},{7,31},{8,16},{9,... | collective-permute-start | bytes 159752 | tf_op jit(solution)/shard_map/ppermute | solution.py:617
  14.1 5.2 %collective-permute-start.1 = (bf16[16,1664]{1,0:T(8,128)(2,1)}, bf16[16,1664]{1,0:T(8,128)(2,1)S(1)}, u32[]{:S(2)}, u32[]{:S(2)}) collective-permute-start(bf16[16,1664]{1,0:T(8,128)(2,1)} %get-tuple-element.102), channel_id=1, source_target_pairs={{0,16},{1,17},{2,18},{3,19},{4,20},{5,21},{6,22},{7,23},{8,24},{9,... | collective-permute-start | bytes 159752 | tf_op jit(solution)/shard_map/ppermute | solution.py:617
  14.1 5.2 %collective-permute-start = (bf16[16,1664]{1,0:T(8,128)(2,1)}, bf16[16,1664]{1,0:T(8,128)(2,1)S(1)}, u32[]{:S(2)}, u32[]{:S(2)}) collective-permute-start(bf16[16,1664]{1,0:T(8,128)(2,1)} %get-tuple-element.102), channel_id=1, source_target_pairs={{0,8},{1,9},{2,10},{3,11},{4,12},{5,13},{6,14},{7,15},{8,0},{9,1},... | collective-permute-start | bytes 159752 | tf_op jit(solution)/shard_map/ppermute | solution.py:617
  20.2 14.5 %collective-permute-start.5 = (bf16[4,16,1664]{2,1,0:T(8,128)(2,1)S(1)}, bf16[4,16,1664]{2,1,0:T(8,128)(2,1)S(1)}, u32[]{:S(2)}, u32[]{:S(2)}) collective-permute-start(bf16[4,16,1664]{2,1,0:T(8,128)(2,1)S(1)} %get-tuple-element.216), channel_id=1, source_target_pairs={{0,6},{1,7},{2,4},{3,5},{4,2},{5,3},{6,0},{7,1},{8,14},{9,15},{10,... | collective-permute-start | bytes 638984 | tf_op jit(solution)/shard_map/ppermute | solution.py:617
  22.7 12.0 %collective-permute-start.4 = (bf16[4,16,1664]{2,1,0:T(8,128)(2,1)S(1)}, bf16[4,16,1664]{2,1,0:T(8,128)(2,1)S(1)}, u32[]{:S(2)}, u32[]{:S(2)}) collective-permute-start(bf16[4,16,1664]{2,1,0:T(8,128)(2,1)S(1)} %get-tuple-element.216), channel_id=1, source_target_pairs={{0,4},{1,5},{2,6},{3,7},{4,0},{5,1},{6,2},{7,3},{8,12},{9,13},{10,... | collective-permute-start | bytes 638984 | tf_op jit(solution)/shard_map/ppermute | solution.py:617
  23.2 11.5 %collective-permute-start.3 = (bf16[4,16,1664]{2,1,0:T(8,128)(2,1)S(1)}, bf16[4,16,1664]{2,1,0:T(8,128)(2,1)S(1)}, u32[]{:S(2)}, u32[]{:S(2)}) collective-permute-start(bf16[4,16,1664]{2,1,0:T(8,128)(2,1)S(1)} %get-tuple-element.216), channel_id=1, source_target_pairs={{0,2},{1,3},{2,0},{3,1},{4,6},{5,7},{6,4},{7,5},{8,10},{9,11},{10,... | collective-permute-start | bytes 638984 | tf_op jit(solution)/shard_map/ppermute | solution.py:617
  23.8 6.3 %collective-permute-start.8 = (bf16[16,2048]{1,0:T(8,128)(2,1)}, bf16[16,2048]{1,0:T(8,128)(2,1)S(1)}, u32[]{:S(2)}, u32[]{:S(2)}) collective-permute-start(bf16[16,2048]{1,0:T(8,128)(2,1)} %get-tuple-element.104), channel_id=1, source_target_pairs={{0,24},{1,25},{2,26},{3,27},{4,28},{5,29},{6,30},{7,31},{8,16},{9,... | collective-permute-start | bytes 196616 | tf_op jit(solution)/shard_map/ppermute | solution.py:617
  27.5 6.1 %collective-permute-start.7 = (bf16[16,2048]{1,0:T(8,128)(2,1)}, bf16[16,2048]{1,0:T(8,128)(2,1)S(1)}, u32[]{:S(2)}, u32[]{:S(2)}) collective-permute-start(bf16[16,2048]{1,0:T(8,128)(2,1)} %get-tuple-element.104), channel_id=1, source_target_pairs={{0,16},{1,17},{2,18},{3,19},{4,20},{5,21},{6,22},{7,23},{8,24},{9,... | collective-permute-start | bytes 196616 | tf_op jit(solution)/shard_map/ppermute | solution.py:617
  30.1 4.6 %collective-permute-start.6 = (bf16[16,2048]{1,0:T(8,128)(2,1)}, bf16[16,2048]{1,0:T(8,128)(2,1)S(1)}, u32[]{:S(2)}, u32[]{:S(2)}) collective-permute-start(bf16[16,2048]{1,0:T(8,128)(2,1)} %get-tuple-element.104), channel_id=1, source_target_pairs={{0,8},{1,9},{2,10},{3,11},{4,12},{5,13},{6,14},{7,15},{8,0},{9,1},... | collective-permute-start | bytes 196616 | tf_op jit(solution)/shard_map/ppermute | solution.py:617
  36.0 13.4 %collective-permute-start.11 = (bf16[4,16,2048]{2,1,0:T(8,128)(2,1)S(1)}, bf16[4,16,2048]{2,1,0:T(8,128)(2,1)S(1)}, u32[]{:S(2)}, u32[]{:S(2)}) collective-permute-start(bf16[4,16,2048]{2,1,0:T(8,128)(2,1)S(1)} %get-tuple-element.211), channel_id=1, source_target_pairs={{0,4},{1,5},{2,6},{3,7},{4,0},{5,1},{6,2},{7,3},{8,12},{9,13},{10,... | collective-permute-start | bytes 786440 | tf_op jit(solution)/shard_map/ppermute | solution.py:617
  37.7 11.7 %collective-permute-start.10 = (bf16[4,16,2048]{2,1,0:T(8,128)(2,1)S(1)}, bf16[4,16,2048]{2,1,0:T(8,128)(2,1)S(1)}, u32[]{:S(2)}, u32[]{:S(2)}) collective-permute-start(bf16[4,16,2048]{2,1,0:T(8,128)(2,1)S(1)} %get-tuple-element.211), channel_id=1, source_target_pairs={{0,2},{1,3},{2,0},{3,1},{4,6},{5,7},{6,4},{7,5},{8,10},{9,11},{10,... | collective-permute-start | bytes 786440 | tf_op jit(solution)/shard_map/ppermute | solution.py:617
  39.2 14.5 %collective-permute-start.12 = (bf16[4,16,2048]{2,1,0:T(8,128)(2,1)S(1)}, bf16[4,16,2048]{2,1,0:T(8,128)(2,1)S(1)}, u32[]{:S(2)}, u32[]{:S(2)}) collective-permute-start(bf16[4,16,2048]{2,1,0:T(8,128)(2,1)S(1)} %get-tuple-element.211), channel_id=1, source_target_pairs={{0,6},{1,7},{2,4},{3,5},{4,2},{5,3},{6,0},{7,1},{8,14},{9,15},{10,... | collective-permute-start | bytes 786440 | tf_op jit(solution)/shard_map/ppermute | solution.py:617
  99.4 15.3 %collective-permute-start.14 = (bf16[16,16,2560]{2,1,0:T(8,128)(2,1)S(1)}, bf16[16,16,2560]{2,1,0:T(8,128)(2,1)S(1)}, u32[]{:S(2)}, u32[]{:S(2)}) collective-permute-start(bf16[16,16,2560]{2,1,0:T(8,128)(2,1)S(1)} %get-tuple-element.138), channel_id=1, source_target_pairs={{0,1},{1,0},{2,3},{3,2},{4,5},{5,4},{6,7},{7,6},{8,9},{9,8},{10,11... | collective-permute-start | bytes 3932168 | tf_op jit(solution)/shard_map/ppermute | solution.py:617
  115.2 16.6 %collective-permute-start.15 = (bf16[4,16,2560]{2,1,0:T(8,128)(2,1)S(1)}, bf16[4,16,2560]{2,1,0:T(8,128)(2,1)S(1)}, u32[]{:S(2)}, u32[]{:S(2)}) collective-permute-start(bf16[4,16,2560]{2,1,0:T(8,128)(2,1)S(1)} %get-tuple-element.195), channel_id=1, source_target_pairs={{0,2},{1,3},{2,0},{3,1},{4,6},{5,7},{6,4},{7,5},{8,10},{9,11},{10,... | collective-permute-start | bytes 983048 | tf_op jit(solution)/shard_map/ppermute | solution.py:617
  115.2 16.5 %collective-permute-start.17 = (bf16[4,16,2560]{2,1,0:T(8,128)(2,1)S(1)}, bf16[4,16,2560]{2,1,0:T(8,128)(2,1)S(1)}, u32[]{:S(2)}, u32[]{:S(2)}) collective-permute-start(bf16[4,16,2560]{2,1,0:T(8,128)(2,1)S(1)} %get-tuple-element.196), channel_id=1, source_target_pairs={{0,6},{1,7},{2,4},{3,5},{4,2},{5,3},{6,0},{7,1},{8,14},{9,15},{10,... | collective-permute-start | bytes 983048 | tf_op jit(solution)/shard_map/ppermute | solution.py:617
  116.7 16.6 %collective-permute-start.16 = (bf16[4,16,2560]{2,1,0:T(8,128)(2,1)S(1)}, bf16[4,16,2560]{2,1,0:T(8,128)(2,1)S(1)}, u32[]{:S(2)}, u32[]{:S(2)}) collective-permute-start(bf16[4,16,2560]{2,1,0:T(8,128)(2,1)S(1)} %get-tuple-element.197), channel_id=1, source_target_pairs={{0,4},{1,5},{2,6},{3,7},{4,0},{5,1},{6,2},{7,3},{8,12},{9,13},{10,... | collective-permute-start | bytes 983048 | tf_op jit(solution)/shard_map/ppermute | solution.py:617
  141.4 9.0 %collective-permute-start.18 = (bf16[16,16,2048]{2,1,0:T(8,128)(2,1)S(1)}, bf16[16,16,2048]{2,1,0:T(8,128)(2,1)S(1)}, u32[]{:S(2)}, u32[]{:S(2)}) collective-permute-start(bf16[16,16,2048]{2,1,0:T(8,128)(2,1)S(1)} %get-tuple-element.153), channel_id=1, source_target_pairs={{0,1},{1,0},{2,3},{3,2},{4,5},{5,4},{6,7},{7,6},{8,9},{9,8},{10,11... | collective-permute-start | bytes 3145736 | tf_op jit(solution)/shard_map/ppermute | solution.py:617
  150.9 14.3 %collective-permute-start.21 = (bf16[4,16,2048]{2,1,0:T(8,128)(2,1)S(1)}, bf16[4,16,2048]{2,1,0:T(8,128)(2,1)S(1)}, u32[]{:S(2)}, u32[]{:S(2)}) collective-permute-start(bf16[4,16,2048]{2,1,0:T(8,128)(2,1)S(1)} %get-tuple-element.198), channel_id=1, source_target_pairs={{0,6},{1,7},{2,4},{3,5},{4,2},{5,3},{6,0},{7,1},{8,14},{9,15},{10,... | collective-permute-start | bytes 786440 | tf_op jit(solution)/shard_map/ppermute | solution.py:617
  152.3 12.9 %collective-permute-start.20 = (bf16[4,16,2048]{2,1,0:T(8,128)(2,1)S(1)}, bf16[4,16,2048]{2,1,0:T(8,128)(2,1)S(1)}, u32[]{:S(2)}, u32[]{:S(2)}) collective-permute-start(bf16[4,16,2048]{2,1,0:T(8,128)(2,1)S(1)} %get-tuple-element.199), channel_id=1, source_target_pairs={{0,4},{1,5},{2,6},{3,7},{4,0},{5,1},{6,2},{7,3},{8,12},{9,13},{10,... | collective-permute-start | bytes 786440 | tf_op jit(solution)/shard_map/ppermute | solution.py:617
  152.3 14.3 %collective-permute-start.19 = (bf16[4,16,2048]{2,1,0:T(8,128)(2,1)S(1)}, bf16[4,16,2048]{2,1,0:T(8,128)(2,1)S(1)}, u32[]{:S(2)}, u32[]{:S(2)}) collective-permute-start(bf16[4,16,2048]{2,1,0:T(8,128)(2,1)S(1)} %get-tuple-element.200), channel_id=1, source_target_pairs={{0,2},{1,3},{2,0},{3,1},{4,6},{5,7},{6,4},{7,5},{8,10},{9,11},{10,... | collective-permute-start | bytes 786440 | tf_op jit(solution)/shard_map/ppermute | solution.py:617
  162.9 8.6 %collective-permute-start.22 = (bf16[16,16,1664]{2,1,0:T(8,128)(2,1)S(1)}, bf16[16,16,1664]{2,1,0:T(8,128)(2,1)S(1)}, u32[]{:S(2)}, u32[]{:S(2)}) collective-permute-start(bf16[16,16,1664]{2,1,0:T(8,128)(2,1)S(1)} %get-tuple-element.165), channel_id=1, source_target_pairs={{0,1},{1,0},{2,3},{3,2},{4,5},{5,4},{6,7},{7,6},{8,9},{9,8},{10,11... | collective-permute-start | bytes 2555912 | tf_op jit(solution)/shard_map/ppermute | solution.py:617
  166.8 8.2 %collective-permute-start.23 = (bf16[16,4608]{1,0:T(8,128)(2,1)S(1)}, bf16[16,4608]{1,0:T(8,128)(2,1)S(1)}, u32[]{:S(2)}, u32[]{:S(2)}) collective-permute-start(bf16[16,4608]{1,0:T(8,128)(2,1)S(1)} %pad_maximum_fusion.5), channel_id=1, source_target_pairs={{0,8},{1,9},{2,10},{3,11},{4,12},{5,13},{6,14},{7,15},{8,0},{9,1},... | collective-permute-start | bytes 442376 | tf_op jit(solution)/shard_map/ppermute | solution.py:617
  169.1 16.5 %collective-permute-start.24 = (bf16[16,4608]{1,0:T(8,128)(2,1)S(1)}, bf16[16,4608]{1,0:T(8,128)(2,1)S(1)}, u32[]{:S(2)}, u32[]{:S(2)}) collective-permute-start(bf16[16,4608]{1,0:T(8,128)(2,1)S(1)} %pad_maximum_fusion.6), channel_id=1, source_target_pairs={{0,16},{1,17},{2,18},{3,19},{4,20},{5,21},{6,22},{7,23},{8,24},{9,... | collective-permute-start | bytes 442376 | tf_op jit(solution)/shard_map/ppermute | solution.py:617
  170.7 14.9 %collective-permute-start.25 = (bf16[16,4608]{1,0:T(8,128)(2,1)S(1)}, bf16[16,4608]{1,0:T(8,128)(2,1)S(1)}, u32[]{:S(2)}, u32[]{:S(2)}) collective-permute-start(bf16[16,4608]{1,0:T(8,128)(2,1)S(1)} %pad_maximum_fusion.7), channel_id=1, source_target_pairs={{0,24},{1,25},{2,26},{3,27},{4,28},{5,29},{6,30},{7,31},{8,16},{9,... | collective-permute-start | bytes 442376 | tf_op jit(solution)/shard_map/ppermute | solution.py:617
  171.8 13.8 %collective-permute-start.28 = (bf16[4,16,1664]{2,1,0:T(8,128)(2,1)S(1)}, bf16[4,16,1664]{2,1,0:T(8,128)(2,1)S(1)}, u32[]{:S(2)}, u32[]{:S(2)}) collective-permute-start(bf16[4,16,1664]{2,1,0:T(8,128)(2,1)S(1)} %get-tuple-element.201), channel_id=1, source_target_pairs={{0,6},{1,7},{2,4},{3,5},{4,2},{5,3},{6,0},{7,1},{8,14},{9,15},{10,... | collective-permute-start | bytes 638984 | tf_op jit(solution)/shard_map/ppermute | solution.py:617
  174.5 11.1 %collective-permute-start.27 = (bf16[4,16,1664]{2,1,0:T(8,128)(2,1)S(1)}, bf16[4,16,1664]{2,1,0:T(8,128)(2,1)S(1)}, u32[]{:S(2)}, u32[]{:S(2)}) collective-permute-start(bf16[4,16,1664]{2,1,0:T(8,128)(2,1)S(1)} %get-tuple-element.202), channel_id=1, source_target_pairs={{0,4},{1,5},{2,6},{3,7},{4,0},{5,1},{6,2},{7,3},{8,12},{9,13},{10,... | collective-permute-start | bytes 638984 | tf_op jit(solution)/shard_map/ppermute | solution.py:617
  175.0 10.6 %collective-permute-start.26 = (bf16[4,16,1664]{2,1,0:T(8,128)(2,1)S(1)}, bf16[4,16,1664]{2,1,0:T(8,128)(2,1)S(1)}, u32[]{:S(2)}, u32[]{:S(2)}) collective-permute-start(bf16[4,16,1664]{2,1,0:T(8,128)(2,1)S(1)} %get-tuple-element.203), channel_id=1, source_target_pairs={{0,2},{1,3},{2,0},{3,1},{4,6},{5,7},{6,4},{7,5},{8,10},{9,11},{10,... | collective-permute-start | bytes 638984 | tf_op jit(solution)/shard_map/ppermute | solution.py:617
  185.8 6.0 %collective-permute-start.31 = (bf16[16,1664]{1,0:T(8,128)(2,1)S(1)}, bf16[16,1664]{1,0:T(8,128)(2,1)S(1)}, u32[]{:S(2)}, u32[]{:S(2)}) collective-permute-start(bf16[16,1664]{1,0:T(8,128)(2,1)S(1)} %get-tuple-element.212), channel_id=1, source_target_pairs={{0,24},{1,25},{2,26},{3,27},{4,28},{5,29},{6,30},{7,31},{8,16},{9,... | collective-permute-start | bytes 159752 | tf_op jit(solution)/shard_map/ppermute | solution.py:617
  189.3 5.0 %collective-permute-start.30 = (bf16[16,1664]{1,0:T(8,128)(2,1)S(1)}, bf16[16,1664]{1,0:T(8,128)(2,1)S(1)}, u32[]{:S(2)}, u32[]{:S(2)}) collective-permute-start(bf16[16,1664]{1,0:T(8,128)(2,1)S(1)} %get-tuple-element.213), channel_id=1, source_target_pairs={{0,16},{1,17},{2,18},{3,19},{4,20},{5,21},{6,22},{7,23},{8,24},{9,... | collective-permute-start | bytes 159752 | tf_op jit(solution)/shard_map/ppermute | solution.py:617
  189.3 5.0 %collective-permute-start.29 = (bf16[16,1664]{1,0:T(8,128)(2,1)S(1)}, bf16[16,1664]{1,0:T(8,128)(2,1)S(1)}, u32[]{:S(2)}, u32[]{:S(2)}) collective-permute-start(bf16[16,1664]{1,0:T(8,128)(2,1)S(1)} %get-tuple-element.214), channel_id=1, source_target_pairs={{0,8},{1,9},{2,10},{3,11},{4,12},{5,13},{6,14},{7,15},{8,0},{9,1},... | collective-permute-start | bytes 159752 | tf_op jit(solution)/shard_map/ppermute | solution.py:617
  203.4 5.4 %collective-permute-start.38 = (f32[8,128]{1,0:T(8,128)S(1)}, f32[8,128]{1,0:T(8,128)S(1)}, u32[]{:S(2)}, u32[]{:S(2)}) collective-permute-start(f32[8,128]{1,0:T(8,128)S(1)} %add_add_fusion.refs_0_), channel_id=1, source_target_pairs={{0,24},{1,25},{2,26},{3,27},{4,28},{5,29},{6,30},{7,31},{8,16},{9,... | collective-permute-start | bytes 12296 | tf_op jit(solution)/shard_map/ppermute | solution.py:617
  (49 other events, 345.2 us)
Sparse Core Ops, SparseCore 0:
  11.5 62.8 all-gather.1

commit v2 on v1

--- a/solution.py
+++ b/solution.py
@@ -22,7 +22,7 @@
 ADAM_EPSILON = 1e-06
 NORM_EPSILON = 1e-05
 
-VMEM_GRANT = 28 * 2**20
+VMEM_GRANT = 32 * 2**20
 
 AXES = ("wide", "narrow")
 F32 = jnp.float32
@@ -90,17 +90,16 @@
         ref[exchange_slot(k), :, cols] = source[pl.ds(row, size), :].astype(BF16)
 
 
-def pack_kernel(wa_ref, wf_ref, wn_ref, first_ref, second_ref, rest_ref):
+def pack_kernel(wa_ref, wf_ref, wn_ref, first_ref, rest_ref):
     width, hidden = wa_ref.shape[2], wf_ref.shape[2]
     for slot in range(3):
         first_ref[:, slot * width : (slot + 1) * width] = wa_ref[slot].astype(BF16)
     rows = [wn_ref[...], jnp.zeros((128 - wn_ref.shape[0], wn_ref.shape[1]), F32)]
     first_ref[:, 3 * width :] = jnp.transpose(jnp.concatenate(rows, axis=0)).astype(BF16)
-    for slot in range(4):
-        second_ref[:, slot * width : (slot + 1) * width] = wa_ref[slot + 3].astype(BF16)
-    rest_ref[:, 0:width] = wa_ref[7].astype(BF16)
+    for slot in range(5):
+        rest_ref[:, slot * width : (slot + 1) * width] = wa_ref[slot + 3].astype(BF16)
     for slot in range(2):
-        begin = width + slot * hidden
+        begin = 5 * width + slot * hidden
         rest_ref[:, begin : begin + hidden] = wf_ref[slot].astype(BF16)
 
 
@@ -270,33 +269,54 @@
 
 
 def cross_blocks(info_ref, rows, run):
-    def pair(index, carry):
-        block = index // TABLES
-        table = index % TABLES
+    def job(index, carry):
+        table = index // 3
+        step = index % 3
         second, third = info_ref[0], info_ref[1]
         begin = jnp.where(table == 0, 0, jnp.where(table == 1, second, third))
         end = jnp.where(table == 0, second, jnp.where(table == 1, third, rows))
-        start = block * QB
-
-        @pl.when(jnp.logical_and(begin < start + QB, end > start))
+        first = begin // QB
+        last = (end - 1) // QB
+        merged = (last > first) & (end % QB > 0) & (end % QB <= begin % QB)
+        count = last - first + 1 - merged.astype(jnp.int32)
+
+        @pl.when(step < count)
         def _():
-            place = start + lax.broadcasted_iota(jnp.int32, (1, QB), 1)
-            run(pl.ds(pl.multiple_of(start, QB), QB), table, (place >= begin) & (place < end))
+            block = first + step
+            other = jnp.where(merged & (step == 0), last, block)
+            lane = lax.broadcasted_iota(jnp.int32, (1, QB), 1)
+            place = block * QB + lane
+            here = (place >= begin) & (place < end)
+            place = other * QB + lane
+            there = (place < end) & (place >= jnp.where(other == block, rows, begin))
+            run(
+                pl.ds(pl.multiple_of(block * QB, QB), QB),
+                pl.ds(pl.multiple_of(other * QB, QB), QB),
+                table, here, there,
+            )
 
         return carry
 
-    lax.fori_loop(0, rows // QB * TABLES, pair, 0)
+    lax.fori_loop(0, TABLES * 3, job, 0)
+
+
+def store_both(ref, index, value, cols, others, here, there):
+    ref[index + (cols,)] = jnp.where(here, value, ref[index + (cols,)])
+    ref[index + (others,)] = jnp.where(there, value, ref[index + (others,)])
 
 
 def cross_forward_kernel(info_ref, q_ref, k_ref, v_ref, o_ref, log_ref, score_ref, prob_ref):
-    def run(cols, table, here):
+    def run(cols, others, table, here, there):
         def finish(index, mixed, logs):
+            store_both(o_ref, (head_rows(index),), mixed, cols, others, here, there)
+            store_both(log_ref, (index, slice(None)), logs, cols, others, here, there)
+
+        def query(index):
             rows = head_rows(index)
-            o_ref[rows, cols] = jnp.where(here, mixed, o_ref[rows, cols])
-            log_ref[index, :, cols] = jnp.where(here, logs, log_ref[index, :, cols])
+            return jnp.where(there, q_ref[rows, others], q_ref[rows, cols])
 
         forward_heads(
-            lambda index: q_ref[head_rows(index), cols],
+            query,
             lambda index: k_ref[table, head_rows(index), :],
             lambda index: v_ref[table, head_rows(index), :],
             finish, q_ref.shape[0] // HD, IMG, None, score_ref, prob_ref,
@@ -312,22 +332,33 @@
     sum_k[...] = jnp.zeros(sum_k.shape, F32)
     sum_v[...] = jnp.zeros(sum_v.shape, F32)
 
-    def run(cols, table, here):
+    def run(cols, others, table, here, there):
         def finish(index, grad_query, grad_key, grad_value):
             rows = head_rows(index)
-            dq_ref[rows, cols] = jnp.where(here, grad_query, dq_ref[rows, cols])
+            store_both(dq_ref, (rows,), grad_query, cols, others, here, there)
             sum_k[table, rows, :] += grad_key
             sum_v[table, rows, :] += grad_value
 
+        def both(ref):
+            def read(index):
+                rows = head_rows(base + index)
+                return jnp.where(there, ref[rows, others], ref[rows, cols])
+
+            return read
+
+        def logs(index):
+            far = jnp.where(there, log_ref[base + index, :, others], -MASKED_SCORE)
+            return jnp.where(here, log_ref[base + index, :, cols], far)
+
+        seen = here | there
+        grads = both(do_ref)
         zero = jnp.zeros((), BF16)
         backward_heads(
-            lambda index: q_ref[head_rows(base + index), cols],
+            both(q_ref),
             lambda index: k_ref[table, head_rows(base + index), :],
             lambda index: v_ref[table, head_rows(base + index), :],
-            lambda index: jnp.where(here, do_ref[head_rows(base + index), cols], zero),
-            lambda index: o_ref[head_rows(base + index), cols],
-            lambda index: jnp.where(here, log_ref[base + index, :, cols], -MASKED_SCORE),
-            finish, dq_ref.shape[0] // HD, IMG, None,
+            lambda index: jnp.where(seen, grads(index), zero),
+            both(o_ref), logs, finish, dq_ref.shape[0] // HD, IMG, None,
             score_ref, level_ref, prob_ref, delta_ref,
         )
 
@@ -337,10 +368,11 @@
 
 
 def feed_kernel(
-    info_ref, o_ref, n1_ref, cot_ref, w_ref, norm_ref,
+    info_ref, o_ref, n1_ref, cot_ref, wnear_ref, wfar_ref, norm_ref,
     result_ref, dh_ref, do_ref, near_ref, far_ref, dnorm_ref,
-    sum_up, sum_out, sum_norm, all_x2, all_active, all_du, all_dz, all_dac,
+    sum_up, sum_out, sum_norm, all_x2, all_active, all_du, all_dz, all_dac, w_ref,
 ):
+    place_blocks(info_ref[3], wnear_ref, wfar_ref, w_ref)
     valid = info_ref[2]
     width = cot_ref.shape[1]
     hidden_width = (w_ref.shape[1] - width) // 2
@@ -710,10 +742,9 @@
         [jnp.sum(segment < 1), jnp.sum(segment < 2), valid_len[0], device_index()]
     ).astype(jnp.int32)
 
-    first_part, second_part, rest_part = call(
+    first_part, second_part = call(
         pack_kernel,
-        [shaped(shard, 3 * width + 128), shaped(shard, 4 * width)]
-        + [shaped(shard, width + 2 * hidden_width)],
+        [shaped(shard, 3 * width + 128), shaped(shard, 5 * width + 2 * hidden_width)],
         (w_attn, w_ffn, norm_params),
         "pack",
         1,
@@ -721,13 +752,14 @@
         (),
         60 * 2**20,
     )
-    rest_full = lax.all_gather(rest_part, AXES, axis=0, tiled=True)
     first_far = gather_far(first_part)
     second_part = before(second_part, first_far)
     first_sent = [swap(first_far, mask) for mask in PLANE_MASKS]
     second_sent = [swap(second_part, mask) for mask in far_masks()]
     first_sent, second_sent, info = lax.optimization_barrier((first_sent, second_sent, info))
     second_far = jnp.stack([second_part] + second_sent)
+    third_far = second_far[:, :, 4 * width :]
+    second_far = second_far[:, :, 0 : 4 * width]
     first_plane = join_plane([first_far] + before(first_sent, second_far))
     first_core = swap(first_plane, 1)
     second_sent = [swap(second_far, mask) for mask in PLANE_MASKS]
@@ -756,6 +788,7 @@
         True,
         [(3 * QB, QB), (2, 3 * QB, QB), (2, 3 * QB, QB, BF16)],
     )
+    third_sent = [swap(third_far, mask) for mask in PLANE_MASKS]
     second_plane = join_plane([second_far] + before(second_sent, o))
     second_core = swap(second_plane, 1)
     image_shape = shaped(TABLES, width, IMG)
@@ -764,7 +797,7 @@
     w_second, kc, vc = call(
         image_kernel,
         [shaped(width, 4 * width)] + [image_shape] * 2,
-        (info, image, *second_blocks),
+        (before(info, third_far), image, *second_blocks),
         "image_project",
         6,
         True,
@@ -788,6 +821,8 @@
         True,
         [(2, IMG, QB), (2, IMG, QB, BF16)],
     )
+    third_plane = join_plane([third_far] + before(third_sent, oc))
+    third_core = swap(third_plane, 1)
     feed_cols = 2 * hidden_width + width
     result, dh2, doc, feed_near, feed_far, norm_feed = call(
         feed_kernel,
@@ -798,13 +833,14 @@
             *spread_shapes(shard, feed_cols),
             shaped(8, width, kind=F32),
         ],
-        (info, oc, n1, cotangent, rest_full, norms),
+        (info, oc, n1, cotangent, *whole_blocks(third_plane, third_core), norms),
         "feed",
         15,
         True,
         [(width, hidden_width), (width, width), (8, width), (tags, width, BF16)]
         + [(tags, hidden_width, BF16)] * 2
-        + [(tags, width, BF16)] * 2,
+        + [(tags, width, BF16)] * 2
+        + [(width, feed_cols, BF16)],
     )
 
     def cross_backward(index, *deps):

time: 222 us -> 201 us (0.905)
  between operations: 15.7 us -> 2.27 us
  local copies, waits for them, and re-layouts: 10.4 us -> 3.87 us
  waiting for transfers between devices: 28.9 us -> 25.2 us
  starting transfers between devices: 52.4 us -> 54.9 us
    unnamed x82 -> x50, local copies, waits for them, and re-layouts: 9.22 us -> 1.44 us
    ppermute x39 -> x43, waiting for transfers between devices: 28.9 us -> 25.2 us  [swap(): return lax.ppermute(value, AXES, [(i, i ^ mask) for i in range(count)])]
    ppermute x39 -> x43, starting transfers between devices: 52.4 us -> 54.9 us  [swap(): return lax.ppermute(value, AXES, [(i, i ^ mask) for i in range(count)])]
  transfers between devices with their start and end apart: 40 -> 43, of which waited for: 19 -> 20; matrix products, arithmetic and copies ran while one was open for 3% -> 2% of each run, Pallas kernels for 36% -> 40%
where the time goes in v2:
time: 201 us; the launch traced here: 197 us
  Pallas kernels  105 us (52%)
  starting transfers between devices  54.9 us (27%)
  waiting for transfers between devices  25.2 us (13%)
  other arithmetic  6.24 us (3%)
  local copies, waits for them, and re-layouts  3.87 us (2%)
  between operations  2.27 us (1%)
    pallas_call x17, Pallas kernels, call(): pl.pallas_call(kernel, out_shape=out_shape, in_specs=specs, out_specs=jax...  105 us
    ppermute x43, starting transfers between devices, swap(): return lax.ppermute(value, AXES, [(i, i ^ mask) for i in range(count)])  54.9 us
    ppermute x43, waiting for transfers between devices, swap(): return lax.ppermute(value, AXES, [(i, i ^ mask) for i in range(count)])  25.2 us
  transfers between devices with their start and end apart: 43, of which 20 were waited for; matrix products, arithmetic and copies ran while one was open for 2% of the time, Pallas kernels for 40%

profile of v2, /device:TPU:0, one launch (start us, length us, event | category | flops | bytes accessed | tf_op | source)
XLA Modules:
  0.0 197.1 jit_solution(4635468487703955497)
XLA Ops:
  0.7 1.7 pack.1
  2.4 5.0 %collective-permute-start.2 = (bf16[16,1664]{1,0:T(8,128)(2,1)}, bf16[16,1664]{1,0:T(8,128)(2,1)S(1)}, u32[]{:S(2)}, u32[]{:S(2)}) collective-permute-start(bf16[16,1664]{1,0:T(8,128)(2,1)} %get-tuple-element.105), channel_id=1, source_target_pairs={{0,24},{1,25},{2,26},{3,27},{4,28},{5,29},{6,30},{7,31},{8,16},{9,... | collective-permute-start | bytes 159752 | tf_op jit(solution)/shard_map/ppermute | solution.py:649
  8.0 2.0 %collective-permute-done.2 = bf16[16,1664]{1,0:T(8,128)(2,1)S(1)} collective-permute-done((bf16[16,1664]{1,0:T(8,128)(2,1)}, bf16[16,1664]{1,0:T(8,128)(2,1)S(1)}, u32[]{:S(2)}, u32[]{:S(2)}) %collective-permute-start.2) | collective-permute-done | bytes 53280 | tf_op jit(solution)/shard_map/ppermute | solution.py:649
  10.0 2.7 %collective-permute-done.1 = bf16[16,1664]{1,0:T(8,128)(2,1)S(1)} collective-permute-done((bf16[16,1664]{1,0:T(8,128)(2,1)}, bf16[16,1664]{1,0:T(8,128)(2,1)S(1)}, u32[]{:S(2)}, u32[]{:S(2)}) %collective-permute-start.1) | collective-permute-done | bytes 53280 | tf_op jit(solution)/shard_map/ppermute | solution.py:649
  13.5 2.4 %collective-permute-start.8 = (bf16[16,4608]{1,0:T(8,128)(2,1)}, bf16[16,4608]{1,0:T(8,128)(2,1)S(1)}, u32[]{:S(2)}, u32[]{:S(2)}) collective-permute-start(bf16[16,4608]{1,0:T(8,128)(2,1)} %get-tuple-element.107), channel_id=1, source_target_pairs={{0,24},{1,25},{2,26},{3,27},{4,28},{5,29},{6,30},{7,31},{8,16},{9,... | collective-permute-start | bytes 442376 | tf_op jit(solution)/shard_map/ppermute | solution.py:649
  15.9 2.1 %collective-permute-start.6 = (bf16[16,4608]{1,0:T(8,128)(2,1)}, bf16[16,4608]{1,0:T(8,128)(2,1)S(1)}, u32[]{:S(2)}, u32[]{:S(2)}) collective-permute-start(bf16[16,4608]{1,0:T(8,128)(2,1)} %get-tuple-element.107), channel_id=1, source_target_pairs={{0,8},{1,9},{2,10},{3,11},{4,12},{5,13},{6,14},{7,15},{8,0},{9,1},... | collective-permute-start | bytes 442376 | tf_op jit(solution)/shard_map/ppermute | solution.py:649
  18.0 2.4 %collective-permute-start.5 = (bf16[4,16,1664]{2,1,0:T(8,128)(2,1)S(1)}, bf16[4,16,1664]{2,1,0:T(8,128)(2,1)S(1)}, u32[]{:S(2)}, u32[]{:S(2)}) collective-permute-start(bf16[4,16,1664]{2,1,0:T(8,128)(2,1)S(1)} %get-tuple-element.220), channel_id=1, source_target_pairs={{0,6},{1,7},{2,4},{3,5},{4,2},{5,3},{6,0},{7,1},{8,14},{9,15},{10,... | collective-permute-start | bytes 638984 | tf_op jit(solution)/shard_map/ppermute | solution.py:649
  33.6 2.6 %project.1 = (f32[8,512]{1,0:T(8,128)S(1)}, bf16[512,1024]{1,0:T(8,128)(2,1)S(1)}, bf16[512,1024]{1,0:T(8,128)(2,1)S(1)}, bf16[512,1024]{1,0:T(8,128)(2,1)S(1)}) custom-call(s32[4]{0:T(128)S(1)} %pad_add_fusion.info_ref, bf16[1024,512]{1,0:T(8,128)(2,1)S(1)} %copy-done.1, bf16[16,16,1664]{2,1,0:T(8,128)(2,1)S(1)} %bitcast.89, ...), custom_call_target="tpu_custom_call" | custom-call | flops 60000000 | tf_op jit(solution)/shard_map/project/pallas_call | solution.py:618
  36.2 7.2 %self_forward.1 = (bf16[512,1024]{1,0:T(8,128)(2,1)S(1)}, f32[8,1,1024]{2,1,0:T(1,128)S(1)}) custom-call(s32[4]{0:T(128)S(1)} %pad_add_fusion.info_ref, bf16[512,1024]{1,0:T(8,128)(2,1)S(1)} %get-tuple-element.119.q_ref, bf16[512,1024]{1,0:T(8,128)(2,1)S(1)} %get-tuple-element.120.k_ref, bf16[512,1024]{1,0:T(8,128)(2,1)S(1)} %get-tuple-element.121.v_ref), custom_call_target="tpu_custom_call" | custom-call | flops 160000000 | tf_op jit(solution)/shard_map/self_forward/pallas_call | solution.py:618
  43.4 2.2 %collective-permute-done.10 = bf16[4,16,2048]{2,1,0:T(8,128)(2,1)S(1)} collective-permute-done((bf16[4,16,2048]{2,1,0:T(8,128)(2,1)S(1)}, bf16[4,16,2048]{2,1,0:T(8,128)(2,1)S(1)}, u32[]{:S(2)}, u32[]{:S(2)}) %collective-permute-start.10) | collective-permute-done | bytes 262176 | tf_op jit(solution)/shard_map/ppermute | solution.py:649
  49.5 4.2 %image_project.1 = (bf16[512,2048]{1,0:T(8,128)(2,1)S(1)}, bf16[3,512,784]{2,1,0:T(8,128)(2,1)S(1)}, bf16[3,512,784]{2,1,0:T(8,128)(2,1)S(1)}) custom-call(s32[4]{0:T(128)S(1)} %pad_add_fusion.info_ref, bf16[2352,512]{1,0:T(8,128)(2,1)S(1)} %copy-done, bf16[16,16,2048]{2,1,0:T(8,128)(2,1)S(1)} %bitcast.85, ...), custom_call_target="tpu_custom_call" | custom-call | flops 120000000 | tf_op jit(solution)/shard_map/image_project/pallas_call | solution.py:618
  53.7 2.0 %mid.1 = (f32[1024,512]{1,0:T(8,128)S(1)}, f32[8,1024]{1,0:T(8,128)S(1)}, bf16[512,1024]{1,0:T(8,128)(2,1)S(1)}) custom-call(bf16[1024,512]{1,0:T(8,128)(2,1)S(1)} %copy-done.1, bf16[512,1024]{1,0:T(8,128)(2,1)S(1)} %get-tuple-element.122.o_ref, bf16[512,2048]{1,0:T(8,128)(2,1)S(1)} %get-tuple-element.127.w_ref, f32[8,512]{1,0:T(8,128)S(1)} %get-tuple-element.128.norm_ref), custom_call_target="tpu_custom_call" | custom-call | flops 60000000 | tf_op jit(solution)/shard_map/mid/pallas_call | solution.py:618
  55.7 13.8 %cross_forward.1 = (bf16[512,1024]{1,0:T(8,128)(2,1)S(1)}, f32[8,1,1024]{2,1,0:T(1,128)S(1)}) custom-call(s32[4]{0:T(128)S(1)} %pad_add_fusion.info_ref, bf16[512,1024]{1,0:T(8,128)(2,1)S(1)} %get-tuple-element.129.q_ref, bf16[3,512,784]{2,1,0:T(8,128)(2,1)S(1)} %get-tuple-element.130.k_ref, bf16[3,512,784]{2,1,0:T(8,128)(2,1)S(1)} %get-tuple-element.131.v_ref), custom_call_target="tpu_custom_call" | custom-call | flops 320000000 | tf_op jit(solution)/shard_map/cross_forward/pallas_call | solution.py:618
  69.9 3.0 %collective-permute-done.17.wfar_ref = bf16[16,16,2560]{2,1,0:T(8,128)(2,1)S(1)} collective-permute-done((bf16[16,16,2560]{2,1,0:T(8,128)(2,1)S(1)}, bf16[16,16,2560]{2,1,0:T(8,128)(2,1)S(1)}, u32[]{:S(2)}, u32[]{:S(2)}) %collective-permute-start.17) | collective-permute-done | bytes 1310752 | tf_op jit(solution)/shard_map/ppermute | solution.py:649
  72.9 13.2 %feed.1 = (bf16[1024,512]{1,0:T(8,128)(2,1)}, f32[1024,512]{1,0:T(8,128)S(1)}, bf16[512,1024]{1,0:T(8,128)(2,1)S(1)}, bf16[16,16,2560]{2,1,0:T(8,128)(2,1)S(1)},...) custom-call(s32[4]{0:T(128)S(1)} %pad_add_fusion.info_ref, bf16[512,1024]{1,0:T(8,128)(2,1)S(1)} %get-tuple-element.132.o_ref, ...), custom_call_target="tpu_custom_call" | custom-call | flops 300000000 | tf_op jit(solution)/shard_map/feed/pallas_call | solution.py:618
  87.5 13.0 %cross_backward.2 = (bf16[256,1024]{1,0:T(8,128)(2,1)S(1)}, bf16[3,256,784]{2,1,0:T(8,128)(2,1)S(1)}, bf16[3,256,784]{2,1,0:T(8,128)(2,1)S(1)}) custom-call(s32[4]{0:T(128)S(1)} %pad_add_fusion.info_ref, bf16[512,1024]{1,0:T(8,128)(2,1)S(1)} %get-tuple-element.129.q_ref, bf16[3,512,784]{2,1,0:T(8,128)(2,1)S(1)} %get-tuple-element.130.k_ref, ...), custom_call_target="tpu_custom_call" | custom-call | flops 280000000 | tf_op jit(solution)/shard_map/cross_backward/pallas_call | solution.py:618
  105.8 12.7 %cross_backward.3 = (bf16[256,1024]{1,0:T(8,128)(2,1)S(1)}, bf16[3,256,784]{2,1,0:T(8,128)(2,1)S(1)}, bf16[3,256,784]{2,1,0:T(8,128)(2,1)S(1)}) custom-call(s32[4]{0:T(128)S(1)} %pad_add_fusion.info_ref, bf16[512,1024]{1,0:T(8,128)(2,1)S(1)} %get-tuple-element.129.q_ref, bf16[3,512,784]{2,1,0:T(8,128)(2,1)S(1)} %get-tuple-element.130.k_ref, ...), custom_call_target="tpu_custom_call" | custom-call | flops 280000000 | tf_op jit(solution)/shard_map/cross_backward/pallas_call | solution.py:618
  120.9 7.8 %inner.1 = (f32[1024,512]{1,0:T(8,128)S(1)}, bf16[512,1024]{1,0:T(8,128)(2,1)S(1)}, bf16[16,16,2048]{2,1,0:T(8,128)(2,1)S(1)}, bf16[16,16,2048]{2,1,0:T(8,128)(2,1)S(1)}, f32[8,512]{1,0:T(8,128)S(1)}) custom-call(s32[4]{0:T(128)S(1)} %pad_add_fusion.info_ref, bf16[256,1024]{1,0:T(8,128)(2,1)S(1)} %get-tuple-element.142.dq0_ref, ...), custom_call_target="tpu_custom_call" | custom-call | flops 200000000 | tf_op jit(solution)/shard_map/inner/pallas_call | solution.py:618
  128.8 6.1 %self_backward.2 = (bf16[256,1024]{1,0:T(8,128)(2,1)S(1)}, bf16[256,1024]{1,0:T(8,128)(2,1)S(1)}, bf16[256,1024]{1,0:T(8,128)(2,1)S(1)}) custom-call(s32[4]{0:T(128)S(1)} %pad_add_fusion.info_ref, bf16[512,1024]{1,0:T(8,128)(2,1)S(1)} %get-tuple-element.119.q_ref, bf16[512,1024]{1,0:T(8,128)(2,1)S(1)} %get-tuple-element.120.k_ref, ...), custom_call_target="tpu_custom_call" | custom-call | flops 140000000 | tf_op jit(solution)/shard_map/self_backward/pallas_call | solution.py:618
  135.4 3.1 %collective-permute-start.25 = (bf16[4,16,2048]{2,1,0:T(8,128)(2,1)S(1)}, bf16[4,16,2048]{2,1,0:T(8,128)(2,1)S(1)}, u32[]{:S(2)}, u32[]{:S(2)}) collective-permute-start(bf16[4,16,2048]{2,1,0:T(8,128)(2,1)S(1)} %get-tuple-element.204), channel_id=1, source_target_pairs={{0,6},{1,7},{2,4},{3,5},{4,2},{5,3},{6,0},{7,1},{8,14},{9,15},{10,... | collective-permute-start | bytes 786440 | tf_op jit(solution)/shard_map/ppermute | solution.py:649
  139.1 5.9 %self_backward.3 = (bf16[256,1024]{1,0:T(8,128)(2,1)S(1)}, bf16[256,1024]{1,0:T(8,128)(2,1)S(1)}, bf16[256,1024]{1,0:T(8,128)(2,1)S(1)}) custom-call(s32[4]{0:T(128)S(1)} %pad_add_fusion.info_ref, bf16[512,1024]{1,0:T(8,128)(2,1)S(1)} %get-tuple-element.119.q_ref, bf16[512,1024]{1,0:T(8,128)(2,1)S(1)} %get-tuple-element.120.k_ref, ...), custom_call_target="tpu_custom_call" | custom-call | flops 140000000 | tf_op jit(solution)/shard_map/self_backward/pallas_call | solution.py:618
  145.1 2.5 %project_weight.1 = (bf16[16,16,1664]{2,1,0:T(8,128)(2,1)S(1)}, bf16[16,16,1664]{2,1,0:T(8,128)(2,1)S(1)}) custom-call(s32[4]{0:T(128)S(1)} %pad_add_fusion.info_ref, bf16[1024,512]{1,0:T(8,128)(2,1)S(1)} %copy-done.1, bf16[256,1024]{1,0:T(8,128)(2,1)S(1)} %get-tuple-element.156.dq0_ref, bf16[256,1024]{1,0:T(8,128)(2,1)S(1)} %get-tuple-element.161.dq1_ref, ...), custom_call_target="tpu_custom_call" | custom-call | flops 60000000 | tf_op jit(solution)/shard_map/project_weight/pallas_call | solution.py:618
  147.6 2.7 %collective-permute-start.26 = (bf16[16,16,1664]{2,1,0:T(8,128)(2,1)S(1)}, bf16[16,16,1664]{2,1,0:T(8,128)(2,1)S(1)}, u32[]{:S(2)}, u32[]{:S(2)}) collective-permute-start(bf16[16,16,1664]{2,1,0:T(8,128)(2,1)S(1)} %get-tuple-element.171), channel_id=1, source_target_pairs={{0,1},{1,0},{2,3},{3,2},{4,5},{5,4},{6,7},{7,6},{8,9},{9,8},{10,11... | collective-permute-start | bytes 2555912 | tf_op jit(solution)/shard_map/ppermute | solution.py:649
  151.4 3.9 %collective-permute-start.27 = (bf16[16,4608]{1,0:T(8,128)(2,1)S(1)}, bf16[16,4608]{1,0:T(8,128)(2,1)S(1)}, u32[]{:S(2)}, u32[]{:S(2)}) collective-permute-start(bf16[16,4608]{1,0:T(8,128)(2,1)S(1)} %pad_maximum_fusion.9), channel_id=1, source_target_pairs={{0,8},{1,9},{2,10},{3,11},{4,12},{5,13},{6,14},{7,15},{8,0},{9,1},... | collective-permute-start | bytes 442376 | tf_op jit(solution)/shard_map/ppermute | solution.py:649
  163.1 5.6 %image_grad.1 = f32[2352,512]{1,0:T(8,128)} custom-call(s32[4]{0:T(128)S(1)} %pad_add_fusion.info_ref, bf16[3,256,784]{2,1,0:T(8,128)(2,1)S(1)} %copy-done.5, bf16[3,256,784]{2,1,0:T(8,128)(2,1)S(1)} %copy-done.9, bf16[3,256,784]{2,1,0:T(8,128)(2,1)S(1)} %copy-done.7, bf16[3,256,784]{2,1,0:T(8,128)(2,1)S(1)} %get-tuple-element.154.dv1_ref, ...), custom_call_target="tpu_custom_call" | custom-call | flops 120000000 | tf_op jit(solution)/shard_map/image_grad/pallas_call | solution.py:618
  168.7 3.9 %token_grad.1 = f32[1024,512]{1,0:T(8,128)} custom-call(s32[4]{0:T(128)S(1)} %pad_add_fusion.info_ref, bf16[256,1024]{1,0:T(8,128)(2,1)S(1)} %get-tuple-element.156.dq0_ref, bf16[256,1024]{1,0:T(8,128)(2,1)S(1)} %get-tuple-element.161.dq1_ref, bf16[256,1024]{1,0:T(8,128)(2,1)S(1)} %get-tuple-element.162.dk0_ref, ...), custom_call_target="tpu_custom_call" | custom-call | flops 80000000 | tf_op jit(solution)/shard_map/token_grad/pallas_call | solution.py:618
  172.9 1.9 collective-permute-start.35
  174.8 2.5 %collective-permute-start.33 = (bf16[16,1664]{1,0:T(8,128)(2,1)S(1)}, bf16[16,1664]{1,0:T(8,128)(2,1)S(1)}, u32[]{:S(2)}, u32[]{:S(2)}) collective-permute-start(bf16[16,1664]{1,0:T(8,128)(2,1)S(1)} %get-tuple-element.218), channel_id=1, source_target_pairs={{0,8},{1,9},{2,10},{3,11},{4,12},{5,13},{6,14},{7,15},{8,0},{9,1},... | collective-permute-start | bytes 159752 | tf_op jit(solution)/shard_map/ppermute | solution.py:649
  177.4 2.0 %collective-permute-done.35.refs_7_ = bf16[16,1664]{1,0:T(8,128)(2,1)S(1)} collective-permute-done((bf16[16,1664]{1,0:T(8,128)(2,1)S(1)}, bf16[16,1664]{1,0:T(8,128)(2,1)S(1)}, u32[]{:S(2)}, u32[]{:S(2)}) %collective-permute-start.35) | collective-permute-done | bytes 53280 | tf_op jit(solution)/shard_map/ppermute | solution.py:649
  183.2 1.8 collective-permute-start.39
  189.0 2.0 collective-permute-start.42
  191.5 1.9 collective-permute-start.40
  (159 shorter events, 49.2 us)
Async XLA Ops:
  2.4 7.6 %collective-permute-start.2 = (bf16[16,1664]{1,0:T(8,128)(2,1)}, bf16[16,1664]{1,0:T(8,128)(2,1)S(1)}, u32[]{:S(2)}, u32[]{:S(2)}) collective-permute-start(bf16[16,1664]{1,0:T(8,128)(2,1)} %get-tuple-element.105), channel_id=1, source_target_pairs={{0,24},{1,25},{2,26},{3,27},{4,28},{5,29},{6,30},{7,31},{8,16},{9,... | collective-permute-start | bytes 159752 | tf_op jit(solution)/shard_map/ppermute | solution.py:649
  13.5 8.9 %collective-permute-start.8 = (bf16[16,4608]{1,0:T(8,128)(2,1)}, bf16[16,4608]{1,0:T(8,128)(2,1)S(1)}, u32[]{:S(2)}, u32[]{:S(2)}) collective-permute-start(bf16[16,4608]{1,0:T(8,128)(2,1)} %get-tuple-element.107), channel_id=1, source_target_pairs={{0,24},{1,25},{2,26},{3,27},{4,28},{5,29},{6,30},{7,31},{8,16},{9,... | collective-permute-start | bytes 442376 | tf_op jit(solution)/shard_map/ppermute | solution.py:649
  15.9 12.4 %collective-permute-start.7 = (bf16[16,4608]{1,0:T(8,128)(2,1)}, bf16[16,4608]{1,0:T(8,128)(2,1)S(1)}, u32[]{:S(2)}, u32[]{:S(2)}) collective-permute-start(bf16[16,4608]{1,0:T(8,128)(2,1)} %get-tuple-element.107), channel_id=1, source_target_pairs={{0,16},{1,17},{2,18},{3,19},{4,20},{5,21},{6,22},{7,23},{8,24},{9,... | collective-permute-start | bytes 442376 | tf_op jit(solution)/shard_map/ppermute | solution.py:649
  15.9 12.3 %collective-permute-start.6 = (bf16[16,4608]{1,0:T(8,128)(2,1)}, bf16[16,4608]{1,0:T(8,128)(2,1)S(1)}, u32[]{:S(2)}, u32[]{:S(2)}) collective-permute-start(bf16[16,4608]{1,0:T(8,128)(2,1)} %get-tuple-element.107), channel_id=1, source_target_pairs={{0,8},{1,9},{2,10},{3,11},{4,12},{5,13},{6,14},{7,15},{8,0},{9,1},... | collective-permute-start | bytes 442376 | tf_op jit(solution)/shard_map/ppermute | solution.py:649
  18.0 10.3 %collective-permute-start.5 = (bf16[4,16,1664]{2,1,0:T(8,128)(2,1)S(1)}, bf16[4,16,1664]{2,1,0:T(8,128)(2,1)S(1)}, u32[]{:S(2)}, u32[]{:S(2)}) collective-permute-start(bf16[4,16,1664]{2,1,0:T(8,128)(2,1)S(1)} %get-tuple-element.220), channel_id=1, source_target_pairs={{0,6},{1,7},{2,4},{3,5},{4,2},{5,3},{6,0},{7,1},{8,14},{9,15},{10,... | collective-permute-start | bytes 638984 | tf_op jit(solution)/shard_map/ppermute | solution.py:649
  20.4 8.4 %collective-permute-start.4 = (bf16[4,16,1664]{2,1,0:T(8,128)(2,1)S(1)}, bf16[4,16,1664]{2,1,0:T(8,128)(2,1)S(1)}, u32[]{:S(2)}, u32[]{:S(2)}) collective-permute-start(bf16[4,16,1664]{2,1,0:T(8,128)(2,1)S(1)} %get-tuple-element.220), channel_id=1, source_target_pairs={{0,4},{1,5},{2,6},{3,7},{4,0},{5,1},{6,2},{7,3},{8,12},{9,13},{10,... | collective-permute-start | bytes 638984 | tf_op jit(solution)/shard_map/ppermute | solution.py:649
  22.4 6.4 %collective-permute-start.3 = (bf16[4,16,1664]{2,1,0:T(8,128)(2,1)S(1)}, bf16[4,16,1664]{2,1,0:T(8,128)(2,1)S(1)}, u32[]{:S(2)}, u32[]{:S(2)}) collective-permute-start(bf16[4,16,1664]{2,1,0:T(8,128)(2,1)S(1)} %get-tuple-element.220), channel_id=1, source_target_pairs={{0,2},{1,3},{2,0},{3,1},{4,6},{5,7},{6,4},{7,5},{8,10},{9,11},{10,... | collective-permute-start | bytes 638984 | tf_op jit(solution)/shard_map/ppermute | solution.py:649
  30.0 13.4 %collective-permute-start.11 = (bf16[4,16,2048]{2,1,0:T(8,128)(2,1)S(1)}, bf16[4,16,2048]{2,1,0:T(8,128)(2,1)S(1)}, u32[]{:S(2)}, u32[]{:S(2)}) collective-permute-start(bf16[4,16,2048]{2,1,0:T(8,128)(2,1)S(1)} %pad_maximum_fusion.7), channel_id=1, source_target_pairs={{0,4},{1,5},{2,6},{3,7},{4,0},{5,1},{6,2},{7,3},{8,12},{9,13},{10,... | collective-permute-start | bytes 786440 | tf_op jit(solution)/shard_map/ppermute | solution.py:649
  31.6 14.0 %collective-permute-start.10 = (bf16[4,16,2048]{2,1,0:T(8,128)(2,1)S(1)}, bf16[4,16,2048]{2,1,0:T(8,128)(2,1)S(1)}, u32[]{:S(2)}, u32[]{:S(2)}) collective-permute-start(bf16[4,16,2048]{2,1,0:T(8,128)(2,1)S(1)} %pad_maximum_fusion.7), channel_id=1, source_target_pairs={{0,2},{1,3},{2,0},{3,1},{4,6},{5,7},{6,4},{7,5},{8,10},{9,11},{10,... | collective-permute-start | bytes 786440 | tf_op jit(solution)/shard_map/ppermute | solution.py:649
  33.0 12.5 %collective-permute-start.12 = (bf16[4,16,2048]{2,1,0:T(8,128)(2,1)S(1)}, bf16[4,16,2048]{2,1,0:T(8,128)(2,1)S(1)}, u32[]{:S(2)}, u32[]{:S(2)}) collective-permute-start(bf16[4,16,2048]{2,1,0:T(8,128)(2,1)S(1)} %pad_maximum_fusion.7), channel_id=1, source_target_pairs={{0,6},{1,7},{2,4},{3,5},{4,2},{5,3},{6,0},{7,1},{8,14},{9,15},{10,... | collective-permute-start | bytes 786440 | tf_op jit(solution)/shard_map/ppermute | solution.py:649
  45.9 23.6 %collective-permute-start.14 = (bf16[4,16,2560]{2,1,0:T(8,128)(2,1)S(1)}, bf16[4,16,2560]{2,1,0:T(8,128)(2,1)S(1)}, u32[]{:S(2)}, u32[]{:S(2)}) collective-permute-start(bf16[4,16,2560]{2,1,0:T(8,128)(2,1)S(1)} %pad_maximum_fusion.3), channel_id=1, source_target_pairs={{0,2},{1,3},{2,0},{3,1},{4,6},{5,7},{6,4},{7,5},{8,10},{9,11},{10,... | collective-permute-start | bytes 983048 | tf_op jit(solution)/shard_map/ppermute | solution.py:649
  47.4 22.1 %collective-permute-start.15 = (bf16[4,16,2560]{2,1,0:T(8,128)(2,1)S(1)}, bf16[4,16,2560]{2,1,0:T(8,128)(2,1)S(1)}, u32[]{:S(2)}, u32[]{:S(2)}) collective-permute-start(bf16[4,16,2560]{2,1,0:T(8,128)(2,1)S(1)} %pad_maximum_fusion.3), channel_id=1, source_target_pairs={{0,4},{1,5},{2,6},{3,7},{4,0},{5,1},{6,2},{7,3},{8,12},{9,13},{10,... | collective-permute-start | bytes 983048 | tf_op jit(solution)/shard_map/ppermute | solution.py:649
  48.1 21.4 %collective-permute-start.16 = (bf16[4,16,2560]{2,1,0:T(8,128)(2,1)S(1)}, bf16[4,16,2560]{2,1,0:T(8,128)(2,1)S(1)}, u32[]{:S(2)}, u32[]{:S(2)}) collective-permute-start(bf16[4,16,2560]{2,1,0:T(8,128)(2,1)S(1)} %pad_maximum_fusion.3), channel_id=1, source_target_pairs={{0,6},{1,7},{2,4},{3,5},{4,2},{5,3},{6,0},{7,1},{8,14},{9,15},{10,... | collective-permute-start | bytes 983048 | tf_op jit(solution)/shard_map/ppermute | solution.py:649
  87.4 13.1 %collective-permute-start.18 = (bf16[16,16,2560]{2,1,0:T(8,128)(2,1)S(1)}, bf16[16,16,2560]{2,1,0:T(8,128)(2,1)S(1)}, u32[]{:S(2)}, u32[]{:S(2)}) collective-permute-start(bf16[16,16,2560]{2,1,0:T(8,128)(2,1)S(1)} %get-tuple-element.144), channel_id=1, source_target_pairs={{0,1},{1,0},{2,3},{3,2},{4,5},{5,4},{6,7},{7,6},{8,9},{9,8},{10,11... | collective-permute-start | bytes 3932168 | tf_op jit(solution)/shard_map/ppermute | solution.py:649
  102.2 17.2 %collective-permute-start.19 = (bf16[4,16,2560]{2,1,0:T(8,128)(2,1)}, bf16[4,16,2560]{2,1,0:T(8,128)(2,1)S(1)}, u32[]{:S(2)}, u32[]{:S(2)}) collective-permute-start(bf16[4,16,2560]{2,1,0:T(8,128)(2,1)} %get-tuple-element.201), channel_id=1, source_target_pairs={{0,2},{1,3},{2,0},{3,1},{4,6},{5,7},{6,4},{7,5},{8,10},{9,11},{10,... | collective-permute-start | bytes 983048 | tf_op jit(solution)/shard_map/ppermute | solution.py:649
  103.7 15.8 %collective-permute-start.21 = (bf16[4,16,2560]{2,1,0:T(8,128)(2,1)}, bf16[4,16,2560]{2,1,0:T(8,128)(2,1)S(1)}, u32[]{:S(2)}, u32[]{:S(2)}) collective-permute-start(bf16[4,16,2560]{2,1,0:T(8,128)(2,1)} %get-tuple-element.202), channel_id=1, source_target_pairs={{0,6},{1,7},{2,4},{3,5},{4,2},{5,3},{6,0},{7,1},{8,14},{9,15},{10,... | collective-permute-start | bytes 983048 | tf_op jit(solution)/shard_map/ppermute | solution.py:649
  104.9 15.8 %collective-permute-start.20 = (bf16[4,16,2560]{2,1,0:T(8,128)(2,1)S(1)}, bf16[4,16,2560]{2,1,0:T(8,128)(2,1)S(1)}, u32[]{:S(2)}, u32[]{:S(2)}) collective-permute-start(bf16[4,16,2560]{2,1,0:T(8,128)(2,1)S(1)} %get-tuple-element.203), channel_id=1, source_target_pairs={{0,4},{1,5},{2,6},{3,7},{4,0},{5,1},{6,2},{7,3},{8,12},{9,13},{10,... | collective-permute-start | bytes 983048 | tf_op jit(solution)/shard_map/ppermute | solution.py:649
  128.7 6.3 %collective-permute-start.22 = (bf16[16,16,2048]{2,1,0:T(8,128)(2,1)S(1)}, bf16[16,16,2048]{2,1,0:T(8,128)(2,1)S(1)}, u32[]{:S(2)}, u32[]{:S(2)}) collective-permute-start(bf16[16,16,2048]{2,1,0:T(8,128)(2,1)S(1)} %get-tuple-element.159), channel_id=1, source_target_pairs={{0,1},{1,0},{2,3},{3,2},{4,5},{5,4},{6,7},{7,6},{8,9},{9,8},{10,11... | collective-permute-start | bytes 3145736 | tf_op jit(solution)/shard_map/ppermute | solution.py:649
  135.4 14.9 %collective-permute-start.25 = (bf16[4,16,2048]{2,1,0:T(8,128)(2,1)S(1)}, bf16[4,16,2048]{2,1,0:T(8,128)(2,1)S(1)}, u32[]{:S(2)}, u32[]{:S(2)}) collective-permute-start(bf16[4,16,2048]{2,1,0:T(8,128)(2,1)S(1)} %get-tuple-element.204), channel_id=1, source_target_pairs={{0,6},{1,7},{2,4},{3,5},{4,2},{5,3},{6,0},{7,1},{8,14},{9,15},{10,... | collective-permute-start | bytes 786440 | tf_op jit(solution)/shard_map/ppermute | solution.py:649
  138.5 11.9 %collective-permute-start.24 = (bf16[4,16,2048]{2,1,0:T(8,128)(2,1)S(1)}, bf16[4,16,2048]{2,1,0:T(8,128)(2,1)S(1)}, u32[]{:S(2)}, u32[]{:S(2)}) collective-permute-start(bf16[4,16,2048]{2,1,0:T(8,128)(2,1)S(1)} %get-tuple-element.205), channel_id=1, source_target_pairs={{0,4},{1,5},{2,6},{3,7},{4,0},{5,1},{6,2},{7,3},{8,12},{9,13},{10,... | collective-permute-start | bytes 786440 | tf_op jit(solution)/shard_map/ppermute | solution.py:649
  138.5 12.7 %collective-permute-start.23 = (bf16[4,16,2048]{2,1,0:T(8,128)(2,1)S(1)}, bf16[4,16,2048]{2,1,0:T(8,128)(2,1)S(1)}, u32[]{:S(2)}, u32[]{:S(2)}) collective-permute-start(bf16[4,16,2048]{2,1,0:T(8,128)(2,1)S(1)} %get-tuple-element.206), channel_id=1, source_target_pairs={{0,2},{1,3},{2,0},{3,1},{4,6},{5,7},{6,4},{7,5},{8,10},{9,11},{10,... | collective-permute-start | bytes 786440 | tf_op jit(solution)/shard_map/ppermute | solution.py:649
  147.6 10.2 %collective-permute-start.26 = (bf16[16,16,1664]{2,1,0:T(8,128)(2,1)S(1)}, bf16[16,16,1664]{2,1,0:T(8,128)(2,1)S(1)}, u32[]{:S(2)}, u32[]{:S(2)}) collective-permute-start(bf16[16,16,1664]{2,1,0:T(8,128)(2,1)S(1)} %get-tuple-element.171), channel_id=1, source_target_pairs={{0,1},{1,0},{2,3},{3,2},{4,5},{5,4},{6,7},{7,6},{8,9},{9,8},{10,11... | collective-permute-start | bytes 2555912 | tf_op jit(solution)/shard_map/ppermute | solution.py:649
  151.4 10.3 %collective-permute-start.27 = (bf16[16,4608]{1,0:T(8,128)(2,1)S(1)}, bf16[16,4608]{1,0:T(8,128)(2,1)S(1)}, u32[]{:S(2)}, u32[]{:S(2)}) collective-permute-start(bf16[16,4608]{1,0:T(8,128)(2,1)S(1)} %pad_maximum_fusion.9), channel_id=1, source_target_pairs={{0,8},{1,9},{2,10},{3,11},{4,12},{5,13},{6,14},{7,15},{8,0},{9,1},... | collective-permute-start | bytes 442376 | tf_op jit(solution)/shard_map/ppermute | solution.py:649
  155.3 17.4 %collective-permute-start.28 = (bf16[16,4608]{1,0:T(8,128)(2,1)S(1)}, bf16[16,4608]{1,0:T(8,128)(2,1)S(1)}, u32[]{:S(2)}, u32[]{:S(2)}) collective-permute-start(bf16[16,4608]{1,0:T(8,128)(2,1)S(1)} %pad_maximum_fusion.10), channel_id=1, source_target_pairs={{0,16},{1,17},{2,18},{3,19},{4,20},{5,21},{6,22},{7,23},{8,24},{9,... | collective-permute-start | bytes 442376 | tf_op jit(solution)/shard_map/ppermute | solution.py:649
  156.1 16.7 %collective-permute-start.29 = (bf16[16,4608]{1,0:T(8,128)(2,1)S(1)}, bf16[16,4608]{1,0:T(8,128)(2,1)S(1)}, u32[]{:S(2)}, u32[]{:S(2)}) collective-permute-start(bf16[16,4608]{1,0:T(8,128)(2,1)S(1)} %pad_maximum_fusion.11), channel_id=1, source_target_pairs={{0,24},{1,25},{2,26},{3,27},{4,28},{5,29},{6,30},{7,31},{8,16},{9,... | collective-permute-start | bytes 442376 | tf_op jit(solution)/shard_map/ppermute | solution.py:649
  158.1 14.6 %collective-permute-start.32 = (bf16[4,16,1664]{2,1,0:T(8,128)(2,1)S(1)}, bf16[4,16,1664]{2,1,0:T(8,128)(2,1)S(1)}, u32[]{:S(2)}, u32[]{:S(2)}) collective-permute-start(bf16[4,16,1664]{2,1,0:T(8,128)(2,1)S(1)} %get-tuple-element.207), channel_id=1, source_target_pairs={{0,6},{1,7},{2,4},{3,5},{4,2},{5,3},{6,0},{7,1},{8,14},{9,15},{10,... | collective-permute-start | bytes 638984 | tf_op jit(solution)/shard_map/ppermute | solution.py:649
  159.5 13.2 %collective-permute-start.31 = (bf16[4,16,1664]{2,1,0:T(8,128)(2,1)S(1)}, bf16[4,16,1664]{2,1,0:T(8,128)(2,1)S(1)}, u32[]{:S(2)}, u32[]{:S(2)}) collective-permute-start(bf16[4,16,1664]{2,1,0:T(8,128)(2,1)S(1)} %get-tuple-element.208), channel_id=1, source_target_pairs={{0,4},{1,5},{2,6},{3,7},{4,0},{5,1},{6,2},{7,3},{8,12},{9,13},{10,... | collective-permute-start | bytes 638984 | tf_op jit(solution)/shard_map/ppermute | solution.py:649
  161.7 11.0 %collective-permute-start.30 = (bf16[4,16,1664]{2,1,0:T(8,128)(2,1)S(1)}, bf16[4,16,1664]{2,1,0:T(8,128)(2,1)S(1)}, u32[]{:S(2)}, u32[]{:S(2)}) collective-permute-start(bf16[4,16,1664]{2,1,0:T(8,128)(2,1)S(1)} %get-tuple-element.209), channel_id=1, source_target_pairs={{0,2},{1,3},{2,0},{3,1},{4,6},{5,7},{6,4},{7,5},{8,10},{9,11},{10,... | collective-permute-start | bytes 638984 | tf_op jit(solution)/shard_map/ppermute | solution.py:649
  172.9 6.5 %collective-permute-start.35 = (bf16[16,1664]{1,0:T(8,128)(2,1)S(1)}, bf16[16,1664]{1,0:T(8,128)(2,1)S(1)}, u32[]{:S(2)}, u32[]{:S(2)}) collective-permute-start(bf16[16,1664]{1,0:T(8,128)(2,1)S(1)} %get-tuple-element.216), channel_id=1, source_target_pairs={{0,24},{1,25},{2,26},{3,27},{4,28},{5,29},{6,30},{7,31},{8,16},{9,... | collective-permute-start | bytes 159752 | tf_op jit(solution)/shard_map/ppermute | solution.py:649
  174.8 5.7 %collective-permute-start.34 = (bf16[16,1664]{1,0:T(8,128)(2,1)S(1)}, bf16[16,1664]{1,0:T(8,128)(2,1)S(1)}, u32[]{:S(2)}, u32[]{:S(2)}) collective-permute-start(bf16[16,1664]{1,0:T(8,128)(2,1)S(1)} %get-tuple-element.217), channel_id=1, source_target_pairs={{0,16},{1,17},{2,18},{3,19},{4,20},{5,21},{6,22},{7,23},{8,24},{9,... | collective-permute-start | bytes 159752 | tf_op jit(solution)/shard_map/ppermute | solution.py:649
  174.8 5.6 %collective-permute-start.33 = (bf16[16,1664]{1,0:T(8,128)(2,1)S(1)}, bf16[16,1664]{1,0:T(8,128)(2,1)S(1)}, u32[]{:S(2)}, u32[]{:S(2)}) collective-permute-start(bf16[16,1664]{1,0:T(8,128)(2,1)S(1)} %get-tuple-element.218), channel_id=1, source_target_pairs={{0,8},{1,9},{2,10},{3,11},{4,12},{5,13},{6,14},{7,15},{8,0},{9,1},... | collective-permute-start | bytes 159752 | tf_op jit(solution)/shard_map/ppermute | solution.py:649
  189.0 5.4 %collective-permute-start.42 = (f32[8,128]{1,0:T(8,128)S(1)}, f32[8,128]{1,0:T(8,128)S(1)}, u32[]{:S(2)}, u32[]{:S(2)}) collective-permute-start(f32[8,128]{1,0:T(8,128)S(1)} %add_add_fusion.refs_0_), channel_id=1, source_target_pairs={{0,24},{1,25},{2,26},{3,27},{4,28},{5,29},{6,30},{7,31},{8,16},{9,... | collective-permute-start | bytes 12296 | tf_op jit(solution)/shard_map/ppermute | solution.py:649
  (36 other events, 224.7 us)

commit v3 on v2

--- a/solution.py
+++ b/solution.py
@@ -74,7 +74,7 @@
     for k in range(2 * near_ref.shape[0]):
         ref = far_ref if k & 1 else near_ref
         row = pl.multiple_of((me ^ k) * size, size)
-        out_ref[pl.ds(row, size), :] = ref[exchange_slot(k)]
+        out_ref[pl.ds(row, size), :] = ref[exchange_slot(k, ref.shape[0])]
 
 
 def spread_blocks(me, source, near_ref, far_ref, col):
@@ -87,10 +87,15 @@
     for k in range(2 * near_ref.shape[0]):
         ref = far_ref if k & 1 else near_ref
         row = pl.multiple_of((me ^ k) * size, size)
-        ref[exchange_slot(k), :, cols] = source[pl.ds(row, size), :].astype(BF16)
-
-
-def pack_kernel(wa_ref, wf_ref, wn_ref, first_ref, rest_ref):
+        ref[exchange_slot(k, ref.shape[0]), :, cols] = source[pl.ds(row, size), :].astype(BF16)
+
+
+def pack_kernel(valid_ref, segment_ref, wa_ref, wf_ref, wn_ref, info_ref, first_ref, rest_ref):
+    segment = segment_ref[...]
+    info_ref[0] = jnp.sum((segment < 1).astype(jnp.int32))
+    info_ref[1] = jnp.sum((segment < 2).astype(jnp.int32))
+    info_ref[2] = valid_ref[0]
+    info_ref[3] = device_index()
     width, hidden = wa_ref.shape[2], wf_ref.shape[2]
     for slot in range(3):
         first_ref[:, slot * width : (slot + 1) * width] = wa_ref[slot].astype(BF16)
@@ -240,7 +245,7 @@
     dv_ref[...] = sum_v[...].astype(BF16)
 
 
-def mid_kernel(x_ref, o_ref, w_ref, norm_ref, n_ref, r_ref, q_ref):
+def mid_kernel(x_ref, o_ref, w_ref, norm_ref, n_ref, nlow_ref, r_ref, q_ref):
     gain, shift = norm_ref[0:1, :], norm_ref[3:4, :]
     width = x_ref.shape[1]
 
@@ -250,6 +255,7 @@
         yield
         normed, scale = normalise(x_ref[rows, :].astype(F32) + branch)
         n_ref[rows, :] = normed
+        nlow_ref[rows, :] = normed.astype(BF16)
         r_ref[:, rows] = jnp.transpose(jnp.broadcast_to(scale, (QB, 128)))[0:8]
         low = (normed * gain + shift).astype(BF16)
         yield
@@ -443,9 +449,9 @@
 
 def inner_kernel(
     info_ref, dq0_ref, dq1_ref, dh2_ref, n1_ref, r1_ref, o_ref, wnear_ref, wfar_ref,
-    norm_ref, image_ref, dk0_ref, dk1_ref, dv0_ref, dv1_ref,
-    dh_ref, do_ref, near_ref, far_ref, dnorm_ref,
-    sum_image, sum_inner, sum_norm, all_low, all_da, w_ref,
+    norm_ref, image_ref, dk0_ref, dk1_ref, dv0_ref, dv1_ref, feed_ref,
+    dh_ref, do_ref, near_ref, far_ref,
+    sum_image, sum_inner, sum_norm, all_low, all_da, w_ref, columns,
 ):
     place_blocks(info_ref[3], wnear_ref, wfar_ref, w_ref)
     sum_norm[...] = jnp.zeros(sum_norm.shape, F32)
@@ -457,7 +463,7 @@
         dq = jnp.concatenate([dq0_ref[:, rows], dq1_ref[:, rows]], axis=0)
         back = dot(dq, w_ref[:, width : 2 * width], 0, 1)
         yield
-        normed = n1_ref[rows, :]
+        normed = n1_ref[rows, :].astype(F32)
         all_low[rows, :] = (normed * gain + shift).astype(BF16)
         dx1 = dh2_ref[rows, :] + back
         sum_norm[0:1, :] += column_sum(dx1 * normed)
@@ -486,7 +492,10 @@
     dq = jnp.concatenate([dq0_ref[...], dq1_ref[...]], axis=0)
     sum_inner[...] = dot(all_low[...], dq, 0, 1)
     spread_blocks(me, sum_inner, near_ref, far_ref, width)
-    dnorm_ref[...] = sum_norm[...]
+    rows = [sum_norm[0:1], feed_ref[1:2], feed_ref[2:3]]
+    rows += [sum_norm[1:2], feed_ref[4:5], feed_ref[5:6], jnp.zeros((122, width), F32)]
+    columns[...] = jnp.transpose(jnp.concatenate(rows, axis=0))
+    spread_blocks(me, columns, near_ref, far_ref, 4 * width)
 
 
 def image_grad_kernel(
@@ -503,16 +512,12 @@
 
 
 def project_weight_kernel(
-    info_ref, x_ref, dq0_ref, dq1_ref, dk0_ref, dk1_ref, dv0_ref, dv1_ref, inner_ref, feed_ref,
-    near_ref, far_ref, total,
+    info_ref, x_ref, dq0_ref, dq1_ref, dk0_ref, dk1_ref, dv0_ref, dv1_ref, near_ref, far_ref, total
 ):
     width = x_ref.shape[1]
     refs = (dq0_ref, dq1_ref, dk0_ref, dk1_ref, dv0_ref, dv1_ref)
     grads = jnp.concatenate([ref[...] for ref in refs], axis=0)
     total[:, 0 : 3 * width] = dot(x_ref[...], grads, 0, 1)
-    order = [inner_ref[0:1], feed_ref[1:2], feed_ref[2:3]]
-    order += [inner_ref[1:2], feed_ref[4:5], feed_ref[5:6], jnp.zeros((122, width), F32)]
-    total[:, 3 * width :] = jnp.transpose(jnp.concatenate(order, axis=0))
     spread_blocks(info_ref[3], total, near_ref, far_ref, 0)
 
 
@@ -578,7 +583,7 @@
     for slot in range(2):
         value = grad(both, slot * hidden, hidden)
         tensor(8 + slot, value, slot, wf, mf, vf, (gf, omf, ovf, uf), WEIGHT_DECAY)
-    norms = jnp.transpose(grad(last, 3 * width, 128))
+    norms = jnp.transpose(grad(both, 2 * hidden + 5 * width, 128))
     for slot in range(6):
         row = slice(slot, slot + 1)
         tensor(10 + slot, norms[row, :], row, wn, mn, vn, (gn, omn, ovn, un), 0.0)
@@ -611,7 +616,7 @@
     return jax.ShapeDtypeStruct(dims, kind)
 
 
-def call(kernel, out_shape, operands, name, micros, info=True, scratch=(), grant=VMEM_GRANT):
+def call(kernel, out_shape, operands, name, micros, info=True, scratch=(), grant=VMEM_GRANT, told=False):
     specs = [VMEM] * len(operands)
     if info:
         specs[0] = SMEM
@@ -619,7 +624,7 @@
         kernel,
         out_shape=out_shape,
         in_specs=specs,
-        out_specs=jax.tree.map(lambda _: VMEM, out_shape),
+        out_specs=[SMEM] + [VMEM] * (len(out_shape) - 1) if told else jax.tree.map(lambda _: VMEM, out_shape),
         scratch_shapes=[
             pltpu.VMEM(dims[:-1], BF16) if dims[-1] is BF16 else pltpu.VMEM(dims, F32)
             for dims in scratch
@@ -640,8 +645,8 @@
     return lax.axis_size("wide") * lax.axis_size("narrow")
 
 
-def exchange_slot(k):
-    return (k >> 3) * 4 + ((k >> 1) & 3)
+def exchange_slot(k, slots):
+    return ((k >> 1) & 3) * (slots // 4) + (k >> 3)
 
 
 def swap(value, mask):
@@ -665,13 +670,14 @@
 
 
 def join_plane(parts):
-    return jnp.stack(parts, axis=1).reshape((-1,) + parts[0].shape[1:])
+    return jnp.concatenate(parts, axis=0)
 
 
 def scatter_core(near, far):
-    total = near.astype(F32) + swap(far, 1).astype(F32)
-    total = total.reshape((-1, 4) + near.shape[1:])
-    return [total[:, k] for k in range(4)]
+    far = swap(far, 1)
+    size = near.shape[0] // 4
+    parts = [slice(k * size, (k + 1) * size) for k in range(4)]
+    return [near[part].astype(F32) + far[part].astype(F32) for part in parts]
 
 
 def scatter_plane(parts):
@@ -693,7 +699,8 @@
 def block_order():
     order = [0] * device_count()
     for k in range(device_count()):
-        order[exchange_slot(k) + (k & 1) * (device_count() // 2)] = k
+        slots = device_count() // 2
+        order[exchange_slot(k, slots) + (k & 1) * slots] = k
     return jnp.array(order, jnp.int32) ^ device_index()
 
 
@@ -737,26 +744,23 @@
     tags, width = tokens.shape
     hidden_width = w_ffn.shape[2]
     shard = w_attn.shape[1]
-    segment = segments[0]
-    info = jnp.stack(
-        [jnp.sum(segment < 1), jnp.sum(segment < 2), valid_len[0], device_index()]
-    ).astype(jnp.int32)
-
-    first_part, second_part = call(
+    info, first_part, second_part = call(
         pack_kernel,
-        [shaped(shard, 3 * width + 128), shaped(shard, 5 * width + 2 * hidden_width)],
-        (w_attn, w_ffn, norm_params),
+        [shaped(4, kind=jnp.int32), shaped(shard, 3 * width + 128)]
+        + [shaped(shard, 5 * width + 2 * hidden_width)],
+        (valid_len, segments, w_attn, w_ffn, norm_params),
         "pack",
         1,
-        False,
+        True,
         (),
         60 * 2**20,
+        True,
     )
     first_far = gather_far(first_part)
     second_part = before(second_part, first_far)
     first_sent = [swap(first_far, mask) for mask in PLANE_MASKS]
     second_sent = [swap(second_part, mask) for mask in far_masks()]
-    first_sent, second_sent, info = lax.optimization_barrier((first_sent, second_sent, info))
+    first_sent, second_sent = lax.optimization_barrier((first_sent, second_sent))
     second_far = jnp.stack([second_part] + second_sent)
     third_far = second_far[:, :, 4 * width :]
     second_far = second_far[:, :, 0 : 4 * width]
@@ -803,9 +807,9 @@
         True,
         (),
     )
-    n1, r1, qc = call(
+    n1, n1_low, r1, qc = call(
         mid_kernel,
-        [f32_rows, shaped(8, tags, kind=F32), wide_shape],
+        [f32_rows, shaped(tags, width), shaped(8, tags, kind=F32), wide_shape],
         (tokens, o, w_second, norms),
         "mid",
         3,
@@ -875,22 +879,21 @@
     dqc1, dkc1, dvc1 = cross_backward(1, send_feed)
     own_feed = before(own_feed, dqc1)
     own_feed, send_feed = scatter_plane_end(own_feed, send_feed)
-    dh1, do, inner_near, inner_far, norm_inner = call(
+    dh1, do, inner_near, inner_far = call(
         inner_kernel,
         [
             f32_rows,
             wide_shape,
-            *spread_shapes(shard, 4 * width),
-            shaped(8, width, kind=F32),
+            *spread_shapes(shard, 4 * width + 128),
         ],
-        (before(info, send_feed), dqc0, dqc1, dh2, n1, r1, o, *second_blocks, norms)
-        + (image, dkc0, dkc1, dvc0, dvc1),
+        (before(info, send_feed), dqc0, dqc1, dh2, n1_low, r1, o, *second_blocks, norms)
+        + (image, dkc0, dkc1, dvc0, dvc1, norm_feed),
         "inner",
         10,
         True,
         [(width, 2 * width), (width, width), (8, width)]
         + [(tags, width, BF16)] * 2
-        + [(width, 4 * width, BF16)],
+        + [(width, 4 * width, BF16), (width, 128)],
     )
     inner_near, inner_far = split_blocks(inner_near, inner_far)
     dq0, dk0, dv0 = self_backward(0)
@@ -898,11 +901,11 @@
     own_inner, send_inner = scatter_plane(scatter_core(inner_near, inner_far))
     dq1, dk1, dv1 = self_backward(1, send_inner)
     grads = (dq0, dq1, dk0, dk1, dv0, dv1)
-    last_cols = 3 * width + 128
+    last_cols = 3 * width
     last_near, last_far = call(
         project_weight_kernel,
         spread_shapes(shard, last_cols),
-        (info, tokens) + grads + (norm_inner, norm_feed),
+        (info, tokens) + grads,
         "project_weight",
         3,
         True,

time: 201 us -> 198 us (0.985)
  waiting for transfers between devices: 25.2 us -> 31.2 us
  starting transfers between devices: 54.9 us -> 51.9 us
  other arithmetic: 6.24 us -> 3.36 us
  local copies, waits for them, and re-layouts: 3.87 us -> 1.66 us
    ppermute x43, waiting for transfers between devices: 25.2 us -> 31.2 us  [swap(): return lax.ppermute(value, AXES, [(i, i ^ mask) for i in range(count)])]
    ppermute x43, starting transfers between devices: 54.9 us -> 51.9 us  [swap(): return lax.ppermute(value, AXES, [(i, i ^ mask) for i in range(count)])]
  transfers between devices with their start and end apart: 43 -> 43, of which waited for: 20 -> 19; matrix products, arithmetic and copies ran while one was open for 2% -> 1% of each run, Pallas kernels for 40% -> 41%
where the time goes in v3:
time: 198 us; the launch traced here: 195 us
  Pallas kernels  105 us (53%)
  starting transfers between devices  51.9 us (26%)
  waiting for transfers between devices  31.2 us (16%)
  other arithmetic  3.36 us (2%)
  between operations  2.15 us (1%)
    pallas_call x17, Pallas kernels, call(): pl.pallas_call(kernel, out_shape=out_shape, in_specs=specs, out_specs=[SM...  105 us
    ppermute x43, starting transfers between devices, swap(): return lax.ppermute(value, AXES, [(i, i ^ mask) for i in range(count)])  51.9 us
    ppermute x43, waiting for transfers between devices, swap(): return lax.ppermute(value, AXES, [(i, i ^ mask) for i in range(count)])  31.2 us
  transfers between devices with their start and end apart: 43, of which 19 were waited for; matrix products, arithmetic and copies ran while one was open for 1% of the time, Pallas kernels for 41%

profile of v3, /device:TPU:0, one launch (start us, length us, event | category | flops | bytes accessed | tf_op | source)
XLA Modules:
  0.0 194.9 jit_solution(10274232966999531903)
XLA Ops:
  3.1 5.1 %collective-permute-start.2 = (bf16[16,1664]{1,0:T(8,128)(2,1)}, bf16[16,1664]{1,0:T(8,128)(2,1)S(1)}, u32[]{:S(2)}, u32[]{:S(2)}) collective-permute-start(bf16[16,1664]{1,0:T(8,128)(2,1)} %get-tuple-element.107), channel_id=1, source_target_pairs={{0,24},{1,25},{2,26},{3,27},{4,28},{5,29},{6,30},{7,31},{8,16},{9,... | collective-permute-start | bytes 159752 | tf_op jit(solution)/shard_map/ppermute | solution.py:654
  10.7 2.7 %collective-permute-done.1 = bf16[16,1664]{1,0:T(8,128)(2,1)S(1)} collective-permute-done((bf16[16,1664]{1,0:T(8,128)(2,1)}, bf16[16,1664]{1,0:T(8,128)(2,1)S(1)}, u32[]{:S(2)}, u32[]{:S(2)}) %collective-permute-start.1) | collective-permute-done | bytes 53280 | tf_op jit(solution)/shard_map/ppermute | solution.py:654
  14.3 2.4 %collective-permute-start.8 = (bf16[16,4608]{1,0:T(8,128)(2,1)}, bf16[16,4608]{1,0:T(8,128)(2,1)S(1)}, u32[]{:S(2)}, u32[]{:S(2)}) collective-permute-start(bf16[16,4608]{1,0:T(8,128)(2,1)} %get-tuple-element.108), channel_id=1, source_target_pairs={{0,24},{1,25},{2,26},{3,27},{4,28},{5,29},{6,30},{7,31},{8,16},{9,... | collective-permute-start | bytes 442376 | tf_op jit(solution)/shard_map/ppermute | solution.py:654
  16.7 2.0 %collective-permute-start.6 = (bf16[16,4608]{1,0:T(8,128)(2,1)}, bf16[16,4608]{1,0:T(8,128)(2,1)S(1)}, u32[]{:S(2)}, u32[]{:S(2)}) collective-permute-start(bf16[16,4608]{1,0:T(8,128)(2,1)} %get-tuple-element.108), channel_id=1, source_target_pairs={{0,8},{1,9},{2,10},{3,11},{4,12},{5,13},{6,14},{7,15},{8,0},{9,1},... | collective-permute-start | bytes 442376 | tf_op jit(solution)/shard_map/ppermute | solution.py:654
  18.7 2.4 %collective-permute-start.5 = (bf16[4,16,1664]{2,1,0:T(8,128)(2,1)S(1)}, bf16[4,16,1664]{2,1,0:T(8,128)(2,1)S(1)}, u32[]{:S(2)}, u32[]{:S(2)}) collective-permute-start(bf16[4,16,1664]{2,1,0:T(8,128)(2,1)S(1)} %pad_maximum_fusion.7), channel_id=1, source_target_pairs={{0,6},{1,7},{2,4},{3,5},{4,2},{5,3},{6,0},{7,1},{8,14},{9,15},{10,... | collective-permute-start | bytes 638984 | tf_op jit(solution)/shard_map/ppermute | solution.py:654
  24.7 4.3 %collective-permute-done.7 = bf16[16,4608]{1,0:T(8,128)(2,1)S(1)} collective-permute-done((bf16[16,4608]{1,0:T(8,128)(2,1)}, bf16[16,4608]{1,0:T(8,128)(2,1)S(1)}, u32[]{:S(2)}, u32[]{:S(2)}) %collective-permute-start.7) | collective-permute-done | bytes 147488 | tf_op jit(solution)/shard_map/ppermute | solution.py:654
  30.6 2.5 %collective-permute-start.12 = (bf16[4,16,2048]{2,1,0:T(8,128)(2,1)S(1)}, bf16[4,16,2048]{2,1,0:T(8,128)(2,1)S(1)}, u32[]{:S(2)}, u32[]{:S(2)}) collective-permute-start(bf16[4,16,2048]{2,1,0:T(8,128)(2,1)S(1)} %pad_maximum_fusion.6), channel_id=1, source_target_pairs={{0,6},{1,7},{2,4},{3,5},{4,2},{5,3},{6,0},{7,1},{8,14},{9,15},{10,... | collective-permute-start | bytes 786440 | tf_op jit(solution)/shard_map/ppermute | solution.py:654
  34.2 2.6 %project.1 = (f32[8,512]{1,0:T(8,128)S(1)}, bf16[512,1024]{1,0:T(8,128)(2,1)S(1)}, bf16[512,1024]{1,0:T(8,128)(2,1)S(1)}, bf16[512,1024]{1,0:T(8,128)(2,1)S(1)}) custom-call(s32[4]{0:T(128)S(1)} %copy-done.17, bf16[1024,512]{1,0:T(8,128)(2,1)S(1)} %copy-done.1, bf16[16,16,1664]{2,1,0:T(8,128)(2,1)S(1)} %constant_dynamic-update-slice_fusion.near_ref, ...), custom_call_target="tpu_custom_call" | custom-call | flops 60000000 | tf_op jit(solution)/shard_map/project/pallas_call | solution.py:623
  36.8 7.2 %self_forward.1 = (bf16[512,1024]{1,0:T(8,128)(2,1)S(1)}, f32[8,1,1024]{2,1,0:T(1,128)S(1)}) custom-call(s32[4]{0:T(128)S(1)} %copy-done.17, bf16[512,1024]{1,0:T(8,128)(2,1)S(1)} %get-tuple-element.119.q_ref, bf16[512,1024]{1,0:T(8,128)(2,1)S(1)} %get-tuple-element.120.k_ref, bf16[512,1024]{1,0:T(8,128)(2,1)S(1)} %get-tuple-element.121.v_ref), custom_call_target="tpu_custom_call" | custom-call | flops 160000000 | tf_op jit(solution)/shard_map/self_forward/pallas_call | solution.py:623
  44.0 1.9 collective-permute-done.11
  46.2 2.4 %collective-permute-start.16 = (bf16[4,16,2560]{2,1,0:T(8,128)(2,1)S(1)}, bf16[4,16,2560]{2,1,0:T(8,128)(2,1)S(1)}, u32[]{:S(2)}, u32[]{:S(2)}) collective-permute-start(bf16[4,16,2560]{2,1,0:T(8,128)(2,1)S(1)} %pad_maximum_fusion.2), channel_id=1, source_target_pairs={{0,6},{1,7},{2,4},{3,5},{4,2},{5,3},{6,0},{7,1},{8,14},{9,15},{10,... | collective-permute-start | bytes 983048 | tf_op jit(solution)/shard_map/ppermute | solution.py:654
  49.7 4.2 %image_project.1 = (bf16[512,2048]{1,0:T(8,128)(2,1)S(1)}, bf16[3,512,784]{2,1,0:T(8,128)(2,1)S(1)}, bf16[3,512,784]{2,1,0:T(8,128)(2,1)S(1)}) custom-call(s32[4]{0:T(128)S(1)} %copy-done.17, bf16[2352,512]{1,0:T(8,128)(2,1)S(1)} %copy-done, bf16[16,16,2048]{2,1,0:T(8,128)(2,1)S(1)} %pad_maximum_fusion.1.near_ref.wnear_ref, ...), custom_call_target="tpu_custom_call" | custom-call | flops 120000000 | tf_op jit(solution)/shard_map/image_project/pallas_call | solution.py:623
  53.9 2.1 %mid.1 = (f32[1024,512]{1,0:T(8,128)S(1)}, bf16[1024,512]{1,0:T(8,128)(2,1)S(1)}, f32[8,1024]{1,0:T(8,128)S(1)}, bf16[512,1024]{1,0:T(8,128)(2,1)S(1)}) custom-call(bf16[1024,512]{1,0:T(8,128)(2,1)S(1)} %copy-done.1, bf16[512,1024]{1,0:T(8,128)(2,1)S(1)} %get-tuple-element.122.o_ref, bf16[512,2048]{1,0:T(8,128)(2,1)S(1)} %get-tuple-element.127.w_ref, ...), custom_call_target="tpu_custom_call" | custom-call | flops 60000000 | tf_op jit(solution)/shard_map/mid/pallas_call | solution.py:623
  55.9 13.8 %cross_forward.1 = (bf16[512,1024]{1,0:T(8,128)(2,1)S(1)}, f32[8,1,1024]{2,1,0:T(1,128)S(1)}) custom-call(s32[4]{0:T(128)S(1)} %copy-done.17, bf16[512,1024]{1,0:T(8,128)(2,1)S(1)} %get-tuple-element.129.q_ref, bf16[3,512,784]{2,1,0:T(8,128)(2,1)S(1)} %get-tuple-element.130.k_ref, bf16[3,512,784]{2,1,0:T(8,128)(2,1)S(1)} %get-tuple-element.131.v_ref), custom_call_target="tpu_custom_call" | custom-call | flops 320000000 | tf_op jit(solution)/shard_map/cross_forward/pallas_call | solution.py:623
  70.0 3.0 %collective-permute-done.17.wfar_ref = bf16[16,16,2560]{2,1,0:T(8,128)(2,1)S(1)} collective-permute-done((bf16[16,16,2560]{2,1,0:T(8,128)(2,1)S(1)}, bf16[16,16,2560]{2,1,0:T(8,128)(2,1)S(1)}, u32[]{:S(2)}, u32[]{:S(2)}) %collective-permute-start.17) | collective-permute-done | bytes 1310752 | tf_op jit(solution)/shard_map/ppermute | solution.py:654
  73.0 13.2 %feed.1 = (bf16[1024,512]{1,0:T(8,128)(2,1)}, f32[1024,512]{1,0:T(8,128)S(1)}, bf16[512,1024]{1,0:T(8,128)(2,1)S(1)}, bf16[16,16,2560]{2,1,0:T(8,128)(2,1)S(1)},...) custom-call(s32[4]{0:T(128)S(1)} %copy-done.17, bf16[512,1024]{1,0:T(8,128)(2,1)S(1)} %get-tuple-element.132.o_ref, ...), custom_call_target="tpu_custom_call" | custom-call | flops 300000000 | tf_op jit(solution)/shard_map/feed/pallas_call | solution.py:623
  86.3 13.0 %cross_backward.2 = (bf16[256,1024]{1,0:T(8,128)(2,1)S(1)}, bf16[3,256,784]{2,1,0:T(8,128)(2,1)S(1)}, bf16[3,256,784]{2,1,0:T(8,128)(2,1)S(1)}) custom-call(s32[4]{0:T(128)S(1)} %copy-done.17, bf16[512,1024]{1,0:T(8,128)(2,1)S(1)} %get-tuple-element.129.q_ref, bf16[3,512,784]{2,1,0:T(8,128)(2,1)S(1)} %get-tuple-element.130.k_ref, ...), custom_call_target="tpu_custom_call" | custom-call | flops 280000000 | tf_op jit(solution)/shard_map/cross_backward/pallas_call | solution.py:623
  103.3 12.8 %cross_backward.3 = (bf16[256,1024]{1,0:T(8,128)(2,1)S(1)}, bf16[3,256,784]{2,1,0:T(8,128)(2,1)S(1)}, bf16[3,256,784]{2,1,0:T(8,128)(2,1)S(1)}) custom-call(s32[4]{0:T(128)S(1)} %copy-done.17, bf16[512,1024]{1,0:T(8,128)(2,1)S(1)} %get-tuple-element.129.q_ref, bf16[3,512,784]{2,1,0:T(8,128)(2,1)S(1)} %get-tuple-element.130.k_ref, ...), custom_call_target="tpu_custom_call" | custom-call | flops 280000000 | tf_op jit(solution)/shard_map/cross_backward/pallas_call | solution.py:623
  118.2 7.8 %inner.1 = (f32[1024,512]{1,0:T(8,128)S(1)}, bf16[512,1024]{1,0:T(8,128)(2,1)S(1)}, bf16[16,16,2176]{2,1,0:T(8,128)(2,1)S(1)}, bf16[16,16,2176]{2,1,0:T(8,128)(2,1)S(1)}) custom-call(s32[4]{0:T(128)S(1)} %copy-done.17, bf16[256,1024]{1,0:T(8,128)(2,1)S(1)} %get-tuple-element.142.dq0_ref, bf16[256,1024]{1,0:T(8,128)(2,1)S(1)} %get-tuple-element.146.dq1_ref, ...), custom_call_target="tpu_custom_call" | custom-call | flops 200000000 | tf_op jit(solution)/shard_map/inner/pallas_call | solution.py:623
  126.1 6.1 %self_backward.2 = (bf16[256,1024]{1,0:T(8,128)(2,1)S(1)}, bf16[256,1024]{1,0:T(8,128)(2,1)S(1)}, bf16[256,1024]{1,0:T(8,128)(2,1)S(1)}) custom-call(s32[4]{0:T(128)S(1)} %copy-done.17, bf16[512,1024]{1,0:T(8,128)(2,1)S(1)} %get-tuple-element.119.q_ref, bf16[512,1024]{1,0:T(8,128)(2,1)S(1)} %get-tuple-element.120.k_ref, ...), custom_call_target="tpu_custom_call" | custom-call | flops 140000000 | tf_op jit(solution)/shard_map/self_backward/pallas_call | solution.py:623
  132.5 2.4 %collective-permute-start.25 = (bf16[4,16,2176]{2,1,0:T(8,128)(2,1)S(1)}, bf16[4,16,2176]{2,1,0:T(8,128)(2,1)S(1)}, u32[]{:S(2)}, u32[]{:S(2)}) collective-permute-start(bf16[4,16,2176]{2,1,0:T(8,128)(2,1)S(1)} %get-tuple-element.204), channel_id=1, source_target_pairs={{0,6},{1,7},{2,4},{3,5},{4,2},{5,3},{6,0},{7,1},{8,14},{9,15},{10,... | collective-permute-start | bytes 835592 | tf_op jit(solution)/shard_map/ppermute | solution.py:654
  134.9 2.1 %collective-permute-start.24 = (bf16[4,16,2176]{2,1,0:T(8,128)(2,1)S(1)}, bf16[4,16,2176]{2,1,0:T(8,128)(2,1)S(1)}, u32[]{:S(2)}, u32[]{:S(2)}) collective-permute-start(bf16[4,16,2176]{2,1,0:T(8,128)(2,1)S(1)} %get-tuple-element.205), channel_id=1, source_target_pairs={{0,4},{1,5},{2,6},{3,7},{4,0},{5,1},{6,2},{7,3},{8,12},{9,13},{10,... | collective-permute-start | bytes 835592 | tf_op jit(solution)/shard_map/ppermute | solution.py:654
  137.1 5.9 %self_backward.3 = (bf16[256,1024]{1,0:T(8,128)(2,1)S(1)}, bf16[256,1024]{1,0:T(8,128)(2,1)S(1)}, bf16[256,1024]{1,0:T(8,128)(2,1)S(1)}) custom-call(s32[4]{0:T(128)S(1)} %copy-done.17, bf16[512,1024]{1,0:T(8,128)(2,1)S(1)} %get-tuple-element.119.q_ref, bf16[512,1024]{1,0:T(8,128)(2,1)S(1)} %get-tuple-element.120.k_ref, ...), custom_call_target="tpu_custom_call" | custom-call | flops 140000000 | tf_op jit(solution)/shard_map/self_backward/pallas_call | solution.py:623
  143.0 2.5 %project_weight.1 = (bf16[16,16,1536]{2,1,0:T(8,128)(2,1)S(1)}, bf16[16,16,1536]{2,1,0:T(8,128)(2,1)S(1)}) custom-call(s32[4]{0:T(128)S(1)} %copy-done.17, bf16[1024,512]{1,0:T(8,128)(2,1)S(1)} %copy-done.1, bf16[256,1024]{1,0:T(8,128)(2,1)S(1)} %get-tuple-element.158.dq0_ref, bf16[256,1024]{1,0:T(8,128)(2,1)S(1)} %get-tuple-element.163.dq1_ref, ...), custom_call_target="tpu_custom_call" | custom-call | flops 60000000 | tf_op jit(solution)/shard_map/project_weight/pallas_call | solution.py:623
  145.6 4.5 %collective-permute-done.24 = bf16[4,16,2176]{2,1,0:T(8,128)(2,1)S(1)} collective-permute-done((bf16[4,16,2176]{2,1,0:T(8,128)(2,1)S(1)}, bf16[4,16,2176]{2,1,0:T(8,128)(2,1)S(1)}, u32[]{:S(2)}, u32[]{:S(2)}) %collective-permute-start.24) | collective-permute-done | bytes 278560 | tf_op jit(solution)/shard_map/ppermute | solution.py:654
  150.3 2.8 %collective-permute-start.27 = (bf16[16,4736]{1,0:T(8,128)(2,1)S(1)}, bf16[16,4736]{1,0:T(8,128)(2,1)S(1)}, u32[]{:S(2)}, u32[]{:S(2)}) collective-permute-start(bf16[16,4736]{1,0:T(8,128)(2,1)S(1)} %pad_maximum_fusion.8), channel_id=1, source_target_pairs={{0,8},{1,9},{2,10},{3,11},{4,12},{5,13},{6,14},{7,15},{8,0},{9,1},... | collective-permute-start | bytes 454664 | tf_op jit(solution)/shard_map/ppermute | solution.py:654
  155.9 2.4 %collective-permute-start.32 = (bf16[4,16,1536]{2,1,0:T(8,128)(2,1)S(1)}, bf16[4,16,1536]{2,1,0:T(8,128)(2,1)S(1)}, u32[]{:S(2)}, u32[]{:S(2)}) collective-permute-start(bf16[4,16,1536]{2,1,0:T(8,128)(2,1)S(1)} %get-tuple-element.208), channel_id=1, source_target_pairs={{0,6},{1,7},{2,4},{3,5},{4,2},{5,3},{6,0},{7,1},{8,14},{9,15},{10,... | collective-permute-start | bytes 589832 | tf_op jit(solution)/shard_map/ppermute | solution.py:654
  160.5 5.6 %image_grad.1 = f32[2352,512]{1,0:T(8,128)} custom-call(s32[4]{0:T(128)S(1)} %copy-done.17, bf16[3,256,784]{2,1,0:T(8,128)(2,1)S(1)} %get-tuple-element.152.dk0_ref, bf16[3,256,784]{2,1,0:T(8,128)(2,1)S(1)} %copy-done.3, bf16[3,256,784]{2,1,0:T(8,128)(2,1)S(1)} %get-tuple-element.154.dv0_ref, bf16[3,256,784]{2,1,0:T(8,128)(2,1)S(1)} %get-tuple-element.155.dv1_ref, ...), custom_call_target="tpu_custom_call" | custom-call | flops 120000000 | tf_op jit(solution)/shard_map/image_grad/pallas_call | solution.py:623
  166.1 3.9 %token_grad.1 = f32[1024,512]{1,0:T(8,128)} custom-call(s32[4]{0:T(128)S(1)} %copy-done.17, bf16[256,1024]{1,0:T(8,128)(2,1)S(1)} %get-tuple-element.158.dq0_ref, bf16[256,1024]{1,0:T(8,128)(2,1)S(1)} %get-tuple-element.163.dq1_ref, bf16[256,1024]{1,0:T(8,128)(2,1)S(1)} %get-tuple-element.164.dk0_ref, bf16[256,1024]{1,0:T(8,128)(2,1)S(1)} %get-tuple-element.165.dk1_ref, ...), custom_call_target="tpu_custom_call" | custom-call | flops 80000000 | tf_op jit(solution)/shard_map/token_grad/pallas_call | solution.py:623
  172.3 2.4 %collective-permute-start.33 = (bf16[16,1536]{1,0:T(8,128)(2,1)S(1)}, bf16[16,1536]{1,0:T(8,128)(2,1)S(1)}, u32[]{:S(2)}, u32[]{:S(2)}) collective-permute-start(bf16[16,1536]{1,0:T(8,128)(2,1)S(1)} %get-tuple-element.219), channel_id=1, source_target_pairs={{0,8},{1,9},{2,10},{3,11},{4,12},{5,13},{6,14},{7,15},{8,0},{9,1},... | collective-permute-start | bytes 147464 | tf_op jit(solution)/shard_map/ppermute | solution.py:654
  180.2 2.2 %collective-permute-start.39 = (f32[8,128]{1,0:T(8,128)S(1)}, f32[8,128]{1,0:T(8,128)S(1)}, u32[]{:S(2)}, u32[]{:S(2)}) collective-permute-start(f32[8,128]{1,0:T(8,128)S(1)} %add.96), channel_id=1, source_target_pairs={{0,6},{1,7},{2,4},{3,5},{4,2},{5,3},{6,0},{7,1},{8,14},{9,15},{10,... | collective-permute-start | bytes 12296 | tf_op jit(solution)/shard_map/ppermute | solution.py:654
  186.6 2.2 %collective-permute-start.42 = (f32[8,128]{1,0:T(8,128)S(1)}, f32[8,128]{1,0:T(8,128)S(1)}, u32[]{:S(2)}, u32[]{:S(2)}) collective-permute-start(f32[8,128]{1,0:T(8,128)S(1)} %add_add_fusion.refs_0_), channel_id=1, source_target_pairs={{0,24},{1,25},{2,26},{3,27},{4,28},{5,29},{6,30},{7,31},{8,16},{9,... | collective-permute-start | bytes 12296 | tf_op jit(solution)/shard_map/ppermute | solution.py:654
  (146 shorter events, 42.6 us)
Async XLA Ops:
  3.1 7.7 %collective-permute-start.2 = (bf16[16,1664]{1,0:T(8,128)(2,1)}, bf16[16,1664]{1,0:T(8,128)(2,1)S(1)}, u32[]{:S(2)}, u32[]{:S(2)}) collective-permute-start(bf16[16,1664]{1,0:T(8,128)(2,1)} %get-tuple-element.107), channel_id=1, source_target_pairs={{0,24},{1,25},{2,26},{3,27},{4,28},{5,29},{6,30},{7,31},{8,16},{9,... | collective-permute-start | bytes 159752 | tf_op jit(solution)/shard_map/ppermute | solution.py:654
  8.2 5.2 %collective-permute-start.1 = (bf16[16,1664]{1,0:T(8,128)(2,1)}, bf16[16,1664]{1,0:T(8,128)(2,1)S(1)}, u32[]{:S(2)}, u32[]{:S(2)}) collective-permute-start(bf16[16,1664]{1,0:T(8,128)(2,1)} %get-tuple-element.107), channel_id=1, source_target_pairs={{0,16},{1,17},{2,18},{3,19},{4,20},{5,21},{6,22},{7,23},{8,24},{9,... | collective-permute-start | bytes 159752 | tf_op jit(solution)/shard_map/ppermute | solution.py:654
  14.3 8.9 %collective-permute-start.8 = (bf16[16,4608]{1,0:T(8,128)(2,1)}, bf16[16,4608]{1,0:T(8,128)(2,1)S(1)}, u32[]{:S(2)}, u32[]{:S(2)}) collective-permute-start(bf16[16,4608]{1,0:T(8,128)(2,1)} %get-tuple-element.108), channel_id=1, source_target_pairs={{0,24},{1,25},{2,26},{3,27},{4,28},{5,29},{6,30},{7,31},{8,16},{9,... | collective-permute-start | bytes 442376 | tf_op jit(solution)/shard_map/ppermute | solution.py:654
  16.7 12.3 %collective-permute-start.7 = (bf16[16,4608]{1,0:T(8,128)(2,1)}, bf16[16,4608]{1,0:T(8,128)(2,1)S(1)}, u32[]{:S(2)}, u32[]{:S(2)}) collective-permute-start(bf16[16,4608]{1,0:T(8,128)(2,1)} %get-tuple-element.108), channel_id=1, source_target_pairs={{0,16},{1,17},{2,18},{3,19},{4,20},{5,21},{6,22},{7,23},{8,24},{9,... | collective-permute-start | bytes 442376 | tf_op jit(solution)/shard_map/ppermute | solution.py:654
  16.7 12.3 %collective-permute-start.6 = (bf16[16,4608]{1,0:T(8,128)(2,1)}, bf16[16,4608]{1,0:T(8,128)(2,1)S(1)}, u32[]{:S(2)}, u32[]{:S(2)}) collective-permute-start(bf16[16,4608]{1,0:T(8,128)(2,1)} %get-tuple-element.108), channel_id=1, source_target_pairs={{0,8},{1,9},{2,10},{3,11},{4,12},{5,13},{6,14},{7,15},{8,0},{9,1},... | collective-permute-start | bytes 442376 | tf_op jit(solution)/shard_map/ppermute | solution.py:654
  18.7 10.3 %collective-permute-start.5 = (bf16[4,16,1664]{2,1,0:T(8,128)(2,1)S(1)}, bf16[4,16,1664]{2,1,0:T(8,128)(2,1)S(1)}, u32[]{:S(2)}, u32[]{:S(2)}) collective-permute-start(bf16[4,16,1664]{2,1,0:T(8,128)(2,1)S(1)} %pad_maximum_fusion.7), channel_id=1, source_target_pairs={{0,6},{1,7},{2,4},{3,5},{4,2},{5,3},{6,0},{7,1},{8,14},{9,15},{10,... | collective-permute-start | bytes 638984 | tf_op jit(solution)/shard_map/ppermute | solution.py:654
  21.2 8.4 %collective-permute-start.4 = (bf16[4,16,1664]{2,1,0:T(8,128)(2,1)S(1)}, bf16[4,16,1664]{2,1,0:T(8,128)(2,1)S(1)}, u32[]{:S(2)}, u32[]{:S(2)}) collective-permute-start(bf16[4,16,1664]{2,1,0:T(8,128)(2,1)S(1)} %pad_maximum_fusion.7), channel_id=1, source_target_pairs={{0,4},{1,5},{2,6},{3,7},{4,0},{5,1},{6,2},{7,3},{8,12},{9,13},{10,... | collective-permute-start | bytes 638984 | tf_op jit(solution)/shard_map/ppermute | solution.py:654
  23.2 6.4 %collective-permute-start.3 = (bf16[4,16,1664]{2,1,0:T(8,128)(2,1)S(1)}, bf16[4,16,1664]{2,1,0:T(8,128)(2,1)S(1)}, u32[]{:S(2)}, u32[]{:S(2)}) collective-permute-start(bf16[4,16,1664]{2,1,0:T(8,128)(2,1)S(1)} %pad_maximum_fusion.7), channel_id=1, source_target_pairs={{0,2},{1,3},{2,0},{3,1},{4,6},{5,7},{6,4},{7,5},{8,10},{9,11},{10,... | collective-permute-start | bytes 638984 | tf_op jit(solution)/shard_map/ppermute | solution.py:654
  30.6 13.4 %collective-permute-start.12 = (bf16[4,16,2048]{2,1,0:T(8,128)(2,1)S(1)}, bf16[4,16,2048]{2,1,0:T(8,128)(2,1)S(1)}, u32[]{:S(2)}, u32[]{:S(2)}) collective-permute-start(bf16[4,16,2048]{2,1,0:T(8,128)(2,1)S(1)} %pad_maximum_fusion.6), channel_id=1, source_target_pairs={{0,6},{1,7},{2,4},{3,5},{4,2},{5,3},{6,0},{7,1},{8,14},{9,15},{10,... | collective-permute-start | bytes 786440 | tf_op jit(solution)/shard_map/ppermute | solution.py:654
  33.1 12.8 %collective-permute-start.11 = (bf16[4,16,2048]{2,1,0:T(8,128)(2,1)S(1)}, bf16[4,16,2048]{2,1,0:T(8,128)(2,1)S(1)}, u32[]{:S(2)}, u32[]{:S(2)}) collective-permute-start(bf16[4,16,2048]{2,1,0:T(8,128)(2,1)S(1)} %pad_maximum_fusion.6), channel_id=1, source_target_pairs={{0,4},{1,5},{2,6},{3,7},{4,0},{5,1},{6,2},{7,3},{8,12},{9,13},{10,... | collective-permute-start | bytes 786440 | tf_op jit(solution)/shard_map/ppermute | solution.py:654
  33.6 12.3 %collective-permute-start.10 = (bf16[4,16,2048]{2,1,0:T(8,128)(2,1)S(1)}, bf16[4,16,2048]{2,1,0:T(8,128)(2,1)S(1)}, u32[]{:S(2)}, u32[]{:S(2)}) collective-permute-start(bf16[4,16,2048]{2,1,0:T(8,128)(2,1)S(1)} %pad_maximum_fusion.6), channel_id=1, source_target_pairs={{0,2},{1,3},{2,0},{3,1},{4,6},{5,7},{6,4},{7,5},{8,10},{9,11},{10,... | collective-permute-start | bytes 786440 | tf_op jit(solution)/shard_map/ppermute | solution.py:654
  46.2 23.6 %collective-permute-start.16 = (bf16[4,16,2560]{2,1,0:T(8,128)(2,1)S(1)}, bf16[4,16,2560]{2,1,0:T(8,128)(2,1)S(1)}, u32[]{:S(2)}, u32[]{:S(2)}) collective-permute-start(bf16[4,16,2560]{2,1,0:T(8,128)(2,1)S(1)} %pad_maximum_fusion.2), channel_id=1, source_target_pairs={{0,6},{1,7},{2,4},{3,5},{4,2},{5,3},{6,0},{7,1},{8,14},{9,15},{10,... | collective-permute-start | bytes 983048 | tf_op jit(solution)/shard_map/ppermute | solution.py:654
  48.6 21.2 %collective-permute-start.15 = (bf16[4,16,2560]{2,1,0:T(8,128)(2,1)S(1)}, bf16[4,16,2560]{2,1,0:T(8,128)(2,1)S(1)}, u32[]{:S(2)}, u32[]{:S(2)}) collective-permute-start(bf16[4,16,2560]{2,1,0:T(8,128)(2,1)S(1)} %pad_maximum_fusion.2), channel_id=1, source_target_pairs={{0,4},{1,5},{2,6},{3,7},{4,0},{5,1},{6,2},{7,3},{8,12},{9,13},{10,... | collective-permute-start | bytes 983048 | tf_op jit(solution)/shard_map/ppermute | solution.py:654
  49.1 20.6 %collective-permute-start.14 = (bf16[4,16,2560]{2,1,0:T(8,128)(2,1)S(1)}, bf16[4,16,2560]{2,1,0:T(8,128)(2,1)S(1)}, u32[]{:S(2)}, u32[]{:S(2)}) collective-permute-start(bf16[4,16,2560]{2,1,0:T(8,128)(2,1)S(1)} %pad_maximum_fusion.2), channel_id=1, source_target_pairs={{0,2},{1,3},{2,0},{3,1},{4,6},{5,7},{6,4},{7,5},{8,10},{9,11},{10,... | collective-permute-start | bytes 983048 | tf_op jit(solution)/shard_map/ppermute | solution.py:654
  86.2 13.1 %collective-permute-start.18 = (bf16[16,16,2560]{2,1,0:T(8,128)(2,1)S(1)}, bf16[16,16,2560]{2,1,0:T(8,128)(2,1)S(1)}, u32[]{:S(2)}, u32[]{:S(2)}) collective-permute-start(bf16[16,16,2560]{2,1,0:T(8,128)(2,1)S(1)} %get-tuple-element.144), channel_id=1, source_target_pairs={{0,1},{1,0},{2,3},{3,2},{4,5},{5,4},{6,7},{7,6},{8,9},{9,8},{10,11... | collective-permute-start | bytes 3932168 | tf_op jit(solution)/shard_map/ppermute | solution.py:654
  99.7 17.1 %collective-permute-start.19 = (bf16[4,16,2560]{2,1,0:T(8,128)(2,1)S(1)}, bf16[4,16,2560]{2,1,0:T(8,128)(2,1)S(1)}, u32[]{:S(2)}, u32[]{:S(2)}) collective-permute-start(bf16[4,16,2560]{2,1,0:T(8,128)(2,1)S(1)} %get-tuple-element.199), channel_id=1, source_target_pairs={{0,2},{1,3},{2,0},{3,1},{4,6},{5,7},{6,4},{7,5},{8,10},{9,11},{10,... | collective-permute-start | bytes 983048 | tf_op jit(solution)/shard_map/ppermute | solution.py:654
  101.2 15.6 %collective-permute-start.21 = (bf16[4,16,2560]{2,1,0:T(8,128)(2,1)S(1)}, bf16[4,16,2560]{2,1,0:T(8,128)(2,1)S(1)}, u32[]{:S(2)}, u32[]{:S(2)}) collective-permute-start(bf16[4,16,2560]{2,1,0:T(8,128)(2,1)S(1)} %get-tuple-element.200), channel_id=1, source_target_pairs={{0,6},{1,7},{2,4},{3,5},{4,2},{5,3},{6,0},{7,1},{8,14},{9,15},{10,... | collective-permute-start | bytes 983048 | tf_op jit(solution)/shard_map/ppermute | solution.py:654
  102.7 15.4 %collective-permute-start.20 = (bf16[4,16,2560]{2,1,0:T(8,128)(2,1)S(1)}, bf16[4,16,2560]{2,1,0:T(8,128)(2,1)S(1)}, u32[]{:S(2)}, u32[]{:S(2)}) collective-permute-start(bf16[4,16,2560]{2,1,0:T(8,128)(2,1)S(1)} %get-tuple-element.201), channel_id=1, source_target_pairs={{0,4},{1,5},{2,6},{3,7},{4,0},{5,1},{6,2},{7,3},{8,12},{9,13},{10,... | collective-permute-start | bytes 983048 | tf_op jit(solution)/shard_map/ppermute | solution.py:654
  126.0 6.2 %collective-permute-start.22 = (bf16[16,16,2176]{2,1,0:T(8,128)(2,1)S(1)}, bf16[16,16,2176]{2,1,0:T(8,128)(2,1)S(1)}, u32[]{:S(2)}, u32[]{:S(2)}) collective-permute-start(bf16[16,16,2176]{2,1,0:T(8,128)(2,1)S(1)} %get-tuple-element.161), channel_id=1, source_target_pairs={{0,1},{1,0},{2,3},{3,2},{4,5},{5,4},{6,7},{7,6},{8,9},{9,8},{10,11... | collective-permute-start | bytes 3342344 | tf_op jit(solution)/shard_map/ppermute | solution.py:654
  132.5 13.1 %collective-permute-start.25 = (bf16[4,16,2176]{2,1,0:T(8,128)(2,1)S(1)}, bf16[4,16,2176]{2,1,0:T(8,128)(2,1)S(1)}, u32[]{:S(2)}, u32[]{:S(2)}) collective-permute-start(bf16[4,16,2176]{2,1,0:T(8,128)(2,1)S(1)} %get-tuple-element.204), channel_id=1, source_target_pairs={{0,6},{1,7},{2,4},{3,5},{4,2},{5,3},{6,0},{7,1},{8,14},{9,15},{10,... | collective-permute-start | bytes 835592 | tf_op jit(solution)/shard_map/ppermute | solution.py:654
  134.9 15.1 %collective-permute-start.24 = (bf16[4,16,2176]{2,1,0:T(8,128)(2,1)S(1)}, bf16[4,16,2176]{2,1,0:T(8,128)(2,1)S(1)}, u32[]{:S(2)}, u32[]{:S(2)}) collective-permute-start(bf16[4,16,2176]{2,1,0:T(8,128)(2,1)S(1)} %get-tuple-element.205), channel_id=1, source_target_pairs={{0,4},{1,5},{2,6},{3,7},{4,0},{5,1},{6,2},{7,3},{8,12},{9,13},{10,... | collective-permute-start | bytes 835592 | tf_op jit(solution)/shard_map/ppermute | solution.py:654
  137.0 13.0 %collective-permute-start.23 = (bf16[4,16,2176]{2,1,0:T(8,128)(2,1)S(1)}, bf16[4,16,2176]{2,1,0:T(8,128)(2,1)S(1)}, u32[]{:S(2)}, u32[]{:S(2)}) collective-permute-start(bf16[4,16,2176]{2,1,0:T(8,128)(2,1)S(1)} %get-tuple-element.206), channel_id=1, source_target_pairs={{0,2},{1,3},{2,0},{3,1},{4,6},{5,7},{6,4},{7,5},{8,10},{9,11},{10,... | collective-permute-start | bytes 835592 | tf_op jit(solution)/shard_map/ppermute | solution.py:654
  145.5 10.1 %collective-permute-start.26 = (bf16[16,16,1536]{2,1,0:T(8,128)(2,1)S(1)}, bf16[16,16,1536]{2,1,0:T(8,128)(2,1)S(1)}, u32[]{:S(2)}, u32[]{:S(2)}) collective-permute-start(bf16[16,16,1536]{2,1,0:T(8,128)(2,1)S(1)} %get-tuple-element.171), channel_id=1, source_target_pairs={{0,1},{1,0},{2,3},{3,2},{4,5},{5,4},{6,7},{7,6},{8,9},{9,8},{10,11... | collective-permute-start | bytes 2359304 | tf_op jit(solution)/shard_map/ppermute | solution.py:654
  150.3 9.3 %collective-permute-start.27 = (bf16[16,4736]{1,0:T(8,128)(2,1)S(1)}, bf16[16,4736]{1,0:T(8,128)(2,1)S(1)}, u32[]{:S(2)}, u32[]{:S(2)}) collective-permute-start(bf16[16,4736]{1,0:T(8,128)(2,1)S(1)} %pad_maximum_fusion.8), channel_id=1, source_target_pairs={{0,8},{1,9},{2,10},{3,11},{4,12},{5,13},{6,14},{7,15},{8,0},{9,1},... | collective-permute-start | bytes 454664 | tf_op jit(solution)/shard_map/ppermute | solution.py:654
  153.1 17.0 %collective-permute-start.28 = (bf16[16,4736]{1,0:T(8,128)(2,1)S(1)}, bf16[16,4736]{1,0:T(8,128)(2,1)S(1)}, u32[]{:S(2)}, u32[]{:S(2)}) collective-permute-start(bf16[16,4736]{1,0:T(8,128)(2,1)S(1)} %pad_maximum_fusion.9), channel_id=1, source_target_pairs={{0,16},{1,17},{2,18},{3,19},{4,20},{5,21},{6,22},{7,23},{8,24},{9,... | collective-permute-start | bytes 454664 | tf_op jit(solution)/shard_map/ppermute | solution.py:654
  154.2 15.9 %collective-permute-start.29 = (bf16[16,4736]{1,0:T(8,128)(2,1)S(1)}, bf16[16,4736]{1,0:T(8,128)(2,1)S(1)}, u32[]{:S(2)}, u32[]{:S(2)}) collective-permute-start(bf16[16,4736]{1,0:T(8,128)(2,1)S(1)} %pad_maximum_fusion.10), channel_id=1, source_target_pairs={{0,24},{1,25},{2,26},{3,27},{4,28},{5,29},{6,30},{7,31},{8,16},{9,... | collective-permute-start | bytes 454664 | tf_op jit(solution)/shard_map/ppermute | solution.py:654
  155.9 14.2 %collective-permute-start.32 = (bf16[4,16,1536]{2,1,0:T(8,128)(2,1)S(1)}, bf16[4,16,1536]{2,1,0:T(8,128)(2,1)S(1)}, u32[]{:S(2)}, u32[]{:S(2)}) collective-permute-start(bf16[4,16,1536]{2,1,0:T(8,128)(2,1)S(1)} %get-tuple-element.208), channel_id=1, source_target_pairs={{0,6},{1,7},{2,4},{3,5},{4,2},{5,3},{6,0},{7,1},{8,14},{9,15},{10,... | collective-permute-start | bytes 589832 | tf_op jit(solution)/shard_map/ppermute | solution.py:654
  158.2 11.9 %collective-permute-start.31 = (bf16[4,16,1536]{2,1,0:T(8,128)(2,1)S(1)}, bf16[4,16,1536]{2,1,0:T(8,128)(2,1)S(1)}, u32[]{:S(2)}, u32[]{:S(2)}) collective-permute-start(bf16[4,16,1536]{2,1,0:T(8,128)(2,1)S(1)} %get-tuple-element.209), channel_id=1, source_target_pairs={{0,4},{1,5},{2,6},{3,7},{4,0},{5,1},{6,2},{7,3},{8,12},{9,13},{10,... | collective-permute-start | bytes 589832 | tf_op jit(solution)/shard_map/ppermute | solution.py:654
  159.6 10.5 %collective-permute-start.30 = (bf16[4,16,1536]{2,1,0:T(8,128)(2,1)S(1)}, bf16[4,16,1536]{2,1,0:T(8,128)(2,1)S(1)}, u32[]{:S(2)}, u32[]{:S(2)}) collective-permute-start(bf16[4,16,1536]{2,1,0:T(8,128)(2,1)S(1)} %get-tuple-element.210), channel_id=1, source_target_pairs={{0,2},{1,3},{2,0},{3,1},{4,6},{5,7},{6,4},{7,5},{8,10},{9,11},{10,... | collective-permute-start | bytes 589832 | tf_op jit(solution)/shard_map/ppermute | solution.py:654
  170.2 6.0 %collective-permute-start.35 = (bf16[16,1536]{1,0:T(8,128)(2,1)S(1)}, bf16[16,1536]{1,0:T(8,128)(2,1)S(1)}, u32[]{:S(2)}, u32[]{:S(2)}) collective-permute-start(bf16[16,1536]{1,0:T(8,128)(2,1)S(1)} %get-tuple-element.217), channel_id=1, source_target_pairs={{0,24},{1,25},{2,26},{3,27},{4,28},{5,29},{6,30},{7,31},{8,16},{9,... | collective-permute-start | bytes 147464 | tf_op jit(solution)/shard_map/ppermute | solution.py:654
  171.9 5.5 %collective-permute-start.34 = (bf16[16,1536]{1,0:T(8,128)(2,1)S(1)}, bf16[16,1536]{1,0:T(8,128)(2,1)S(1)}, u32[]{:S(2)}, u32[]{:S(2)}) collective-permute-start(bf16[16,1536]{1,0:T(8,128)(2,1)S(1)} %get-tuple-element.218), channel_id=1, source_target_pairs={{0,16},{1,17},{2,18},{3,19},{4,20},{5,21},{6,22},{7,23},{8,24},{9,... | collective-permute-start | bytes 147464 | tf_op jit(solution)/shard_map/ppermute | solution.py:654
  186.6 5.4 %collective-permute-start.42 = (f32[8,128]{1,0:T(8,128)S(1)}, f32[8,128]{1,0:T(8,128)S(1)}, u32[]{:S(2)}, u32[]{:S(2)}) collective-permute-start(f32[8,128]{1,0:T(8,128)S(1)} %add_add_fusion.refs_0_), channel_id=1, source_target_pairs={{0,24},{1,25},{2,26},{3,27},{4,28},{5,29},{6,30},{7,31},{8,16},{9,... | collective-permute-start | bytes 12296 | tf_op jit(solution)/shard_map/ppermute | solution.py:654
  (33 other events, 200.2 us)

commit v4 on v3

--- a/solution.py
+++ b/solution.py
@@ -56,13 +56,13 @@
     return jnp.sum(value, axis=0, keepdims=True)
 
 
-def pipeline(chains):
+def pipeline(chains, oldest_first=False):
     done = object()
     live = []
     waiting = list(chains)
     while live or waiting:
         if waiting:
-            live.insert(0, waiting.pop(0))
+            live.insert(len(live) if oldest_first else 0, waiting.pop(0))
         live = [chain for chain in live if next(chain, done) is not done]
 
 
@@ -165,7 +165,7 @@
             dot(grad(index), prob_ref[slot, 0:count], 1, 1),
         )
 
-    pipeline([chain(index) for index in range(heads)])
+    pipeline([chain(index) for index in range(heads)], oldest_first=True)
 
 
 def self_blocks(info_ref, rows, bias, run):

time: 198 us -> 198 us (level)
  starting transfers between devices: 51.9 us -> 54.9 us
  waiting for transfers between devices: 31.2 us -> 28.9 us
    ppermute x43, starting transfers between devices: 51.9 us -> 54.9 us  [swap(): return lax.ppermute(value, AXES, [(i, i ^ mask) for i in range(count)])]
    ppermute x43, waiting for transfers between devices: 31.2 us -> 28.9 us  [swap(): return lax.ppermute(value, AXES, [(i, i ^ mask) for i in range(count)])]
  transfers between devices with their start and end apart: 43 -> 43, of which waited for: 19 -> 21; matrix products, arithmetic and copies ran while one was open for 1% -> 1% of each run, Pallas kernels for 41% -> 40%
where the time goes in v4:
time: 198 us; the launch traced here: 195 us
  Pallas kernels  104 us (53%)
  starting transfers between devices  54.9 us (28%)
  waiting for transfers between devices  28.9 us (15%)
  other arithmetic  3.36 us (2%)
  between operations  2.13 us (1%)
    pallas_call x17, Pallas kernels, call(): pl.pallas_call(kernel, out_shape=out_shape, in_specs=specs, out_specs=[SM...  104 us
    ppermute x43, starting transfers between devices, swap(): return lax.ppermute(value, AXES, [(i, i ^ mask) for i in range(count)])  54.9 us
    ppermute x43, waiting for transfers between devices, swap(): return lax.ppermute(value, AXES, [(i, i ^ mask) for i in range(count)])  28.9 us
  transfers between devices with their start and end apart: 43, of which 21 were waited for; matrix products, arithmetic and copies ran while one was open for 1% of the time, Pallas kernels for 40%

profile of v4, /device:TPU:0, one launch (start us, length us, event | category | flops | bytes accessed | tf_op | source)
XLA Modules:
  0.0 195.0 jit_solution(5587719093763531794)
XLA Ops:
  1.3 1.7 pack.1
  3.1 5.1 %collective-permute-start.2 = (bf16[16,1664]{1,0:T(8,128)(2,1)}, bf16[16,1664]{1,0:T(8,128)(2,1)S(1)}, u32[]{:S(2)}, u32[]{:S(2)}) collective-permute-start(bf16[16,1664]{1,0:T(8,128)(2,1)} %get-tuple-element.107), channel_id=1, source_target_pairs={{0,24},{1,25},{2,26},{3,27},{4,28},{5,29},{6,30},{7,31},{8,16},{9,... | collective-permute-start | bytes 159752 | tf_op jit(solution)/shard_map/ppermute | solution.py:654
  10.7 2.7 %collective-permute-done.1 = bf16[16,1664]{1,0:T(8,128)(2,1)S(1)} collective-permute-done((bf16[16,1664]{1,0:T(8,128)(2,1)}, bf16[16,1664]{1,0:T(8,128)(2,1)S(1)}, u32[]{:S(2)}, u32[]{:S(2)}) %collective-permute-start.1) | collective-permute-done | bytes 53280 | tf_op jit(solution)/shard_map/ppermute | solution.py:654
  14.3 2.4 %collective-permute-start.8 = (bf16[16,4608]{1,0:T(8,128)(2,1)}, bf16[16,4608]{1,0:T(8,128)(2,1)S(1)}, u32[]{:S(2)}, u32[]{:S(2)}) collective-permute-start(bf16[16,4608]{1,0:T(8,128)(2,1)} %get-tuple-element.108), channel_id=1, source_target_pairs={{0,24},{1,25},{2,26},{3,27},{4,28},{5,29},{6,30},{7,31},{8,16},{9,... | collective-permute-start | bytes 442376 | tf_op jit(solution)/shard_map/ppermute | solution.py:654
  16.7 2.0 %collective-permute-start.6 = (bf16[16,4608]{1,0:T(8,128)(2,1)}, bf16[16,4608]{1,0:T(8,128)(2,1)S(1)}, u32[]{:S(2)}, u32[]{:S(2)}) collective-permute-start(bf16[16,4608]{1,0:T(8,128)(2,1)} %get-tuple-element.108), channel_id=1, source_target_pairs={{0,8},{1,9},{2,10},{3,11},{4,12},{5,13},{6,14},{7,15},{8,0},{9,1},... | collective-permute-start | bytes 442376 | tf_op jit(solution)/shard_map/ppermute | solution.py:654
  18.7 2.4 %collective-permute-start.5 = (bf16[4,16,1664]{2,1,0:T(8,128)(2,1)S(1)}, bf16[4,16,1664]{2,1,0:T(8,128)(2,1)S(1)}, u32[]{:S(2)}, u32[]{:S(2)}) collective-permute-start(bf16[4,16,1664]{2,1,0:T(8,128)(2,1)S(1)} %pad_maximum_fusion.7), channel_id=1, source_target_pairs={{0,6},{1,7},{2,4},{3,5},{4,2},{5,3},{6,0},{7,1},{8,14},{9,15},{10,... | collective-permute-start | bytes 638984 | tf_op jit(solution)/shard_map/ppermute | solution.py:654
  24.7 4.3 %collective-permute-done.7 = bf16[16,4608]{1,0:T(8,128)(2,1)S(1)} collective-permute-done((bf16[16,4608]{1,0:T(8,128)(2,1)}, bf16[16,4608]{1,0:T(8,128)(2,1)S(1)}, u32[]{:S(2)}, u32[]{:S(2)}) %collective-permute-start.7) | collective-permute-done | bytes 147488 | tf_op jit(solution)/shard_map/ppermute | solution.py:654
  30.6 2.5 %collective-permute-start.12 = (bf16[4,16,2048]{2,1,0:T(8,128)(2,1)S(1)}, bf16[4,16,2048]{2,1,0:T(8,128)(2,1)S(1)}, u32[]{:S(2)}, u32[]{:S(2)}) collective-permute-start(bf16[4,16,2048]{2,1,0:T(8,128)(2,1)S(1)} %pad_maximum_fusion.6), channel_id=1, source_target_pairs={{0,6},{1,7},{2,4},{3,5},{4,2},{5,3},{6,0},{7,1},{8,14},{9,15},{10,... | collective-permute-start | bytes 786440 | tf_op jit(solution)/shard_map/ppermute | solution.py:654
  34.2 2.6 %project.1 = (f32[8,512]{1,0:T(8,128)S(1)}, bf16[512,1024]{1,0:T(8,128)(2,1)S(1)}, bf16[512,1024]{1,0:T(8,128)(2,1)S(1)}, bf16[512,1024]{1,0:T(8,128)(2,1)S(1)}) custom-call(s32[4]{0:T(128)S(1)} %copy-done.17, bf16[1024,512]{1,0:T(8,128)(2,1)S(1)} %copy-done.1, bf16[16,16,1664]{2,1,0:T(8,128)(2,1)S(1)} %constant_dynamic-update-slice_fusion.near_ref, ...), custom_call_target="tpu_custom_call" | custom-call | flops 60000000 | tf_op jit(solution)/shard_map/project/pallas_call | solution.py:623
  36.8 7.2 %self_forward.1 = (bf16[512,1024]{1,0:T(8,128)(2,1)S(1)}, f32[8,1,1024]{2,1,0:T(1,128)S(1)}) custom-call(s32[4]{0:T(128)S(1)} %copy-done.17, bf16[512,1024]{1,0:T(8,128)(2,1)S(1)} %get-tuple-element.119.q_ref, bf16[512,1024]{1,0:T(8,128)(2,1)S(1)} %get-tuple-element.120.k_ref, bf16[512,1024]{1,0:T(8,128)(2,1)S(1)} %get-tuple-element.121.v_ref), custom_call_target="tpu_custom_call" | custom-call | flops 160000000 | tf_op jit(solution)/shard_map/self_forward/pallas_call | solution.py:623
  44.0 1.9 collective-permute-done.11
  46.2 2.5 %collective-permute-start.16 = (bf16[4,16,2560]{2,1,0:T(8,128)(2,1)S(1)}, bf16[4,16,2560]{2,1,0:T(8,128)(2,1)S(1)}, u32[]{:S(2)}, u32[]{:S(2)}) collective-permute-start(bf16[4,16,2560]{2,1,0:T(8,128)(2,1)S(1)} %pad_maximum_fusion.2), channel_id=1, source_target_pairs={{0,6},{1,7},{2,4},{3,5},{4,2},{5,3},{6,0},{7,1},{8,14},{9,15},{10,... | collective-permute-start | bytes 983048 | tf_op jit(solution)/shard_map/ppermute | solution.py:654
  49.7 4.2 %image_project.1 = (bf16[512,2048]{1,0:T(8,128)(2,1)S(1)}, bf16[3,512,784]{2,1,0:T(8,128)(2,1)S(1)}, bf16[3,512,784]{2,1,0:T(8,128)(2,1)S(1)}) custom-call(s32[4]{0:T(128)S(1)} %copy-done.17, bf16[2352,512]{1,0:T(8,128)(2,1)S(1)} %copy-done, bf16[16,16,2048]{2,1,0:T(8,128)(2,1)S(1)} %pad_maximum_fusion.1.near_ref.wnear_ref, ...), custom_call_target="tpu_custom_call" | custom-call | flops 120000000 | tf_op jit(solution)/shard_map/image_project/pallas_call | solution.py:623
  53.9 2.1 %mid.1 = (f32[1024,512]{1,0:T(8,128)S(1)}, bf16[1024,512]{1,0:T(8,128)(2,1)S(1)}, f32[8,1024]{1,0:T(8,128)S(1)}, bf16[512,1024]{1,0:T(8,128)(2,1)S(1)}) custom-call(bf16[1024,512]{1,0:T(8,128)(2,1)S(1)} %copy-done.1, bf16[512,1024]{1,0:T(8,128)(2,1)S(1)} %get-tuple-element.122.o_ref, bf16[512,2048]{1,0:T(8,128)(2,1)S(1)} %get-tuple-element.127.w_ref, ...), custom_call_target="tpu_custom_call" | custom-call | flops 60000000 | tf_op jit(solution)/shard_map/mid/pallas_call | solution.py:623
  55.9 13.8 %cross_forward.1 = (bf16[512,1024]{1,0:T(8,128)(2,1)S(1)}, f32[8,1,1024]{2,1,0:T(1,128)S(1)}) custom-call(s32[4]{0:T(128)S(1)} %copy-done.17, bf16[512,1024]{1,0:T(8,128)(2,1)S(1)} %get-tuple-element.129.q_ref, bf16[3,512,784]{2,1,0:T(8,128)(2,1)S(1)} %get-tuple-element.130.k_ref, bf16[3,512,784]{2,1,0:T(8,128)(2,1)S(1)} %get-tuple-element.131.v_ref), custom_call_target="tpu_custom_call" | custom-call | flops 320000000 | tf_op jit(solution)/shard_map/cross_forward/pallas_call | solution.py:623
  70.0 3.0 %collective-permute-done.17.wfar_ref = bf16[16,16,2560]{2,1,0:T(8,128)(2,1)S(1)} collective-permute-done((bf16[16,16,2560]{2,1,0:T(8,128)(2,1)S(1)}, bf16[16,16,2560]{2,1,0:T(8,128)(2,1)S(1)}, u32[]{:S(2)}, u32[]{:S(2)}) %collective-permute-start.17) | collective-permute-done | bytes 1310752 | tf_op jit(solution)/shard_map/ppermute | solution.py:654
  73.0 13.2 %feed.1 = (bf16[1024,512]{1,0:T(8,128)(2,1)}, f32[1024,512]{1,0:T(8,128)S(1)}, bf16[512,1024]{1,0:T(8,128)(2,1)S(1)}, bf16[16,16,2560]{2,1,0:T(8,128)(2,1)S(1)},...) custom-call(s32[4]{0:T(128)S(1)} %copy-done.17, bf16[512,1024]{1,0:T(8,128)(2,1)S(1)} %get-tuple-element.132.o_ref, ...), custom_call_target="tpu_custom_call" | custom-call | flops 300000000 | tf_op jit(solution)/shard_map/feed/pallas_call | solution.py:623
  86.3 12.8 %cross_backward.2 = (bf16[256,1024]{1,0:T(8,128)(2,1)S(1)}, bf16[3,256,784]{2,1,0:T(8,128)(2,1)S(1)}, bf16[3,256,784]{2,1,0:T(8,128)(2,1)S(1)}) custom-call(s32[4]{0:T(128)S(1)} %copy-done.17, bf16[512,1024]{1,0:T(8,128)(2,1)S(1)} %get-tuple-element.129.q_ref, bf16[3,512,784]{2,1,0:T(8,128)(2,1)S(1)} %get-tuple-element.130.k_ref, ...), custom_call_target="tpu_custom_call" | custom-call | flops 280000000 | tf_op jit(solution)/shard_map/cross_backward/pallas_call | solution.py:623
  103.1 12.6 %cross_backward.3 = (bf16[256,1024]{1,0:T(8,128)(2,1)S(1)}, bf16[3,256,784]{2,1,0:T(8,128)(2,1)S(1)}, bf16[3,256,784]{2,1,0:T(8,128)(2,1)S(1)}) custom-call(s32[4]{0:T(128)S(1)} %copy-done.17, bf16[512,1024]{1,0:T(8,128)(2,1)S(1)} %get-tuple-element.129.q_ref, bf16[3,512,784]{2,1,0:T(8,128)(2,1)S(1)} %get-tuple-element.130.k_ref, ...), custom_call_target="tpu_custom_call" | custom-call | flops 280000000 | tf_op jit(solution)/shard_map/cross_backward/pallas_call | solution.py:623
  118.1 7.8 %inner.1 = (f32[1024,512]{1,0:T(8,128)S(1)}, bf16[512,1024]{1,0:T(8,128)(2,1)S(1)}, bf16[16,16,2176]{2,1,0:T(8,128)(2,1)S(1)}, bf16[16,16,2176]{2,1,0:T(8,128)(2,1)S(1)}) custom-call(s32[4]{0:T(128)S(1)} %copy-done.17, bf16[256,1024]{1,0:T(8,128)(2,1)S(1)} %get-tuple-element.142.dq0_ref, bf16[256,1024]{1,0:T(8,128)(2,1)S(1)} %get-tuple-element.146.dq1_ref, ...), custom_call_target="tpu_custom_call" | custom-call | flops 200000000 | tf_op jit(solution)/shard_map/inner/pallas_call | solution.py:623
  126.0 6.0 %self_backward.2 = (bf16[256,1024]{1,0:T(8,128)(2,1)S(1)}, bf16[256,1024]{1,0:T(8,128)(2,1)S(1)}, bf16[256,1024]{1,0:T(8,128)(2,1)S(1)}) custom-call(s32[4]{0:T(128)S(1)} %copy-done.17, bf16[512,1024]{1,0:T(8,128)(2,1)S(1)} %get-tuple-element.119.q_ref, bf16[512,1024]{1,0:T(8,128)(2,1)S(1)} %get-tuple-element.120.k_ref, ...), custom_call_target="tpu_custom_call" | custom-call | flops 140000000 | tf_op jit(solution)/shard_map/self_backward/pallas_call | solution.py:623
  132.2 3.8 %collective-permute-start.25 = (bf16[4,16,2176]{2,1,0:T(8,128)(2,1)S(1)}, bf16[4,16,2176]{2,1,0:T(8,128)(2,1)S(1)}, u32[]{:S(2)}, u32[]{:S(2)}) collective-permute-start(bf16[4,16,2176]{2,1,0:T(8,128)(2,1)S(1)} %get-tuple-element.204), channel_id=1, source_target_pairs={{0,6},{1,7},{2,4},{3,5},{4,2},{5,3},{6,0},{7,1},{8,14},{9,15},{10,... | collective-permute-start | bytes 835592 | tf_op jit(solution)/shard_map/ppermute | solution.py:654
  136.6 5.8 %self_backward.3 = (bf16[256,1024]{1,0:T(8,128)(2,1)S(1)}, bf16[256,1024]{1,0:T(8,128)(2,1)S(1)}, bf16[256,1024]{1,0:T(8,128)(2,1)S(1)}) custom-call(s32[4]{0:T(128)S(1)} %copy-done.17, bf16[512,1024]{1,0:T(8,128)(2,1)S(1)} %get-tuple-element.119.q_ref, bf16[512,1024]{1,0:T(8,128)(2,1)S(1)} %get-tuple-element.120.k_ref, ...), custom_call_target="tpu_custom_call" | custom-call | flops 140000000 | tf_op jit(solution)/shard_map/self_backward/pallas_call | solution.py:623
  142.4 2.5 %project_weight.1 = (bf16[16,16,1536]{2,1,0:T(8,128)(2,1)S(1)}, bf16[16,16,1536]{2,1,0:T(8,128)(2,1)S(1)}) custom-call(s32[4]{0:T(128)S(1)} %copy-done.17, bf16[1024,512]{1,0:T(8,128)(2,1)S(1)} %copy-done.1, bf16[256,1024]{1,0:T(8,128)(2,1)S(1)} %get-tuple-element.158.dq0_ref, bf16[256,1024]{1,0:T(8,128)(2,1)S(1)} %get-tuple-element.163.dq1_ref, ...), custom_call_target="tpu_custom_call" | custom-call | flops 60000000 | tf_op jit(solution)/shard_map/project_weight/pallas_call | solution.py:623
  149.7 4.5 %collective-permute-start.27 = (bf16[16,4736]{1,0:T(8,128)(2,1)S(1)}, bf16[16,4736]{1,0:T(8,128)(2,1)S(1)}, u32[]{:S(2)}, u32[]{:S(2)}) collective-permute-start(bf16[16,4736]{1,0:T(8,128)(2,1)S(1)} %pad_maximum_fusion.8), channel_id=1, source_target_pairs={{0,8},{1,9},{2,10},{3,11},{4,12},{5,13},{6,14},{7,15},{8,0},{9,1},... | collective-permute-start | bytes 454664 | tf_op jit(solution)/shard_map/ppermute | solution.py:654
  154.4 2.2 %collective-permute-start.29 = (bf16[16,4736]{1,0:T(8,128)(2,1)S(1)}, bf16[16,4736]{1,0:T(8,128)(2,1)S(1)}, u32[]{:S(2)}, u32[]{:S(2)}) collective-permute-start(bf16[16,4736]{1,0:T(8,128)(2,1)S(1)} %pad_maximum_fusion.10), channel_id=1, source_target_pairs={{0,24},{1,25},{2,26},{3,27},{4,28},{5,29},{6,30},{7,31},{8,16},{9,... | collective-permute-start | bytes 454664 | tf_op jit(solution)/shard_map/ppermute | solution.py:654
  158.0 1.8 collective-permute-start.31
  161.2 5.6 %image_grad.1 = f32[2352,512]{1,0:T(8,128)} custom-call(s32[4]{0:T(128)S(1)} %copy-done.17, bf16[3,256,784]{2,1,0:T(8,128)(2,1)S(1)} %get-tuple-element.152.dk0_ref, bf16[3,256,784]{2,1,0:T(8,128)(2,1)S(1)} %copy-done.3, bf16[3,256,784]{2,1,0:T(8,128)(2,1)S(1)} %get-tuple-element.154.dv0_ref, bf16[3,256,784]{2,1,0:T(8,128)(2,1)S(1)} %get-tuple-element.155.dv1_ref, ...), custom_call_target="tpu_custom_call" | custom-call | flops 120000000 | tf_op jit(solution)/shard_map/image_grad/pallas_call | solution.py:623
  166.8 3.9 %token_grad.1 = f32[1024,512]{1,0:T(8,128)} custom-call(s32[4]{0:T(128)S(1)} %copy-done.17, bf16[256,1024]{1,0:T(8,128)(2,1)S(1)} %get-tuple-element.158.dq0_ref, bf16[256,1024]{1,0:T(8,128)(2,1)S(1)} %get-tuple-element.163.dq1_ref, bf16[256,1024]{1,0:T(8,128)(2,1)S(1)} %get-tuple-element.164.dk0_ref, bf16[256,1024]{1,0:T(8,128)(2,1)S(1)} %get-tuple-element.165.dk1_ref, ...), custom_call_target="tpu_custom_call" | custom-call | flops 80000000 | tf_op jit(solution)/shard_map/token_grad/pallas_call | solution.py:623
  170.9 2.0 %collective-permute-start.35 = (bf16[16,1536]{1,0:T(8,128)(2,1)S(1)}, bf16[16,1536]{1,0:T(8,128)(2,1)S(1)}, u32[]{:S(2)}, u32[]{:S(2)}) collective-permute-start(bf16[16,1536]{1,0:T(8,128)(2,1)S(1)} %get-tuple-element.217), channel_id=1, source_target_pairs={{0,24},{1,25},{2,26},{3,27},{4,28},{5,29},{6,30},{7,31},{8,16},{9,... | collective-permute-start | bytes 147464 | tf_op jit(solution)/shard_map/ppermute | solution.py:654
  175.4 2.0 %collective-permute-done.35.refs_7_ = bf16[16,1536]{1,0:T(8,128)(2,1)S(1)} collective-permute-done((bf16[16,1536]{1,0:T(8,128)(2,1)S(1)}, bf16[16,1536]{1,0:T(8,128)(2,1)S(1)}, u32[]{:S(2)}, u32[]{:S(2)}) %collective-permute-start.35) | collective-permute-done | bytes 49184 | tf_op jit(solution)/shard_map/ppermute | solution.py:654
  189.8 1.7 collective-permute-start.40
  (146 shorter events, 44.3 us)
Async XLA Ops:
  3.1 7.7 %collective-permute-start.2 = (bf16[16,1664]{1,0:T(8,128)(2,1)}, bf16[16,1664]{1,0:T(8,128)(2,1)S(1)}, u32[]{:S(2)}, u32[]{:S(2)}) collective-permute-start(bf16[16,1664]{1,0:T(8,128)(2,1)} %get-tuple-element.107), channel_id=1, source_target_pairs={{0,24},{1,25},{2,26},{3,27},{4,28},{5,29},{6,30},{7,31},{8,16},{9,... | collective-permute-start | bytes 159752 | tf_op jit(solution)/shard_map/ppermute | solution.py:654
  8.2 5.2 %collective-permute-start.1 = (bf16[16,1664]{1,0:T(8,128)(2,1)}, bf16[16,1664]{1,0:T(8,128)(2,1)S(1)}, u32[]{:S(2)}, u32[]{:S(2)}) collective-permute-start(bf16[16,1664]{1,0:T(8,128)(2,1)} %get-tuple-element.107), channel_id=1, source_target_pairs={{0,16},{1,17},{2,18},{3,19},{4,20},{5,21},{6,22},{7,23},{8,24},{9,... | collective-permute-start | bytes 159752 | tf_op jit(solution)/shard_map/ppermute | solution.py:654
  14.3 8.9 %collective-permute-start.8 = (bf16[16,4608]{1,0:T(8,128)(2,1)}, bf16[16,4608]{1,0:T(8,128)(2,1)S(1)}, u32[]{:S(2)}, u32[]{:S(2)}) collective-permute-start(bf16[16,4608]{1,0:T(8,128)(2,1)} %get-tuple-element.108), channel_id=1, source_target_pairs={{0,24},{1,25},{2,26},{3,27},{4,28},{5,29},{6,30},{7,31},{8,16},{9,... | collective-permute-start | bytes 442376 | tf_op jit(solution)/shard_map/ppermute | solution.py:654
  16.7 12.3 %collective-permute-start.7 = (bf16[16,4608]{1,0:T(8,128)(2,1)}, bf16[16,4608]{1,0:T(8,128)(2,1)S(1)}, u32[]{:S(2)}, u32[]{:S(2)}) collective-permute-start(bf16[16,4608]{1,0:T(8,128)(2,1)} %get-tuple-element.108), channel_id=1, source_target_pairs={{0,16},{1,17},{2,18},{3,19},{4,20},{5,21},{6,22},{7,23},{8,24},{9,... | collective-permute-start | bytes 442376 | tf_op jit(solution)/shard_map/ppermute | solution.py:654
  16.7 12.3 %collective-permute-start.6 = (bf16[16,4608]{1,0:T(8,128)(2,1)}, bf16[16,4608]{1,0:T(8,128)(2,1)S(1)}, u32[]{:S(2)}, u32[]{:S(2)}) collective-permute-start(bf16[16,4608]{1,0:T(8,128)(2,1)} %get-tuple-element.108), channel_id=1, source_target_pairs={{0,8},{1,9},{2,10},{3,11},{4,12},{5,13},{6,14},{7,15},{8,0},{9,1},... | collective-permute-start | bytes 442376 | tf_op jit(solution)/shard_map/ppermute | solution.py:654
  18.7 10.3 %collective-permute-start.5 = (bf16[4,16,1664]{2,1,0:T(8,128)(2,1)S(1)}, bf16[4,16,1664]{2,1,0:T(8,128)(2,1)S(1)}, u32[]{:S(2)}, u32[]{:S(2)}) collective-permute-start(bf16[4,16,1664]{2,1,0:T(8,128)(2,1)S(1)} %pad_maximum_fusion.7), channel_id=1, source_target_pairs={{0,6},{1,7},{2,4},{3,5},{4,2},{5,3},{6,0},{7,1},{8,14},{9,15},{10,... | collective-permute-start | bytes 638984 | tf_op jit(solution)/shard_map/ppermute | solution.py:654
  21.2 8.4 %collective-permute-start.4 = (bf16[4,16,1664]{2,1,0:T(8,128)(2,1)S(1)}, bf16[4,16,1664]{2,1,0:T(8,128)(2,1)S(1)}, u32[]{:S(2)}, u32[]{:S(2)}) collective-permute-start(bf16[4,16,1664]{2,1,0:T(8,128)(2,1)S(1)} %pad_maximum_fusion.7), channel_id=1, source_target_pairs={{0,4},{1,5},{2,6},{3,7},{4,0},{5,1},{6,2},{7,3},{8,12},{9,13},{10,... | collective-permute-start | bytes 638984 | tf_op jit(solution)/shard_map/ppermute | solution.py:654
  23.2 6.4 %collective-permute-start.3 = (bf16[4,16,1664]{2,1,0:T(8,128)(2,1)S(1)}, bf16[4,16,1664]{2,1,0:T(8,128)(2,1)S(1)}, u32[]{:S(2)}, u32[]{:S(2)}) collective-permute-start(bf16[4,16,1664]{2,1,0:T(8,128)(2,1)S(1)} %pad_maximum_fusion.7), channel_id=1, source_target_pairs={{0,2},{1,3},{2,0},{3,1},{4,6},{5,7},{6,4},{7,5},{8,10},{9,11},{10,... | collective-permute-start | bytes 638984 | tf_op jit(solution)/shard_map/ppermute | solution.py:654
  30.6 13.4 %collective-permute-start.12 = (bf16[4,16,2048]{2,1,0:T(8,128)(2,1)S(1)}, bf16[4,16,2048]{2,1,0:T(8,128)(2,1)S(1)}, u32[]{:S(2)}, u32[]{:S(2)}) collective-permute-start(bf16[4,16,2048]{2,1,0:T(8,128)(2,1)S(1)} %pad_maximum_fusion.6), channel_id=1, source_target_pairs={{0,6},{1,7},{2,4},{3,5},{4,2},{5,3},{6,0},{7,1},{8,14},{9,15},{10,... | collective-permute-start | bytes 786440 | tf_op jit(solution)/shard_map/ppermute | solution.py:654
  33.1 12.8 %collective-permute-start.11 = (bf16[4,16,2048]{2,1,0:T(8,128)(2,1)S(1)}, bf16[4,16,2048]{2,1,0:T(8,128)(2,1)S(1)}, u32[]{:S(2)}, u32[]{:S(2)}) collective-permute-start(bf16[4,16,2048]{2,1,0:T(8,128)(2,1)S(1)} %pad_maximum_fusion.6), channel_id=1, source_target_pairs={{0,4},{1,5},{2,6},{3,7},{4,0},{5,1},{6,2},{7,3},{8,12},{9,13},{10,... | collective-permute-start | bytes 786440 | tf_op jit(solution)/shard_map/ppermute | solution.py:654
  33.6 12.3 %collective-permute-start.10 = (bf16[4,16,2048]{2,1,0:T(8,128)(2,1)S(1)}, bf16[4,16,2048]{2,1,0:T(8,128)(2,1)S(1)}, u32[]{:S(2)}, u32[]{:S(2)}) collective-permute-start(bf16[4,16,2048]{2,1,0:T(8,128)(2,1)S(1)} %pad_maximum_fusion.6), channel_id=1, source_target_pairs={{0,2},{1,3},{2,0},{3,1},{4,6},{5,7},{6,4},{7,5},{8,10},{9,11},{10,... | collective-permute-start | bytes 786440 | tf_op jit(solution)/shard_map/ppermute | solution.py:654
  46.2 23.6 %collective-permute-start.16 = (bf16[4,16,2560]{2,1,0:T(8,128)(2,1)S(1)}, bf16[4,16,2560]{2,1,0:T(8,128)(2,1)S(1)}, u32[]{:S(2)}, u32[]{:S(2)}) collective-permute-start(bf16[4,16,2560]{2,1,0:T(8,128)(2,1)S(1)} %pad_maximum_fusion.2), channel_id=1, source_target_pairs={{0,6},{1,7},{2,4},{3,5},{4,2},{5,3},{6,0},{7,1},{8,14},{9,15},{10,... | collective-permute-start | bytes 983048 | tf_op jit(solution)/shard_map/ppermute | solution.py:654
  48.6 21.1 %collective-permute-start.15 = (bf16[4,16,2560]{2,1,0:T(8,128)(2,1)S(1)}, bf16[4,16,2560]{2,1,0:T(8,128)(2,1)S(1)}, u32[]{:S(2)}, u32[]{:S(2)}) collective-permute-start(bf16[4,16,2560]{2,1,0:T(8,128)(2,1)S(1)} %pad_maximum_fusion.2), channel_id=1, source_target_pairs={{0,4},{1,5},{2,6},{3,7},{4,0},{5,1},{6,2},{7,3},{8,12},{9,13},{10,... | collective-permute-start | bytes 983048 | tf_op jit(solution)/shard_map/ppermute | solution.py:654
  49.1 20.6 %collective-permute-start.14 = (bf16[4,16,2560]{2,1,0:T(8,128)(2,1)S(1)}, bf16[4,16,2560]{2,1,0:T(8,128)(2,1)S(1)}, u32[]{:S(2)}, u32[]{:S(2)}) collective-permute-start(bf16[4,16,2560]{2,1,0:T(8,128)(2,1)S(1)} %pad_maximum_fusion.2), channel_id=1, source_target_pairs={{0,2},{1,3},{2,0},{3,1},{4,6},{5,7},{6,4},{7,5},{8,10},{9,11},{10,... | collective-permute-start | bytes 983048 | tf_op jit(solution)/shard_map/ppermute | solution.py:654
  86.2 13.0 %collective-permute-start.18 = (bf16[16,16,2560]{2,1,0:T(8,128)(2,1)S(1)}, bf16[16,16,2560]{2,1,0:T(8,128)(2,1)S(1)}, u32[]{:S(2)}, u32[]{:S(2)}) collective-permute-start(bf16[16,16,2560]{2,1,0:T(8,128)(2,1)S(1)} %get-tuple-element.144), channel_id=1, source_target_pairs={{0,1},{1,0},{2,3},{3,2},{4,5},{5,4},{6,7},{7,6},{8,9},{9,8},{10,11... | collective-permute-start | bytes 3932168 | tf_op jit(solution)/shard_map/ppermute | solution.py:654
  99.6 17.1 %collective-permute-start.19 = (bf16[4,16,2560]{2,1,0:T(8,128)(2,1)S(1)}, bf16[4,16,2560]{2,1,0:T(8,128)(2,1)S(1)}, u32[]{:S(2)}, u32[]{:S(2)}) collective-permute-start(bf16[4,16,2560]{2,1,0:T(8,128)(2,1)S(1)} %get-tuple-element.199), channel_id=1, source_target_pairs={{0,2},{1,3},{2,0},{3,1},{4,6},{5,7},{6,4},{7,5},{8,10},{9,11},{10,... | collective-permute-start | bytes 983048 | tf_op jit(solution)/shard_map/ppermute | solution.py:654
  101.0 15.7 %collective-permute-start.21 = (bf16[4,16,2560]{2,1,0:T(8,128)(2,1)S(1)}, bf16[4,16,2560]{2,1,0:T(8,128)(2,1)S(1)}, u32[]{:S(2)}, u32[]{:S(2)}) collective-permute-start(bf16[4,16,2560]{2,1,0:T(8,128)(2,1)S(1)} %get-tuple-element.200), channel_id=1, source_target_pairs={{0,6},{1,7},{2,4},{3,5},{4,2},{5,3},{6,0},{7,1},{8,14},{9,15},{10,... | collective-permute-start | bytes 983048 | tf_op jit(solution)/shard_map/ppermute | solution.py:654
  102.6 15.3 %collective-permute-start.20 = (bf16[4,16,2560]{2,1,0:T(8,128)(2,1)S(1)}, bf16[4,16,2560]{2,1,0:T(8,128)(2,1)S(1)}, u32[]{:S(2)}, u32[]{:S(2)}) collective-permute-start(bf16[4,16,2560]{2,1,0:T(8,128)(2,1)S(1)} %get-tuple-element.201), channel_id=1, source_target_pairs={{0,4},{1,5},{2,6},{3,7},{4,0},{5,1},{6,2},{7,3},{8,12},{9,13},{10,... | collective-permute-start | bytes 983048 | tf_op jit(solution)/shard_map/ppermute | solution.py:654
  125.9 6.1 %collective-permute-start.22 = (bf16[16,16,2176]{2,1,0:T(8,128)(2,1)S(1)}, bf16[16,16,2176]{2,1,0:T(8,128)(2,1)S(1)}, u32[]{:S(2)}, u32[]{:S(2)}) collective-permute-start(bf16[16,16,2176]{2,1,0:T(8,128)(2,1)S(1)} %get-tuple-element.161), channel_id=1, source_target_pairs={{0,1},{1,0},{2,3},{3,2},{4,5},{5,4},{6,7},{7,6},{8,9},{9,8},{10,11... | collective-permute-start | bytes 3342344 | tf_op jit(solution)/shard_map/ppermute | solution.py:654
  132.2 14.1 %collective-permute-start.25 = (bf16[4,16,2176]{2,1,0:T(8,128)(2,1)S(1)}, bf16[4,16,2176]{2,1,0:T(8,128)(2,1)S(1)}, u32[]{:S(2)}, u32[]{:S(2)}) collective-permute-start(bf16[4,16,2176]{2,1,0:T(8,128)(2,1)S(1)} %get-tuple-element.204), channel_id=1, source_target_pairs={{0,6},{1,7},{2,4},{3,5},{4,2},{5,3},{6,0},{7,1},{8,14},{9,15},{10,... | collective-permute-start | bytes 835592 | tf_op jit(solution)/shard_map/ppermute | solution.py:654
  136.0 11.9 %collective-permute-start.24 = (bf16[4,16,2176]{2,1,0:T(8,128)(2,1)S(1)}, bf16[4,16,2176]{2,1,0:T(8,128)(2,1)S(1)}, u32[]{:S(2)}, u32[]{:S(2)}) collective-permute-start(bf16[4,16,2176]{2,1,0:T(8,128)(2,1)S(1)} %get-tuple-element.205), channel_id=1, source_target_pairs={{0,4},{1,5},{2,6},{3,7},{4,0},{5,1},{6,2},{7,3},{8,12},{9,13},{10,... | collective-permute-start | bytes 835592 | tf_op jit(solution)/shard_map/ppermute | solution.py:654
  136.0 13.5 %collective-permute-start.23 = (bf16[4,16,2176]{2,1,0:T(8,128)(2,1)S(1)}, bf16[4,16,2176]{2,1,0:T(8,128)(2,1)S(1)}, u32[]{:S(2)}, u32[]{:S(2)}) collective-permute-start(bf16[4,16,2176]{2,1,0:T(8,128)(2,1)S(1)} %get-tuple-element.206), channel_id=1, source_target_pairs={{0,2},{1,3},{2,0},{3,1},{4,6},{5,7},{6,4},{7,5},{8,10},{9,11},{10,... | collective-permute-start | bytes 835592 | tf_op jit(solution)/shard_map/ppermute | solution.py:654
  144.9 11.7 %collective-permute-start.26 = (bf16[16,16,1536]{2,1,0:T(8,128)(2,1)S(1)}, bf16[16,16,1536]{2,1,0:T(8,128)(2,1)S(1)}, u32[]{:S(2)}, u32[]{:S(2)}) collective-permute-start(bf16[16,16,1536]{2,1,0:T(8,128)(2,1)S(1)} %get-tuple-element.171), channel_id=1, source_target_pairs={{0,1},{1,0},{2,3},{3,2},{4,5},{5,4},{6,7},{7,6},{8,9},{9,8},{10,11... | collective-permute-start | bytes 2359304 | tf_op jit(solution)/shard_map/ppermute | solution.py:654
  149.7 10.3 %collective-permute-start.27 = (bf16[16,4736]{1,0:T(8,128)(2,1)S(1)}, bf16[16,4736]{1,0:T(8,128)(2,1)S(1)}, u32[]{:S(2)}, u32[]{:S(2)}) collective-permute-start(bf16[16,4736]{1,0:T(8,128)(2,1)S(1)} %pad_maximum_fusion.8), channel_id=1, source_target_pairs={{0,8},{1,9},{2,10},{3,11},{4,12},{5,13},{6,14},{7,15},{8,0},{9,1},... | collective-permute-start | bytes 454664 | tf_op jit(solution)/shard_map/ppermute | solution.py:654
  154.2 16.6 %collective-permute-start.28 = (bf16[16,4736]{1,0:T(8,128)(2,1)S(1)}, bf16[16,4736]{1,0:T(8,128)(2,1)S(1)}, u32[]{:S(2)}, u32[]{:S(2)}) collective-permute-start(bf16[16,4736]{1,0:T(8,128)(2,1)S(1)} %pad_maximum_fusion.9), channel_id=1, source_target_pairs={{0,16},{1,17},{2,18},{3,19},{4,20},{5,21},{6,22},{7,23},{8,24},{9,... | collective-permute-start | bytes 454664 | tf_op jit(solution)/shard_map/ppermute | solution.py:654
  154.4 16.4 %collective-permute-start.29 = (bf16[16,4736]{1,0:T(8,128)(2,1)S(1)}, bf16[16,4736]{1,0:T(8,128)(2,1)S(1)}, u32[]{:S(2)}, u32[]{:S(2)}) collective-permute-start(bf16[16,4736]{1,0:T(8,128)(2,1)S(1)} %pad_maximum_fusion.10), channel_id=1, source_target_pairs={{0,24},{1,25},{2,26},{3,27},{4,28},{5,29},{6,30},{7,31},{8,16},{9,... | collective-permute-start | bytes 454664 | tf_op jit(solution)/shard_map/ppermute | solution.py:654
  156.9 13.9 %collective-permute-start.32 = (bf16[4,16,1536]{2,1,0:T(8,128)(2,1)S(1)}, bf16[4,16,1536]{2,1,0:T(8,128)(2,1)S(1)}, u32[]{:S(2)}, u32[]{:S(2)}) collective-permute-start(bf16[4,16,1536]{2,1,0:T(8,128)(2,1)S(1)} %get-tuple-element.208), channel_id=1, source_target_pairs={{0,6},{1,7},{2,4},{3,5},{4,2},{5,3},{6,0},{7,1},{8,14},{9,15},{10,... | collective-permute-start | bytes 589832 | tf_op jit(solution)/shard_map/ppermute | solution.py:654
  158.0 12.8 %collective-permute-start.31 = (bf16[4,16,1536]{2,1,0:T(8,128)(2,1)S(1)}, bf16[4,16,1536]{2,1,0:T(8,128)(2,1)S(1)}, u32[]{:S(2)}, u32[]{:S(2)}) collective-permute-start(bf16[4,16,1536]{2,1,0:T(8,128)(2,1)S(1)} %get-tuple-element.209), channel_id=1, source_target_pairs={{0,4},{1,5},{2,6},{3,7},{4,0},{5,1},{6,2},{7,3},{8,12},{9,13},{10,... | collective-permute-start | bytes 589832 | tf_op jit(solution)/shard_map/ppermute | solution.py:654
  160.0 10.7 %collective-permute-start.30 = (bf16[4,16,1536]{2,1,0:T(8,128)(2,1)S(1)}, bf16[4,16,1536]{2,1,0:T(8,128)(2,1)S(1)}, u32[]{:S(2)}, u32[]{:S(2)}) collective-permute-start(bf16[4,16,1536]{2,1,0:T(8,128)(2,1)S(1)} %get-tuple-element.210), channel_id=1, source_target_pairs={{0,2},{1,3},{2,0},{3,1},{4,6},{5,7},{6,4},{7,5},{8,10},{9,11},{10,... | collective-permute-start | bytes 589832 | tf_op jit(solution)/shard_map/ppermute | solution.py:654
  170.9 6.4 %collective-permute-start.35 = (bf16[16,1536]{1,0:T(8,128)(2,1)S(1)}, bf16[16,1536]{1,0:T(8,128)(2,1)S(1)}, u32[]{:S(2)}, u32[]{:S(2)}) collective-permute-start(bf16[16,1536]{1,0:T(8,128)(2,1)S(1)} %get-tuple-element.217), channel_id=1, source_target_pairs={{0,24},{1,25},{2,26},{3,27},{4,28},{5,29},{6,30},{7,31},{8,16},{9,... | collective-permute-start | bytes 147464 | tf_op jit(solution)/shard_map/ppermute | solution.py:654
  173.0 5.4 %collective-permute-start.34 = (bf16[16,1536]{1,0:T(8,128)(2,1)S(1)}, bf16[16,1536]{1,0:T(8,128)(2,1)S(1)}, u32[]{:S(2)}, u32[]{:S(2)}) collective-permute-start(bf16[16,1536]{1,0:T(8,128)(2,1)S(1)} %get-tuple-element.218), channel_id=1, source_target_pairs={{0,16},{1,17},{2,18},{3,19},{4,20},{5,21},{6,22},{7,23},{8,24},{9,... | collective-permute-start | bytes 147464 | tf_op jit(solution)/shard_map/ppermute | solution.py:654
  187.1 5.4 %collective-permute-start.42 = (f32[8,128]{1,0:T(8,128)S(1)}, f32[8,128]{1,0:T(8,128)S(1)}, u32[]{:S(2)}, u32[]{:S(2)}) collective-permute-start(f32[8,128]{1,0:T(8,128)S(1)} %add_add_fusion.refs_0_), channel_id=1, source_target_pairs={{0,24},{1,25},{2,26},{3,27},{4,28},{5,29},{6,30},{7,31},{8,16},{9,... | collective-permute-start | bytes 12296 | tf_op jit(solution)/shard_map/ppermute | solution.py:654
  (33 other events, 202.1 us)
